TPU v7x, 128 devices: a whole 4x4x4 slice. The times are simulated.
128 devices in a mesh: shard: 16 (over y_hi, x, core), context: 2 (over y_lo), tensor: 4 (over z).
Axes of the slice: x: 4, y: 4 (y_hi: 2, y_lo: 2; y = y_hi * 2 + y_lo), z: 4, core: 2. Of those that a mesh axis runs over, the one named last changes fastest.
Arguments:
- tokens: bfloat16 [32768, 1024], P(('shard', 'context')), may hold values from -6 to 6
- segment: int32 [32768], P(('shard', 'context')), may hold values from 0 to 64, as said below
- norm_gain: bfloat16 [1024], P('shard'), may hold values from 0.5 to 1.5
- w_z: bfloat16 [1024, 2048], P('shard', 'tensor'), may hold values from -0.1875 to 0.1875
- w_x: bfloat16 [1024, 2048], P('shard', 'tensor'), may hold values from -0.1875 to 0.1875
- w_dt: bfloat16 [1024, 32], P('shard', 'tensor'), may hold values from -0.1875 to 0.1875
- w_bc: bfloat16 [1024, 256], P('shard'), may hold values from -0.1875 to 0.1875
- conv_x: float32 [4, 2048], P(None, 'tensor'), may hold values from -3 to 3
- conv_xb: float32 [2048], P('tensor'), may hold values from -0.5 to 0.5
- conv_bc: float32 [4, 256], replicated, may hold values from -3 to 3
- conv_bcb: float32 [256], replicated, may hold values from -0.5 to 0.5
- dt_bias: float32 [32], P('tensor'), may hold values from -4 to -1
- a_log: float32 [32], P('tensor'), may hold values from -3.5 to 1
- d_skip: float32 [32], P('tensor'), may hold values from 0.3 to 1
- gate_gain: float32 [2048], P('tensor'), may hold values from 0.5 to 1.5
- w_out: bfloat16 [1024, 2048], P('shard', 'tensor'), may hold values from -0.125 to 0.125
- cotangent: bfloat16 [32768, 1024], P(('shard', 'context')), may hold values from -6 to 6
Outputs:
- output: bfloat16 [32768, 1024], P(('shard', 'context'))
- d_tokens: bfloat16 [32768, 1024], P(('shard', 'context'))
- g_norm_gain: float32 [1024], P('shard')
- g_w_z: float32 [1024, 2048], P('shard', 'tensor')
- g_w_x: float32 [1024, 2048], P('shard', 'tensor')
- g_w_dt: float32 [1024, 32], P('shard', 'tensor')
- g_w_bc: float32 [1024, 256], P('shard')
- g_conv_x: float32 [4, 2048], P(None, 'tensor')
- g_conv_xb: float32 [2048], P('tensor')
- g_conv_bc: float32 [4, 256], replicated
- g_conv_bcb: float32 [256], replicated
- g_dt_bias: float32 [32], P('tensor')
- g_a_log: float32 [32], P('tensor')
- g_d_skip: float32 [32], P('tensor')
- g_gate_gain: float32 [2048], P('tensor')
- g_w_out: float32 [1024, 2048], P('shard', 'tensor')
Inputs may be any that keep to these rules, and one draw needn't show every extreme that they name: Along each packed row of 2048 tokens the segment numbers start at 0, never fall, and rise by at most 1 from one token to the next; each row ends with segment number 1024 // 16.
All inputs are finite; a program needn't handle non-finite values.
Results may differ from a plain program's by a relative error of at most 0.012.
The roundings to bfloat16 on the way count: a program that leaves them out, or rounds other values in their place, can miss the bound.
Values may be sent and summed in bfloat16 or wider, within the bound.
A program may use at most 192 MiB of HBM per device.

v0:
```python
from functools import partial

import jax
import jax.numpy as jnp
from jax import lax
from jax.sharding import PartitionSpec as P

HEADDIM = 64
STATE = 128
CONV = 4
STRETCH = 256
INNER = 2048


EPSILON = 1e-05
TOP_PRECISION = lax.Precision.HIGHEST


def passed_along(value, axis, by):
    count = lax.axis_size(axis)
    pairs = [(i, i + by) for i in range(count) if 0 <= i + by < count]
    return lax.ppermute(value, axis, pairs)


def carried_in_2(value, axis, combine, identity):
    count, place = (lax.axis_size(axis), lax.axis_index(axis))
    everything = jax.tree.map(lambda part: lax.all_gather(part, axis), value)
    start = jax.tree.map(
        lambda part, zero: jnp.broadcast_to(jnp.asarray(zero, part.dtype), part.shape),
        value,
        identity,
    )

    def turn(k, before):
        reached = k < place
        new = combine(before, jax.tree.map(lambda part: part[k], everything))
        return jax.tree.map(lambda a, b: jnp.where(reached, a, b), new, before)

    return lax.fori_loop(0, count, turn, start)


def carried_in_3(value, axis, join, neutral):
    count = lax.axis_size(axis)
    place = lax.axis_index(axis)
    ahead = count - 1 - place
    gathered = jax.tree.map(
        lambda a, kind: lax.all_gather(a.astype(kind), axis),
        value,
        jax.tree.map(lambda a: jnp.bfloat16 if a.dtype == jnp.float32 else a.dtype, value),
    )
    state = jax.tree.map(lambda a, e: jnp.zeros_like(a) + jnp.asarray(e, a.dtype), value, neutral)

    def one(turn, state):
        source = count - 1 - turn
        return join(
            state,
            jax.tree.map(
                lambda a, own: lax.dynamic_index_in_dim(a, source, 0, False).astype(own.dtype),
                gathered,
                value,
            ),
        )

    return lax.fori_loop(0, ahead, one, state)


def against(left, right):
    return lax.dot_general(
        left, right, (((1,), (1,)), ((), ())), preferred_element_type=jnp.float32
    )


def over_rows(left, right):
    return lax.dot_general(
        left, right, (((0,), (0,)), ((), ())), preferred_element_type=jnp.float32
    )


def silu_slope(value):
    sigma = jax.nn.sigmoid(value)
    return sigma * (1.0 + value * (1.0 - sigma))


def chain_combine(earlier, later):
    return (earlier[0] * later[0], later[0][:, None, None] * earlier[1] + later[1])


def block_step(a_neg, carried, block_in):
    state_now, last_seg = carried
    x_act, b_act, c_act, dt_val, seg_ids = block_in
    cum_decay = jnp.cumsum(dt_val * a_neg[None, :], axis=0)
    length = seg_ids.shape[0]
    causal = jnp.arange(length)[:, None] >= jnp.arange(length)[None, :]
    pair_mask = (causal & (seg_ids[:, None] == seg_ids[None, :]))[:, :, None]
    log_gap = jnp.where(pair_mask, cum_decay[:, None, :] - cum_decay[None, :, :], 0.0)
    pair_decay = jnp.where(pair_mask, jnp.exp(log_gap), 0.0)
    scores = jnp.dot(c_act, b_act.T, precision=TOP_PRECISION)
    weights = pair_decay * scores[:, :, None] * dt_val[None, :, :]
    mixed_out = jnp.einsum("ijh,jhp->ihp", weights, x_act, precision=TOP_PRECISION)
    enter_decay = jnp.where((seg_ids == last_seg)[:, None], jnp.exp(cum_decay), 0.0)
    mixed_out = mixed_out + enter_decay[:, :, None] * jnp.einsum(
        "in,hpn->ihp", c_act, state_now, precision=TOP_PRECISION
    )
    tail_decay = (
        jnp.where(
            (seg_ids == seg_ids[-1])[:, None], jnp.exp(cum_decay[-1][None, :] - cum_decay), 0.0
        )
        * dt_val
    )
    keep_decay = jnp.where(seg_ids[-1] == last_seg, jnp.exp(cum_decay[-1]), 0.0)
    fresh_state = jnp.einsum("jh,jhp,jn->hpn", tail_decay, x_act, b_act, precision=TOP_PRECISION)
    return ((keep_decay[:, None, None] * state_now + fresh_state, seg_ids[-1]), mixed_out)


def mixer(
    extended,
    conv_w,
    conv_b,
    dt_raw,
    dt_bias,
    a_log,
    d_skip,
    state_in,
    tap_masks=None,
    seg_float=None,
    start_seg=None,
):
    length = dt_raw.shape[0]
    head_count = dt_raw.shape[1]
    inner_width = head_count * HEADDIM
    pre_conv = jnp.broadcast_to(conv_b[None, :], (length, conv_b.shape[0]))
    for offset in range(CONV):
        pre_conv = pre_conv + conv_w[offset][None, :] * jnp.where(
            tap_masks[offset][:, None], extended[offset : offset + length], 0.0
        )
    activated = jax.nn.silu(pre_conv)
    x_act = activated[:, :inner_width].reshape(length, head_count, HEADDIM)
    b_act = activated[:, inner_width : inner_width + STATE]
    c_act = activated[:, inner_width + STATE :]
    dt_val = jax.nn.softplus(dt_raw + dt_bias[None, :])
    a_neg = -jnp.exp(a_log)
    block_count = length // STRETCH
    blocks = (
        x_act.reshape(block_count, STRETCH, head_count, HEADDIM),
        b_act.reshape(block_count, STRETCH, STATE),
        c_act.reshape(block_count, STRETCH, STATE),
        dt_val.reshape(block_count, STRETCH, head_count),
        seg_float.reshape(block_count, STRETCH),
    )
    final_carry, mixed_out = lax.scan(partial(block_step, a_neg), (state_in, start_seg), blocks)
    y_mixed = mixed_out.reshape(length, inner_width) + (d_skip[None, :, None] * x_act).reshape(
        length, inner_width
    )
    running = jnp.cumsum(dt_val * a_neg[None, :], axis=0)
    enter_decay = jnp.where((seg_float == start_seg)[:, None], jnp.exp(running), 0.0)
    return ((y_mixed, final_carry[0]), (enter_decay, enter_decay[-1], c_act))


def local(
    tokens,
    segment,
    norm_gain,
    w_z,
    w_x,
    w_dt,
    w_bc,
    conv_x,
    conv_xb,
    conv_bc,
    conv_bcb,
    dt_bias,
    a_log,
    d_skip,
    gate_gain,
    w_out,
    cotangent,
):
    gain_all, z_all, x_all, dt_all, bc_all, out_all = (
        lax.all_gather(norm_gain, "shard", axis=0, tiled=True),
        lax.all_gather(w_z, "shard", axis=0, tiled=True),
        lax.all_gather(w_x, "shard", axis=0, tiled=True),
        lax.all_gather(w_dt, "shard", axis=0, tiled=True),
        lax.all_gather(w_bc, "shard", axis=0, tiled=True),
        lax.all_gather(w_out, "shard", axis=0, tiled=True),
    )
    length = tokens.shape[0]
    head_count = dt_bias.shape[0]
    inner_width = head_count * HEADDIM
    bc_width = 2 * STATE
    border = CONV - 1
    plain = tokens.astype(jnp.float32)
    root_inv = lax.rsqrt(jnp.mean(plain * plain, axis=1, keepdims=True) + EPSILON)
    gain_float = gain_all.astype(jnp.float32)
    x_normed = (plain * root_inv * gain_float[None, :]).astype(jnp.bfloat16)
    z_gate = jnp.dot(x_normed, z_all, preferred_element_type=jnp.float32)
    x_part = jnp.dot(x_normed, x_all, preferred_element_type=jnp.float32).astype(jnp.bfloat16)
    bc_part = jnp.dot(x_normed, bc_all, preferred_element_type=jnp.float32).astype(jnp.bfloat16)
    dt_raw = jnp.dot(x_normed, dt_all, preferred_element_type=jnp.float32)
    x_bc = jnp.concatenate([x_part, bc_part], axis=1)
    seg_mod = (segment % 128).astype(jnp.bfloat16)
    edge_rows, edge_ids = passed_along(
        (x_bc[length - border :], seg_mod[length - border :]), "context", 1
    )
    extended = jnp.concatenate([edge_rows, x_bc], axis=0).astype(jnp.float32)
    ext_ids = jnp.concatenate([edge_ids, seg_mod]).astype(jnp.float32)
    own_ids = seg_mod.astype(jnp.float32)
    tap_masks = jnp.stack([ext_ids[offset : offset + length] == own_ids for offset in range(CONV)])
    seg_float = segment.astype(jnp.float32)
    start_seg = jnp.where(edge_ids[-1].astype(jnp.float32) == own_ids[0], seg_float[0], -1.0)
    conv_w = jnp.concatenate([conv_x, conv_bc], axis=1)
    conv_b = jnp.concatenate([conv_xb, conv_bcb])
    local_mixer = partial(mixer, tap_masks=tap_masks, seg_float=seg_float, start_seg=start_seg)
    zero_state = jnp.zeros((head_count, HEADDIM, STATE), jnp.float32)
    (y_zero, state_local), (enter_decay, passing, c_act) = local_mixer(
        extended, conv_w, conv_b, dt_raw, dt_bias, a_log, d_skip, zero_state
    )
    state_in = carried_in_2(
        (passing, state_local),
        "context",
        chain_combine,
        (jnp.ones_like(passing), jnp.zeros_like(state_local)),
    )[1]
    carried_in = enter_decay[:, :, None] * jnp.einsum(
        "tn,hpn->thp", c_act, state_in, precision=TOP_PRECISION
    )
    y_mixed = y_zero + carried_in.reshape(length, inner_width)
    gate_act = jax.nn.silu(z_gate)
    gated = y_mixed * gate_act
    total_sq = lax.psum(jnp.sum(gated * gated, axis=1), "tensor")
    gate_root = lax.rsqrt(total_sq / INNER + EPSILON)[:, None]
    y_normed = (gated * gate_root * gate_gain[None, :]).astype(jnp.bfloat16)
    branch = lax.psum(against(y_normed, out_all), "tensor")
    output = (plain + branch).astype(jnp.bfloat16)
    d_y_normed = jnp.dot(cotangent, out_all, preferred_element_type=jnp.float32)
    g_w_out = over_rows(cotangent, y_normed)
    g_gate_gain = jnp.sum(d_y_normed * gated * gate_root, axis=0)
    d_scaled = d_y_normed * gate_gain[None, :]
    cross_sum = lax.psum(jnp.sum(d_scaled * gated, axis=1), "tensor")
    d_gated = gate_root * d_scaled - gated * gate_root**3 * (cross_sum / INNER)[:, None]
    d_y = d_gated * gate_act
    d_z = (d_gated * y_mixed * silu_slope(z_gate)).astype(jnp.bfloat16)
    d_carry_local = jnp.einsum(
        "thp,th,tn->hpn",
        d_y.reshape(length, head_count, HEADDIM),
        enter_decay,
        c_act,
        precision=TOP_PRECISION,
    )
    d_state_out = carried_in_3(
        (passing, d_carry_local),
        "context",
        chain_combine,
        (jnp.ones_like(passing), jnp.zeros_like(d_carry_local)),
    )[1]
    forward_again, pullback, extras_again = jax.vjp(
        local_mixer,
        extended,
        conv_w,
        conv_b,
        dt_raw,
        dt_bias,
        a_log,
        d_skip,
        state_in,
        has_aux=True,
    )
    d_ext, d_conv_w, d_conv_b, d_dt_raw, g_dt_bias, g_a_log, g_d_skip, d_state_in = pullback(
        (d_y, d_state_out)
    )
    returned = passed_along(d_ext[:border], "context", -1)
    d_mixed = d_ext[border:]
    d_mixed = jnp.concatenate(
        [d_mixed[: length - border], d_mixed[length - border :] + returned], axis=0
    )
    d_x_low = d_mixed[:, :inner_width].astype(jnp.bfloat16)
    d_dt_low = d_dt_raw.astype(jnp.bfloat16)
    part_in = against(d_z, z_all) + against(d_x_low, x_all) + against(d_dt_low, dt_all)
    stat_rows = plain * root_inv
    in_sum, bc_sum, conv_bc_sum, conv_bcb_sum = lax.psum(
        (part_in, d_mixed[:, inner_width:], d_conv_w[:, inner_width:], d_conv_b[inner_width:]),
        "tensor",
    )
    d_bc_low = bc_sum.astype(jnp.bfloat16)
    d_x_normed = in_sum + against(d_bc_low, bc_all)
    g_norm_gain = jnp.sum(d_x_normed * stat_rows, axis=0)
    d_plain = d_x_normed * gain_float[None, :]
    d_tokens = (
        cotangent.astype(jnp.float32)
        + root_inv * d_plain
        - plain * root_inv**3 * jnp.mean(d_plain * plain, axis=1, keepdims=True)
    ).astype(jnp.bfloat16)
    g_w_z = over_rows(x_normed, d_z)
    g_w_x = over_rows(x_normed, d_x_low)
    g_w_dt = over_rows(x_normed, d_dt_low)
    g_w_bc = over_rows(x_normed, d_bc_low)
    small_grads = jnp.concatenate(
        [
            d_conv_w[:, :inner_width].reshape(-1),
            d_conv_b[:inner_width],
            conv_bc_sum.reshape(-1),
            conv_bcb_sum,
            g_dt_bias,
            g_a_log,
            g_d_skip,
            g_gate_gain,
        ]
    )
    shard_count = lax.axis_size("shard")
    tiled_small = jnp.broadcast_to(small_grads[None, :], (shard_count, small_grads.shape[0]))
    whole_sums = lax.psum(
        (g_norm_gain, g_w_z, g_w_x, g_w_dt, g_w_bc, g_w_out, tiled_small), "context"
    )
    owned_sums = (
        lax.psum_scatter(whole_sums[0], "shard", scatter_dimension=0, tiled=True),
        lax.psum_scatter(whole_sums[1], "shard", scatter_dimension=0, tiled=True),
        lax.psum_scatter(whole_sums[2], "shard", scatter_dimension=0, tiled=True),
        lax.psum_scatter(whole_sums[3], "shard", scatter_dimension=0, tiled=True),
        lax.psum_scatter(whole_sums[4], "shard", scatter_dimension=0, tiled=True),
        lax.psum_scatter(whole_sums[5], "shard", scatter_dimension=0, tiled=True),
        lax.psum_scatter(whole_sums[6], "shard", scatter_dimension=0, tiled=True),
    )
    small_sum = owned_sums[6][0]
    first_end = CONV * inner_width
    second_end = first_end + inner_width
    third_end = second_end + CONV * bc_width
    fourth_end = third_end + bc_width
    fifth_end = fourth_end + head_count
    sixth_end = fifth_end + head_count
    seventh_end = sixth_end + head_count
    return (
        output,
        d_tokens,
        owned_sums[0],
        owned_sums[1],
        owned_sums[2],
        owned_sums[3],
        owned_sums[4],
        small_sum[:first_end].reshape(CONV, inner_width),
        small_sum[first_end:second_end],
        small_sum[second_end:third_end].reshape(CONV, bc_width),
        small_sum[third_end:fourth_end],
        small_sum[fourth_end:fifth_end],
        small_sum[fifth_end:sixth_end],
        small_sum[sixth_end:seventh_end],
        small_sum[seventh_end:],
        owned_sums[5],
    )


def solution(mesh):
    in_specs = (
        P(("shard", "context"), None),
        P(("shard", "context")),
        P("shard"),
        P("shard", "tensor"),
        P("shard", "tensor"),
        P("shard", "tensor"),
        P("shard", None),
        P(None, "tensor"),
        P("tensor"),
        P(),
        P(),
        P("tensor"),
        P("tensor"),
        P("tensor"),
        P("tensor"),
        P("shard", "tensor"),
        P(("shard", "context"), None),
    )
    out_specs = (
        P(("shard", "context"), None),
        P(("shard", "context"), None),
        P("shard"),
        P("shard", "tensor"),
        P("shard", "tensor"),
        P("shard", "tensor"),
        P("shard", None),
        P(None, "tensor"),
        P("tensor"),
        P(),
        P(),
        P("tensor"),
        P("tensor"),
        P("tensor"),
        P("tensor"),
        P("shard", "tensor"),
    )
    return jax.shard_map(local, mesh=mesh, in_specs=in_specs, out_specs=out_specs, check_vma=False)
```

profile of v0, /device:TPU:1, one launch (start us, length us, event | category | flops | bytes accessed | tf_op | source)
XLA Modules:
  0.0 1401.7 jit_solution(3742205216731800913)
XLA Ops:
  17.8 33.5 %all-reduce.13 = bf16[1024]{0:T(1024)(128)(2,1)S(1)} all-reduce(bf16[1024]{0:T(1024)(128)(2,1)S(1)} %dynamic-update-slice), channel_id=1, replica_groups=mesh['shard'=16,'context'=2,'tensor'=4] {'shard'}, use_global_device_ids=true, to_apply=%add.13 | all-reduce | flops 1024 | bytes 4096
  54.0 25.4 %all_gather.40 = bf16[1024,256]{1,0:T(8,128)(2,1)S(1)} all-gather(bf16[64,256]{1,0:T(8,128)(2,1)S(1)} %copy-done.48), channel_id=1, replica_groups=mesh['shard'=16,'context'=2,'tensor'=4] {'shard'}, dimensions={0}, use_global_device_ids=true | all-gather | bytes 557056 | tf_op jit(solution)/shard_map/all_gather | solution.py:183
  79.5 21.1 %all-gather.2 = bf16[16,64,8]{1,2,0:T(8,128)(2,1)S(1)} all-gather(bf16[1,64,8]{1,2,0:T(8,128)(2,1)S(1)} %bitcast.611), channel_id=1, replica_groups=mesh['shard'=16,'context'=2,'tensor'=4] {'shard'}, dimensions={0}, use_global_device_ids=true | all-gather | bytes 17408 | tf_op jit(solution)/shard_map/all_gather | solution.py:182
  146.3 99.5 %while.130 = (s32[]{:T(128)}, f32[8,64,128]{2,1,0:T(8,128)S(1)}, f32[]{:T(128)}, f32[4,256,8,64]{1,0,3,2:T(4,128)}, f32[4,256]{1,0:T(4,128)S(1)}, /*index=5*/f32...) while((s32[]{:T(128)}, f32[8,64,128]{2,1,0:T(8,128)S(1)}, ...), condition=%wide.region_4.5_spmd.clone, body=%wide.region_1.4_spmd.clone.sunk | while | flops 909715968 | bytes 6825334 | solution.py:150
  155.5 12.3 dynamic_update_slice.289
  180.4 12.3 dynamic_update_slice.289
  205.2 12.3 dynamic_update_slice.289
  230.1 12.3 dynamic_update_slice.289
  257.3 88.5 %while.129 = (s32[]{:T(128)}, f32[8,64,128]{2,1,0:T(8,128)S(1)}, f32[]{:T(128)}, pred[4,256,256,8]{2,3,1,0:T(8,128)(4,1)}, f32[4,256,256,8]{2,3,1,0:T(8,128)}, /...) while((s32[]{:T(128)}, f32[8,64,128]{2,1,0:T(8,128)S(1)}, ...), condition=%wide.region_19.20_spmd.clone, body=%wide.region_16.19_spmd.clone.sunk | while | flops 506800704 | bytes 14307734 | solution.py:150
  361.0 8.5 psum.98
  405.3 222.7 %while.132 = (s32[]{:T(128)}, f32[8]{0:T(128)}, f32[8,64,128]{2,1,0:T(8,128)S(1)}, f32[4,256,8,64]{1,0,3,2:T(4,128)}, f32[4,256,128]{2,1,0:T(8,128)}, /*index=5*...) while((s32[]{:T(128)}, f32[8]{0:T(128)}, ...), condition=%wide.region_31.32_spmd.clone, body=%wide.region_20.31_spmd.clone.sunk | while | flops 1819310080 | bytes 47211384 | solution.py:150
  445.9 12.3 dynamic_update_slice.293
  501.6 12.3 dynamic_update_slice.293
  557.3 12.3 dynamic_update_slice.293
  613.0 12.3 dynamic_update_slice.293
  654.4 26.0 %all-reduce.30 = (bf16[1024,256]{0,1:T(8,128)(2,1)}, f32[1024]{0:T(1024)}, f32[256]{0:T(256)}) all-reduce(f32[1024,256]{0,1:T(8,128)S(1)} %pad_maximum_fusion, f32[1024]{0:T(1024)} %bitcast.608, f32[256]{0:T(256)} %slice.257), channel_id=1, replica_groups=mesh['shard'=16,'context'=2,'tensor'=4] {'tensor'}, use_global_device_ids=true, to_apply=%region_33.34 | all-reduce | flops 263424 | bytes 1583104 | tf_op jit(solution)/shard_map/psum | solution.py:279
  710.6 67.8 %reduce-scatter.14.cloned.1.call-done = f32[64,256]{1,0:T(8,128)} async-done(((f32[1024,256]{1,0:T(8,128)}), f32[64,256]{1,0:T(8,128)}) %reduce-scatter.14.cloned.1.call-update) | async-done | bytes 65552 | tf_op jit(solution)/shard_map/reduce_scatter | solution.py:318
  778.3 74.9 %reduce-scatter.10.cloned.1.call-done = f32[64,512]{1,0:T(8,128)} async-done(((f32[1024,512]{1,0:T(8,128)}), f32[64,512]{1,0:T(8,128)}) %reduce-scatter.10.cloned.1.call-update) | async-done | bytes 131088 | tf_op jit(solution)/shard_map/reduce_scatter | solution.py:315
  853.3 74.4 %reduce-scatter.12.cloned.1.call-done = f32[64,512]{1,0:T(8,128)} async-done(((f32[1024,512]{1,0:T(8,128)}), f32[64,512]{1,0:T(8,128)}) %reduce-scatter.12.cloned.1.call-update) | async-done | bytes 131088 | tf_op jit(solution)/shard_map/reduce_scatter | solution.py:316
  935.7 60.6 %reduce-scatter.16.cloned.1.call-done = f32[64,8]{1,0:T(8,128)} async-done(((f32[1024,8]{1,0:T(8,128)}), f32[64,8]{1,0:T(8,128)}) %reduce-scatter.16.cloned.1.call-update) | async-done | bytes 2064
  997.1 134.8 %all-reduce.25.cloned.1.call-done = f32[16,4376]{1,0:T(8,128)} async-done(((f32[16,4376]{1,0:T(8,128)}), f32[16,4376]{1,0:T(8,128)}) %all-reduce.25.cloned.1.call-update) | async-done | bytes 280080
  1133.5 39.9 %all-reduce.29.cloned.1.call-done = (f32[64,512]{1,0:T(8,128)}, f32[64,512]{1,0:T(8,128)}, f32[64,256]{1,0:T(8,128)}, f32[64,512]{0,1:T(8,128)}) async-done(((f32[64,512]{1,0:T(8,128)}, f32[64,512]{1,0:T(8,128)}, f32[64,256]{1,0:T(8,128)}, f32[64,512]{0,1:T(8,128)}), (f32[64,512]{1,0:T(8,128)}, f32[64,512]{1,0:T(8,128)}, f32[64,256]{1,0:T(8,128)}, f32[64,512]{0,1:T(8,128)})) %all-reduce.29.cloned.1.call-update) | async-done | bytes 458768 | tf_op jit(solution)/shard_map/psum | solution.py:310
  1175.1 162.7 %all-reduce.27.cloned.1.call-done = (f32[1024,1024]{1,0:T(8,128)}, f32[1024,1024]{1,0:T(8,128)}) async-done(((f32[1024,1024]{1,0:T(8,128)}, f32[1024,1024]{1,0:T(8,128)}), (f32[1024,1024]{1,0:T(8,128)}, f32[1024,1024]{1,0:T(8,128)})) %all-reduce.27.cloned.1.call-update) | async-done | bytes 8388624 | tf_op jit(solution)/shard_map/psum | solution.py:232
  1343.7 33.2 %all-reduce.14 = f32[1024]{0:T(1024)S(1)} all-reduce(f32[1024]{0:T(1024)S(1)} %get-tuple-element.2133), channel_id=4, replica_groups=mesh['shard'=16,'context'=2,'tensor'=4] {'shard'}, use_global_device_ids=true, to_apply=%region_37.38.clone | all-reduce | flops 1024 | bytes 8192
  (714 shorter events, 511.9 us)
Async XLA Ops:
  7.2 72.2 %copy-start.67 = (f32[4,512]{1,0:T(4,128)S(1)}, f32[4,512]{1,0:T(4,128)}, u32[]{:S(2)}) copy-start(f32[4,512]{1,0:T(4,128)} %param.34) | copy-start | bytes 24580
  7.2 72.3 %copy-start.69 = (bf16[64,8]{0,1:T(8,128)(2,1)S(1)}, bf16[64,8]{0,1:T(8,128)(2,1)}, u32[]{:S(2)}) copy-start(bf16[64,8]{0,1:T(8,128)(2,1)} %param.32) | copy-start | bytes 3076
  7.2 93.5 %copy-start.74 = (f32[8]{0:T(128)S(1)}, f32[8]{0:T(128)}, u32[]{:S(2)}) copy-start(f32[8]{0:T(128)} %param.39) | copy-start | bytes 100
  7.2 104.3 %all-gather.9.cloned.1.call-start = ((), (), s32[]{:S(2)}) async-start(), calls=%async_computation.5 | async-start | bytes 1114112 | tf_op jit(solution)/shard_map/all_gather | solution.py:181
  8.0 345.4 %all-gather.11.cloned.1.call-start = ((), (), s32[]{:S(2)}) async-start(), calls=%async_computation.6 | async-start | bytes 1114112 | tf_op jit(solution)/shard_map/all_gather | solution.py:180
  8.7 365.8 %all-gather.13.cloned.1.call-start = ((), (), s32[]{:S(2)}) async-start(), calls=%async_computation.7 | async-start | bytes 1114112 | tf_op jit(solution)/shard_map/all_gather | solution.py:184
  9.6 99.0 %collective-permute-start = (bf16[3]{0:T(256)(128)(2,1)S(1)}, bf16[3]{0:T(256)(128)(2,1)S(1)}, u32[]{:S(2)}, u32[]{:S(2)}) collective-permute-start(bf16[3]{0:T(256)(128)(2,1)S(1)} %slice.225), channel_id=1, source_target_pairs={{0,4},{1,5},{2,6},{3,7},{8,12},{9,13},{10,14},{11,15},{16,20},{17,... | collective-permute-start | bytes 26 | tf_op jit(solution)/shard_map/ppermute | solution.py:22
  13.7 695.1 %reduce-scatter.18.cloned.1.call-start = ((), (), s32[]{:S(2)}) async-start(), calls=%async_computation.12 | async-start | bytes 2228224
  102.9 250.5 %copy-start.2 = (bf16[1024,1024]{1,0:T(8,128)(2,1)}, bf16[1024,1024]{1,0:T(8,128)(2,1)S(1)}, u32[]{:S(2)}) copy-start(bf16[1024,1024]{1,0:T(8,128)(2,1)S(1)} %fusion.132) | copy-start | bytes 6291460
  115.2 11.6 collective-permute-start.1
  637.0 141.3 %reduce-scatter.14.cloned.1.call-start = ((), (), s32[]{:S(2)}) async-start(), calls=%async_computation.10 | async-start | bytes 1114112 | tf_op jit(solution)/shard_map/reduce_scatter | solution.py:318
  645.3 8.5 collective-permute-start.2
  683.3 170.0 %reduce-scatter.10.cloned.1.call-start = ((), (), s32[]{:S(2)}) async-start(), calls=%async_computation.8 | async-start | bytes 2228224 | tf_op jit(solution)/shard_map/reduce_scatter | solution.py:315
  686.0 241.7 %reduce-scatter.12.cloned.1.call-start = ((), (), s32[]{:S(2)}) async-start(), calls=%async_computation.9 | async-start | bytes 2228224 | tf_op jit(solution)/shard_map/reduce_scatter | solution.py:316
  690.6 305.7 %reduce-scatter.16.cloned.1.call-start = ((), (), s32[]{:S(2)}) async-start(), calls=%async_computation.11 | async-start | bytes 557056
  693.6 438.3 %all-reduce.25.cloned.1.call-start = ((), (), s32[]{:S(2)}) async-start(), calls=%async_computation.13 | async-start | bytes 573440
  704.6 223.2 %copy-start.5 = (f32[1021,768]{0,1:T(8,128)S(1)}, f32[1021,768]{0,1:T(8,128)}, u32[]{:S(2)}) copy-start(f32[1021,768]{0,1:T(8,128)} %copy-done.4) | copy-start | bytes 9409540
  704.6 468.8 %all-reduce.29.cloned.1.call-start = ((), (), s32[]{:S(2)}) async-start(), calls=%async_computation.15 | async-start | bytes 1179648 | tf_op jit(solution)/shard_map/psum | solution.py:310
  927.7 410.2 %all-reduce.27.cloned.1.call-start = ((), (), s32[]{:S(2)}) async-start(), calls=%async_computation.14 | async-start | bytes 16777216 | tf_op jit(solution)/shard_map/psum | solution.py:232
  934.9 403.0 %copy-start.8 = (bf16[1024,1024]{1,0:T(8,128)(2,1)S(1)}, bf16[1024,1024]{1,0:T(8,128)(2,1)}, u32[]{:S(2)}) copy-start(bf16[1024,1024]{1,0:T(8,128)(2,1)} %param.27) | copy-start | bytes 6291460
  934.9 403.0 %copy-start.17 = (bf16[1024,256]{0,1:T(8,128)(2,1)S(1)}, bf16[1024,256]{0,1:T(8,128)(2,1)}, u32[]{:S(2)}) copy-start(bf16[1024,256]{0,1:T(8,128)(2,1)} %get-tuple-element.2310) | copy-start | bytes 1572868
  934.9 403.0 %copy-start.19 = (bf16[1024,256]{1,0:T(8,128)(2,1)S(1)}, bf16[1024,256]{1,0:T(8,128)(2,1)}, u32[]{:S(2)}) copy-start(bf16[1024,256]{1,0:T(8,128)(2,1)} %copy-done.18) | copy-start | bytes 1572868
  934.9 403.0 %copy-start.39 = (f32[1024]{0:T(1024)S(1)}, f32[1024]{0:T(1024)}, u32[]{:S(2)}) copy-start(f32[1024]{0:T(1024)} %copy-done.38) | copy-start | bytes 12292
  934.9 403.0 %copy-start.41 = (f32[1024]{0:T(1024)S(1)}, f32[1024]{0:T(1024)}, u32[]{:S(2)}) copy-start(f32[1024]{0:T(1024)} %copy-done.40) | copy-start | bytes 12292
  (94 other events, 1048.1 us)
Sparse Core Ops, SparseCore 0:
  10.5 48.5 all-gather.8
  61.6 43.8 all-gather.10
  108.0 43.7 all-gather.12
  637.1 71.6 reduce-scatter.17
  712.5 65.7 reduce-scatter.13
  783.2 69.9 reduce-scatter.9
  857.7 69.9 reduce-scatter.11
  931.9 64.3 reduce-scatter.15
  999.3 132.5 all-reduce.24
  1134.7 38.6 all-reduce.28
  1176.0 161.8 all-reduce.26
where the time goes:
time: 1420 us; the launch traced here: 1400 us
  waiting for transfers between devices  619 us (44%)
  local copies, waits for them, and re-layouts  239 us (17%)
  matrix products  200 us (14%)
  blocking collectives  183 us (13%)
  other arithmetic  123 us (9%)
  between operations  18.6 us (1%)
    unnamed x14, waiting for transfers between devices  198 us
    psum x1, waiting for transfers between devices, local(): branch = lax.psum(against(y_normed, out_all), 'tensor')  163 us
    dynamic_update_slice x48, local copies, waits for them, and re-layouts, mixer(): lax.scan(partial(block_step, a_neg), (state_in, start_seg), blocks)  125 us
    reduce_scatter x1, waiting for transfers between devices, local(): lax.psum_scatter(whole_sums[1], 'shard', scatter_dimension=0, tiled=True)  74.9 us
    reduce_scatter x1, waiting for transfers between devices, local(): lax.psum_scatter(whole_sums[2], 'shard', scatter_dimension=0, tiled=True)  74.4 us
    reduce_scatter x1, waiting for transfers between devices, local(): lax.psum_scatter(whole_sums[4], 'shard', scatter_dimension=0, tiled=True)  67.8 us
    unnamed x2, blocking collectives  66.7 us
    dot_general x12, matrix products, block_step(): jnp.einsum('ijh,jhp->ihp', weights, x_act, precision=TOP_PRECISION)  47.2 us
  transfers between devices with their start and end apart: 14, of which 9 were waited for; matrix products, arithmetic and copies ran while one was open for 21% of the time, Pallas kernels for 0%

commit v1 on v0

v1 whole, which is shorter than its diff:
```python
from functools import partial

import jax
import jax.numpy as jnp
import numpy as np
from jax import lax
from jax.experimental import pallas as pl
from jax.experimental.pallas import tpu as pltpu
from jax.sharding import PartitionSpec as P

HEADDIM = 64
STATE = 128
CONV = 4
INNER = 2048


EPSILON = 1e-05


F32 = jnp.float32
BF = jnp.bfloat16
Q = 128
EDGE = 16
VMEM_LIMIT = 58 * 1024 * 1024


def mm(a, b):
    return lax.dot_general(a, b, (((1,), (0,)), ((), ())), preferred_element_type=F32)


def mm_nt(a, b):
    return lax.dot_general(a, b, (((1,), (1,)), ((), ())), preferred_element_type=F32)


def mm_tn(a, b):
    return lax.dot_general(a, b, (((0,), (0,)), ((), ())), preferred_element_type=F32)


def split2(v):
    hi = v.astype(BF)
    return hi, (v - hi.astype(F32)).astype(BF)


def mm2(a, b):
    hi, lo = split2(a)
    return mm(hi, b) + mm(lo, b)


def mm3_left(a, b):
    hi, lo = split2(b)
    lo2 = (b - hi.astype(F32) - lo.astype(F32)).astype(BF)
    return mm(a, hi) + (mm(a, lo) + mm(a, lo2))


def softplus(v):
    return jnp.maximum(v, 0.0) + jnp.log1p(jnp.exp(-jnp.abs(v)))


def sigmoid(v):
    return 1.0 / (1.0 + jnp.exp(-v))


def triangles():
    rows = lax.broadcasted_iota(jnp.int32, (Q, Q), 0)
    cols = lax.broadcasted_iota(jnp.int32, (Q, Q), 1)
    return rows >= cols, rows <= cols


def as_low(mask):
    return jnp.where(mask, 1.0, 0.0).astype(BF)


def halves(slab):
    lane = lax.broadcasted_iota(jnp.int32, slab.shape, 1)
    zero = jnp.zeros_like(slab)
    first = jnp.where(lane < HEADDIM, slab, zero)
    second = jnp.where(lane >= HEADDIM, slab, zero)
    return jnp.concatenate([first, second], axis=0)


def front_kernel(
    tok, etok, gain, w, colm, segr, cw, cb, dtb, alog, dsk, ex,
    xn_o, z_o, xbc_o, pre_o, dtr_o, y_o, er_o, c_o, st_o, xs,
):
    a_neg = -jnp.exp(alog[...])
    causal, _ = triangles()
    lower = as_low(causal)
    gain_row = gain[...].astype(F32)

    def normed(block):
        plain = block.astype(F32)
        root = lax.rsqrt(jnp.mean(plain * plain, axis=1, keepdims=True) + EPSILON)
        return (plain * root * gain_row).astype(BF)

    edge = mm(normed(etok[...]), w[:, 512:1280]).astype(BF)
    xbc_o[0:EDGE] = edge
    xs[0:EDGE] = edge.astype(F32)
    st_o[...] = jnp.zeros_like(st_o)
    expand = ex[...]
    dsk_e = mm2(dsk[...], expand)

    def body(b, run):
        r = pl.ds(pl.multiple_of(b * Q, Q), Q)
        rn = pl.ds(pl.multiple_of(b * Q + EDGE, EDGE), Q)
        xn = normed(tok[r])
        xn_o[r] = xn
        z_o[r] = mm(xn, w[:, 0:512])
        xb = mm(xn, w[:, 512:1280]).astype(BF)
        xbc_o[rn] = xb
        xs[rn] = xb.astype(F32)
        raw = mm(xn, w[:, 1280:1408])[:, 0:8]
        dtr_o[r] = raw
        marks = colm[r]
        acts = []
        for c in range(6):
            lanes = slice(c * 128, c * 128 + 128)
            slab = xs[pl.ds(pl.multiple_of(b * Q, Q), Q + EDGE), lanes]
            pre = cb[:, lanes] + cw[3:4, lanes] * slab[EDGE:]
            for d in range(1, 4):
                pre = pre + (cw[3 - d : 4 - d, lanes] * slab[EDGE - d : Q + EDGE - d]) * marks[:, d : d + 1]
            pre_o[r, lanes] = pre
            acts.append(pre * sigmoid(pre))
        b_low = acts[4].astype(BF)
        c_low = acts[5].astype(BF)
        c_o[r] = c_low
        dt = softplus(raw + dtb[...])
        cum = mm3_left(lower, dt * a_neg)
        er_o[r] = jnp.exp(run + cum) * marks[:, 4:5]
        cum_t = cum.T
        last = cum[Q - 1 : Q]
        enter = jnp.exp(cum) * marks[:, 5:6]
        tail = jnp.exp(last - cum) * marks[:, 6:7]
        dt_e = mm2(dt, expand)
        enter_e = mm2(enter, expand)
        tail_e = mm2(tail, expand)
        mask = causal & (marks[:, 0:1] == segr[pl.ds(b, 1), :])
        scores = jnp.where(mask, mm_nt(c_low, b_low), 0.0)
        state = st_o[...]
        inter = mm(c_low, state.astype(BF))
        pieces = []
        for p in range(4):
            lanes = slice(p * 128, p * 128 + 128)
            xdt = acts[p] * dt_e[:, lanes]
            pieces.append((xdt * tail_e[:, lanes]).astype(BF))
            ws = []
            for h in (2 * p, 2 * p + 1):
                decay = jnp.exp(jnp.minimum(cum[:, h : h + 1] - cum_t[h : h + 1, :], 0.0))
                ws.append((decay * scores).astype(BF))
            intra = mm(jnp.concatenate(ws, axis=1), halves(xdt.astype(BF)))
            y_o[r, lanes] = intra + enter_e[:, lanes] * inter[:, lanes] + dsk_e[:, lanes] * acts[p]
        fresh = mm_tn(b_low, jnp.concatenate(pieces, axis=1))
        st_o[...] = enter_e[Q - 1 : Q] * state + fresh
        return run + last

    lax.fori_loop(0, 8, body, jnp.zeros((1, 8), F32))


def back_kernel(
    dy, colm, segr, xbc, pre_r, dtr, st_in, g_in, cw, dtb, alog, dsk, ex, ext,
    dx_o, dbc_o, tail_o, ret_o, ddt_o, gcw_o, gcb_o, gh_o,
    states, acts, dpre, grad, heads,
):
    a_neg = -jnp.exp(alog[...])
    causal, anti = triangles()
    lower = as_low(causal)
    upper = as_low(anti)
    expand = ex[...]
    expand_t = ext[...]
    dsk_e = mm2(dsk[...], expand)

    def head_sum(v):
        return mm2(v, expand_t)

    states[0] = st_in[...]

    def forward(b, carry):
        r = pl.ds(pl.multiple_of(b * Q, Q), Q)
        marks = colm[r]
        dt = softplus(dtr[r] + dtb[...])
        cum = mm3_left(lower, dt * a_neg)
        last = cum[Q - 1 : Q]
        tail = jnp.exp(last - cum) * marks[:, 6:7] * dt
        keep_e = mm2(jnp.exp(last) * marks[Q - 1 : Q, 5:6], expand)
        tail_e = mm2(tail, expand)
        pieces = []
        for c in range(6):
            lanes = slice(c * 128, c * 128 + 128)
            pre = pre_r[r, lanes]
            act = pre * sigmoid(pre)
            acts[r, lanes] = act
            if c < 4:
                pieces.append((act * tail_e[:, lanes]).astype(BF))
            if c == 4:
                b_low = act.astype(BF)
        fresh = mm_tn(b_low, jnp.concatenate(pieces, axis=1))
        states[b + 1] = keep_e * states[b] + fresh
        return carry

    lax.fori_loop(0, 7, forward, 0)
    r7 = slice(7 * Q, 8 * Q)
    for c in range(6):
        lanes = slice(c * 128, c * 128 + 128)
        pre = pre_r[r7, lanes]
        acts[r7, lanes] = pre * sigmoid(pre)
    grad[...] = g_in[...]
    heads[...] = jnp.zeros_like(heads)
    dpre[0:8] = jnp.zeros((8, 768), F32)
    dpre[1032:1040] = jnp.zeros((8, 768), F32)

    def backward(i, carry):
        b = 7 - i
        r = pl.ds(pl.multiple_of(b * Q, Q), Q)
        rp = pl.ds(pl.multiple_of(b * Q + 8, 8), Q)
        marks = colm[r]
        raw = dtr[r] + dtb[...]
        dt = softplus(raw)
        cum = mm3_left(lower, dt * a_neg)
        cum_t = cum.T
        last = cum[Q - 1 : Q]
        enter = jnp.exp(cum) * marks[:, 5:6]
        tail = jnp.exp(last - cum) * marks[:, 6:7]
        dt_e = mm2(dt, expand)
        enter_e = mm2(enter, expand)
        tail_e = mm2(tail, expand)
        keep_e = enter_e[Q - 1 : Q]
        b_low = acts[r, 512:640].astype(BF)
        c_low = acts[r, 640:768].astype(BF)
        state = states[b]
        state_low = state.astype(BF)
        g_now = grad[...]
        g_low = g_now.astype(BF)
        inter = mm(c_low, state_low)
        back = mm(b_low, g_low)
        mask = causal & (marks[:, 0:1] == segr[pl.ds(b, 1), :])
        scores = jnp.where(mask, mm_nt(c_low, b_low), 0.0)
        kept = jnp.sum(state * g_now, axis=0, keepdims=True) * keep_e
        entered, tailed, e_terms, q_terms, x_terms, k_terms = [], [], [], [], [], []
        rows, cols = [], []
        d_scores = jnp.zeros((Q, Q), F32)
        for p in range(4):
            lanes = slice(p * 128, p * 128 + 128)
            x = acts[r, lanes]
            dys = dy[r, lanes]
            xdt = x * dt_e[:, lanes]
            xdt_low = xdt.astype(BF)
            ed = enter_e[:, lanes] * dys
            tx = tail_e[:, lanes] * xdt
            entered.append(ed.astype(BF))
            tailed.append(tx.astype(BF))
            dy_two = halves(dys.astype(BF))
            dw_two = mm_nt(dy_two, xdt_low)
            ws = []
            for k in range(2):
                h = 2 * p + k
                decay = jnp.exp(jnp.minimum(cum[:, h : h + 1] - cum_t[h : h + 1, :], 0.0))
                weight = decay * scores
                dw = dw_two[k * Q : k * Q + Q]
                d_scores = d_scores + decay * dw
                both = weight * dw
                rows.append(jnp.sum(both, axis=1, keepdims=True))
                cols.append(jnp.sum(both, axis=0, keepdims=True))
                ws.append(weight.astype(BF))
            dxdt = mm_tn(jnp.concatenate(ws, axis=0), dy_two) + tail_e[:, lanes] * back[:, lanes]
            e_terms.append(ed * inter[:, lanes] - tx * back[:, lanes])
            q_terms.append(jnp.sum(tx * back[:, lanes], axis=0, keepdims=True) + kept[:, lanes])
            x_terms.append(dxdt * x)
            k_terms.append(jnp.sum(dys * x, axis=0, keepdims=True))
            pre = pre_r[r, lanes]
            sig = sigmoid(pre)
            dpre[rp, lanes] = (dxdt * dt_e[:, lanes] + dsk_e[:, lanes] * dys) * (sig * (1.0 + pre * (1.0 - sig)))
        entered = jnp.concatenate(entered, axis=1)
        tailed = jnp.concatenate(tailed, axis=1)
        ds_low = jnp.where(mask, d_scores, 0.0).astype(BF)
        d_c = mm_nt(entered, state_low) + mm(ds_low, b_low)
        d_b = mm_nt(tailed, g_low) + mm_tn(ds_low, c_low)
        grad[...] = keep_e * g_now + mm_tn(c_low, entered)
        for c, value in ((4, d_b), (5, d_c)):
            lanes = slice(c * 128, c * 128 + 128)
            pre = pre_r[r, lanes]
            sig = sigmoid(pre)
            dpre[rp, lanes] = value * (sig * (1.0 + pre * (1.0 - sig)))
        d_cum = jnp.concatenate(rows, axis=1) - jnp.concatenate(cols, axis=0).T
        d_cum = d_cum + head_sum(jnp.concatenate(e_terms, axis=1))
        d_log = mm3_left(upper, d_cum) + head_sum(jnp.concatenate(q_terms, axis=1))
        d_dt = d_log * a_neg + head_sum(jnp.concatenate(x_terms, axis=1))
        d_raw = d_dt * sigmoid(raw)
        ddt_o[r] = d_raw
        heads[0:1] += jnp.sum(d_raw, axis=0, keepdims=True)
        heads[1:2] += jnp.sum(d_log * dt, axis=0, keepdims=True) * a_neg
        heads[2:3] += head_sum(jnp.concatenate(k_terms, axis=1))
        return carry

    lax.fori_loop(0, 8, backward, 0)
    gh_o[...] = heads[...]

    for c in range(6):
        lanes = slice(c * 128, c * 128 + 128)
        first = dpre[0:16, lanes]
        flags = jnp.concatenate([jnp.zeros((8, 8), F32), colm[0:8]], axis=0)
        total = jnp.zeros((8, 128), F32)
        for d in range(1, 4):
            total = total + cw[3 - d : 4 - d, lanes] * (first * flags[:, d : d + 1])[d : d + 8]
        ret_o[:, lanes] = total

        def conv(b, sums, lanes=lanes, c=c):
            r = pl.ds(pl.multiple_of(b * Q, Q), Q)
            slab = dpre[pl.ds(pl.multiple_of(b * Q + 8, 8), Q + 8), lanes]
            marks = colm[pl.ds(pl.multiple_of(b * Q, Q), Q + 8)]
            xin = xbc[pl.ds(pl.multiple_of(b * Q, Q), Q + EDGE), lanes].astype(F32)
            main = slab[0:Q]
            out = cw[3:4, lanes] * main
            new = [sums[0] + jnp.sum(main, axis=0, keepdims=True),
                   sums[1] + jnp.sum(main * xin[EDGE:], axis=0, keepdims=True)]
            for d in range(1, 4):
                masked = slab * marks[:, d : d + 1]
                out = out + cw[3 - d : 4 - d, lanes] * masked[d : d + Q]
                new.append(sums[d + 1] + jnp.sum(masked[0:Q] * xin[EDGE - d : Q + EDGE - d], axis=0, keepdims=True))
            if c < 4:
                dx_o[r, lanes] = out.astype(BF)
            else:
                dbc_o[r, slice(c * 128 - 512, c * 128 - 384)] = out

            @pl.when(b == 7)
            def _():
                tail_o[:, lanes] = out[Q - EDGE :]

            return tuple(new)

        zero = jnp.zeros((1, 128), F32)
        sums = lax.fori_loop(0, 8, conv, (zero,) * 5)
        gcb_o[:, lanes] = sums[0]
        for d in range(4):
            gcw_o[3 - d : 4 - d, lanes] = sums[d + 1]


def passed_along(value, axis, by):
    count = lax.axis_size(axis)
    pairs = [(i, i + by) for i in range(count) if 0 <= i + by < count]
    return lax.ppermute(value, axis, pairs)


def against(left, right):
    return lax.dot_general(
        left, right, (((1,), (1,)), ((), ())), preferred_element_type=jnp.float32
    )


def over_rows(left, right):
    return lax.dot_general(
        left, right, (((0,), (0,)), ((), ())), preferred_element_type=jnp.float32
    )


def silu_slope(value):
    sigma = jax.nn.sigmoid(value)
    return sigma * (1.0 + value * (1.0 - sigma))


def call(kernel, out_shapes, scratch, *args):
    return pl.pallas_call(
        kernel,
        out_shape=[jax.ShapeDtypeStruct(s, d) for s, d in out_shapes],
        in_specs=[pl.BlockSpec(memory_space=pltpu.VMEM)] * len(args),
        out_specs=[pl.BlockSpec(memory_space=pltpu.VMEM)] * len(out_shapes),
        scratch_shapes=[pltpu.VMEM(s, d) for s, d in scratch],
        compiler_params=pltpu.CompilerParams(vmem_limit_bytes=VMEM_LIMIT),
    )(*args)


def local(
    tokens,
    segment,
    norm_gain,
    w_z,
    w_x,
    w_dt,
    w_bc,
    conv_x,
    conv_xb,
    conv_bc,
    conv_bcb,
    dt_bias,
    a_log,
    d_skip,
    gate_gain,
    w_out,
    cotangent,
):
    gain_all, z_all, x_all, dt_all, bc_all, out_all = (
        lax.all_gather(norm_gain, "shard", axis=0, tiled=True),
        lax.all_gather(w_z, "shard", axis=0, tiled=True),
        lax.all_gather(w_x, "shard", axis=0, tiled=True),
        lax.all_gather(w_dt, "shard", axis=0, tiled=True),
        lax.all_gather(w_bc, "shard", axis=0, tiled=True),
        lax.all_gather(w_out, "shard", axis=0, tiled=True),
    )
    length = tokens.shape[0]
    head_count = dt_bias.shape[0]
    inner_width = head_count * HEADDIM
    bc_width = 2 * STATE
    pad_dt = jnp.pad(dt_all, ((0, 0), (0, 120)))
    w_in = jnp.concatenate([z_all, x_all, bc_all, pad_dt], axis=1)
    edge_tokens, edge_ids = passed_along((tokens[length - EDGE :], segment[length - EDGE :]), "context", 1)
    seg = segment
    ext_ids = jnp.concatenate([edge_ids[-3:], seg])
    start_seg = jnp.where(edge_ids[-1] == seg[0], seg[0], -1)
    blocks = seg.reshape(length // Q, Q)
    before = jnp.concatenate([start_seg[None], blocks[:-1, -1]])
    marks = [seg.astype(F32)]
    marks += [(ext_ids[3 - d : 3 - d + length] == seg).astype(F32) for d in (1, 2, 3)]
    marks += [(seg == start_seg).astype(F32)]
    marks += [(blocks == before[:, None]).astype(F32).reshape(-1)]
    marks += [(blocks == blocks[:, -1:]).astype(F32).reshape(-1)]
    marks += [jnp.zeros((length,), F32)]
    colm = jnp.pad(jnp.stack(marks, axis=1), ((0, 8), (0, 0)))
    segr = blocks.astype(F32)
    conv_w = jnp.concatenate([conv_x, conv_bc], axis=1)
    conv_b = jnp.concatenate([conv_xb, conv_bcb])[None]
    expand_np = np.kron(np.eye(8), np.ones((1, HEADDIM)))
    expand = jnp.asarray(expand_np, BF)
    expand_t = jnp.asarray(expand_np.T, BF)
    wide = (length, inner_width)
    x_normed, z_gate, xbc, pre, dt_raw, y_zero, enter_decay, c_act, state_local = call(
        front_kernel,
        [((length, 1024), BF), (wide, F32), ((length + EDGE, 768), BF), ((length, 768), F32), ((length, 8), F32),
         (wide, F32), ((length, 8), F32), ((length, STATE), BF), ((STATE, inner_width), F32)],
        [((length + EDGE, 768), F32)],
        tokens, edge_tokens, gain_all[None], w_in, colm, segr, conv_w, conv_b, dt_bias[None], a_log[None], d_skip[None], expand,
    )
    plain = tokens.astype(F32)
    root_inv = lax.rsqrt(jnp.mean(plain * plain, axis=1, keepdims=True) + EPSILON)
    gain_float = gain_all.astype(F32)
    state_in = passed_along(state_local, "context", 1)
    decay_e = jnp.repeat(enter_decay, HEADDIM, axis=1)
    y_mixed = y_zero + decay_e * jnp.dot(c_act, state_in.astype(BF), preferred_element_type=F32)
    gate_act = jax.nn.silu(z_gate)
    gated = y_mixed * gate_act
    d_y_normed = jnp.dot(cotangent, out_all, preferred_element_type=F32)
    d_scaled = d_y_normed * gate_gain[None, :]
    sums = lax.psum(jnp.stack([jnp.sum(gated * gated, axis=1), jnp.sum(d_scaled * gated, axis=1)]), "tensor")
    gate_root = lax.rsqrt(sums[0] / INNER + EPSILON)[:, None]
    y_normed = (gated * gate_root * gate_gain[None, :]).astype(BF)
    branch_part = against(y_normed, out_all).astype(BF)
    g_w_out = over_rows(cotangent, y_normed).astype(BF)
    g_gate_gain = jnp.sum(d_y_normed * gated * gate_root, axis=0)
    d_gated = gate_root * d_scaled - gated * gate_root**3 * (sums[1] / INNER)[:, None]
    d_y = d_gated * gate_act
    d_z = (d_gated * y_mixed * silu_slope(z_gate)).astype(BF)
    d_carry = over_rows(c_act, (d_y * decay_e).astype(BF)).astype(BF)
    d_state_out = passed_along(d_carry, "context", -1).astype(F32)
    d_x_first, d_bc_first, tail_rows, back_rows, d_dt_raw, g_conv_w, g_conv_b, g_heads = call(
        back_kernel,
        [(wide, BF), ((length, bc_width), F32), ((EDGE, 768), F32), ((8, 768), F32), ((length, 8), F32),
         ((CONV, 768), F32), ((1, 768), F32), ((8, 8), F32)],
        [((8, STATE, inner_width), F32), ((length, 768), F32), ((length + 16, 768), F32), ((STATE, inner_width), F32), ((8, 8), F32)],
        d_y, colm, segr, xbc, pre, dt_raw, state_in, d_state_out, conv_w, dt_bias[None], a_log[None], d_skip[None], expand, expand_t,
    )
    returned = passed_along(back_rows, "context", -1)
    tail_rows = tail_rows + jnp.pad(returned, ((EDGE - 8, 0), (0, 0)))
    d_x_low = lax.dynamic_update_slice(d_x_first, tail_rows[:, :inner_width].astype(BF), (length - EDGE, 0))
    d_bc = lax.dynamic_update_slice(d_bc_first, tail_rows[:, inner_width:], (length - EDGE, 0))
    d_dt_low = d_dt_raw.astype(BF)
    part_in = (against(d_z, z_all) + against(d_x_low, x_all) + against(d_dt_low, dt_all)).astype(BF)
    g_w_z = over_rows(x_normed, d_z).astype(BF)
    g_w_x = over_rows(x_normed, d_x_low).astype(BF)
    g_w_dt = over_rows(x_normed, d_dt_low).astype(BF)
    in_sum, bc_sum, branch, conv_bc_sum, conv_bcb_sum = lax.psum(
        (part_in, d_bc.astype(BF), branch_part, g_conv_w[:, inner_width:], g_conv_b[:, inner_width:]), "tensor"
    )
    output = (plain + branch).astype(BF)
    d_bc_low = bc_sum.astype(BF)
    d_x_normed = in_sum + against(d_bc_low, bc_all)
    stat_rows = plain * root_inv
    g_norm_gain = jnp.sum(d_x_normed * stat_rows, axis=0)
    d_plain = d_x_normed * gain_float[None, :]
    d_tokens = (
        cotangent.astype(F32)
        + root_inv * d_plain
        - plain * root_inv**3 * jnp.mean(d_plain * plain, axis=1, keepdims=True)
    ).astype(BF)
    g_w_bc = over_rows(x_normed, d_bc_low).astype(BF)
    whole = jnp.concatenate([g_w_z, g_w_x, g_w_out, g_w_bc, g_w_dt], axis=1)
    owned = lax.psum(lax.psum_scatter(whole, "shard", scatter_dimension=0, tiled=True), "context").astype(F32)
    small, gn = lax.psum((jnp.concatenate([g_conv_w[:, :inner_width].reshape(-1), g_conv_b[0, :inner_width], conv_bc_sum.reshape(-1),
        conv_bcb_sum[0], g_heads[0], g_heads[1], g_heads[2], g_gate_gain]), g_norm_gain), ("shard", "context"))
    own_norm = lax.dynamic_slice(gn, (lax.axis_index("shard") * 64,), (64,))
    cuts = np.cumsum([2048, 512, 1024, 256, 8, 8, 8])
    pieces = jnp.split(small, cuts)
    return (
        output,
        d_tokens,
        own_norm,
        owned[:, 0:512],
        owned[:, 512:1024],
        owned[:, 1792:1800],
        owned[:, 1536:1792],
        pieces[0].reshape(CONV, inner_width),
        pieces[1],
        pieces[2].reshape(CONV, bc_width),
        pieces[3],
        pieces[4],
        pieces[5],
        pieces[6],
        pieces[7],
        owned[:, 1024:1536],
    )


def solution(mesh):
    in_specs = (
        P(("shard", "context"), None),
        P(("shard", "context")),
        P("shard"),
        P("shard", "tensor"),
        P("shard", "tensor"),
        P("shard", "tensor"),
        P("shard", None),
        P(None, "tensor"),
        P("tensor"),
        P(),
        P(),
        P("tensor"),
        P("tensor"),
        P("tensor"),
        P("tensor"),
        P("shard", "tensor"),
        P(("shard", "context"), None),
    )
    out_specs = (
        P(("shard", "context"), None),
        P(("shard", "context"), None),
        P("shard"),
        P("shard", "tensor"),
        P("shard", "tensor"),
        P("shard", "tensor"),
        P("shard", None),
        P(None, "tensor"),
        P("tensor"),
        P(),
        P(),
        P("tensor"),
        P("tensor"),
        P("tensor"),
        P("tensor"),
        P("shard", "tensor"),
    )
    return jax.shard_map(local, mesh=mesh, in_specs=in_specs, out_specs=out_specs, check_vma=False)
```

time: 1420 us -> 530 us (0.37); the launches traced: 1400 us -> 529 us
  waiting for transfers between devices: 619 us -> 137 us
  local copies, waits for them, and re-layouts: 239 us -> 38.8 us
  matrix products: 200 us -> 37 us
  other arithmetic: 123 us -> 18.5 us
  Pallas kernels: 0 us -> 48.6 us
  blocking collectives: 183 us -> 222 us
    reduce_scatter x3 -> x0, waiting for transfers between devices: 217 us -> none  [the longest x1 74.9 us: local(): lax.psum_scatter(whole_sums[1], 'shard', scatter_dimension=0, tiled=True)]
    unnamed x14 -> x7, waiting for transfers between devices: 198 us -> 1.44 us
    dot_general x67 -> x2, matrix products: 159 us -> 8.98 us  [the longest x1 7.24 us: local(): d_y_normed = jnp.dot(cotangent, out_all, preferred_element_type=F32)]
    dynamic_update_slice x48 -> x2, local copies, waits for them, and re-layouts: 125 us -> 0.01 us  [the longest x1 0.01 us: local(): lax.dynamic_update_slice(d_x_first, tail_rows[:, :inner_width].astype(BF)...]
    psum x4 -> x3, blocking collectives: 47.4 us -> 142 us  [the longest x1 126 us: local(): lax.psum((jnp.concatenate([g_conv_w[:, :inner_width].reshape(-1), g_conv_...]
    psum x2, waiting for transfers between devices: 203 us -> 120 us  [the longest x1 92.9 us: local(): lax.psum((part_in, d_bc.astype(BF), branch_part, g_conv_w[:, inner_width:...]
    pallas_call x0 -> x2, Pallas kernels: none -> 48.6 us  [call(): pl.pallas_call(kernel, out_shape=[jax.ShapeDtypeStruct(s, d) for s, d in...]
    dynamic_slice x28 -> x1, local copies, waits for them, and re-layouts: 39.1 us -> 0.58 us  [local(): own_norm = lax.dynamic_slice(gn, (lax.axis_index('shard') * 64,), (64,))]
  transfers between devices with their start and end apart: 14 -> 11, of which waited for: 9 -> 5; matrix products, arithmetic and copies ran while one was open for 21% -> 10% of each run, Pallas kernels for 0% -> 4%
where the time goes in v1:
time: 530 us; the launch traced here: 529 us
  blocking collectives  222 us (42%)
  waiting for transfers between devices  137 us (26%)
  Pallas kernels  48.6 us (9%)
  local copies, waits for them, and re-layouts  38.8 us (7%)
  matrix products  37 us (7%)
  other arithmetic  18.5 us (3%)
  between operations  17.2 us (3%)
  starting transfers between devices  9.85 us (2%)
    psum x1, blocking collectives, local(): lax.psum((jnp.concatenate([g_conv_w[:, :inner_width].reshape(-1), g_conv_...  126 us
    psum x1, waiting for transfers between devices, local(): lax.psum((part_in, d_bc.astype(BF), branch_part, g_conv_w[:, inner_width:...  92.9 us
    pallas_call x2, Pallas kernels, call(): pl.pallas_call(kernel, out_shape=[jax.ShapeDtypeStruct(s, d) for s, d in...  48.6 us
    unnamed x1, blocking collectives  32.7 us
    psum x1, waiting for transfers between devices, local(): lax.psum(lax.psum_scatter(whole, 'shard', scatter_dimension=0, tiled=True...  27.3 us
    all_gather x1, blocking collectives, local(): lax.all_gather(w_dt, 'shard', axis=0, tiled=True)  25.1 us
    all_gather x1, blocking collectives, local(): lax.all_gather(w_bc, 'shard', axis=0, tiled=True)  21.7 us
    unnamed x62, local copies, waits for them, and re-layouts  18.1 us
  transfers between devices with their start and end apart: 11, of which 5 were waited for; matrix products, arithmetic and copies ran while one was open for 10% of the time, Pallas kernels for 4%

profile of v1, /device:TPU:1, one launch (start us, length us, event | category | flops | bytes accessed | tf_op | source)
XLA Modules:
  0.0 528.7 jit_solution(9536249558053126740)
XLA Ops:
  9.5 4.0 collective-permute-start.1
  18.6 25.1 %all-gather = bf16[16,64,8]{1,2,0:T(8,128)(2,1)S(1)} all-gather(bf16[1,64,8]{1,2,0:T(8,128)(2,1)} %bitcast.99), channel_id=1, replica_groups=mesh['shard'=16,'context'=2,'tensor'=4] {'shard'}, dimensions={0}, use_global_device_ids=true | all-gather | bytes 17408 | tf_op jit(solution)/shard_map/all_gather | solution.py:393
  46.6 32.7 %all-reduce.3 = bf16[1024]{0:T(1024)(128)(2,1)S(1)} all-reduce(bf16[1024]{0:T(1024)(128)(2,1)S(1)} %dynamic-update-slice), channel_id=1, replica_groups=mesh['shard'=16,'context'=2,'tensor'=4] {'shard'}, use_global_device_ids=true, to_apply=%add.3 | all-reduce | flops 1024 | bytes 4096
  83.4 21.7 %all_gather.21 = bf16[1024,256]{1,0:T(8,128)(2,1)S(1)} all-gather(bf16[64,256]{1,0:T(8,128)(2,1)} %param.25), channel_id=1, replica_groups=mesh['shard'=16,'context'=2,'tensor'=4] {'shard'}, dimensions={0}, use_global_device_ids=true | all-gather | bytes 557056 | tf_op jit(solution)/shard_map/all_gather | solution.py:394
  110.4 2.9 fusion.9.w
  113.9 18.7 %shard_map.306 = (bf16[1024,1024]{1,0:T(8,128)(2,1)}, f32[1024,512]{1,0:T(8,128)}, bf16[1040,768]{1,0:T(8,128)(2,1)}, f32[1024,768]{1,0:T(8,128)}, f32[1024,8]{1...) custom-call(bf16[1024,1024]{1,0:T(8,128)(2,1)} %tok.1, ...), custom_call_target="tpu_custom_call" | custom-call | tf_op jit(solution)/shard_map/pallas_call | solution.py:360
  138.6 4.1 collective-permute-done.2.st_in
  144.5 8.2 %all-gather.9.cloned.1.call-done = bf16[1024,512]{1,0:T(8,128)(2,1)} async-done(((bf16[64,512]{1,0:T(8,128)(2,1)}), bf16[1024,512]{1,0:T(8,128)(2,1)}) %all-gather.9.cloned.1.call-update) | async-done | bytes 1048592 | tf_op jit(solution)/shard_map/all_gather | solution.py:395
  152.7 7.2 %multiply_reduce_fusion.2 = (f32[1024]{0:T(1024)S(1)}, f32[1024]{0:T(1024)S(1)}, f32[1024,512]{1,0:T(8,128)}, f32[1024,512]{1,0:T(8,128)}) fusion(f32[512]{0:T(512)S(1)} %copy-done.19, f32[1024,512]{1,0:T(8,128)} %get-tuple-element.37, f32[1024,512]{1,0:T(8,128)} %get-tuple-element.33, f32[1024,512]{1,0:T(8,128)S(1)} %copy.60, f32[1024,512]{1,0:T(8,128)} %fusion.21, ...), kind=kOutput, calls=%fused_computation.24 | convolution fusion | flops 1080031232 | bytes 15738880 | tf_op jit(solution)/shard_map/dot_general | solution.py:438
  160.0 9.7 %psum.63 = f32[2,1024]{1,0:T(2,128)S(1)} all-reduce(f32[2,1024]{1,0:T(2,128)S(1)} %pad_maximum_fusion), channel_id=1, replica_groups=mesh['shard'=16,'context'=2,'tensor'=4] {'tensor'}, use_global_device_ids=true, to_apply=%region_2.3 | all-reduce | flops 2048 | bytes 16384 | tf_op jit(solution)/shard_map/psum | solution.py:440
  169.7 4.9 multiply_convert_fusion.1
  178.5 3.1 collective-permute-done.3
  182.3 29.9 %shard_map.307 = (bf16[1024,512]{1,0:T(8,128)(2,1)}, f32[1024,256]{1,0:T(8,128)}, f32[16,768]{1,0:T(8,128)}, f32[8,768]{1,0:T(8,128)}, f32[1024,8]{1,0:T(8,128)}...) custom-call(f32[1024,512]{1,0:T(8,128)} %copy-done.1, f32[1032,8]{1,0:T(8,128)} %pad.13.colm, ...), custom_call_target="tpu_custom_call" | custom-call | tf_op jit(solution)/shard_map/pallas_call | solution.py:360
  214.0 4.5 convolution_convert_fusion
  224.2 4.1 fusion.12
  228.2 2.4 fusion.11
  233.0 92.9 %all-reduce.12.cloned.1.call-done = (bf16[1024,256]{1,0:T(8,128)(2,1)}, bf16[1024,1024]{1,0:T(8,128)(2,1)}, bf16[1024,1024]{1,0:T(8,128)(2,1)}) async-done(((bf16[1024,256]{1,0:T(8,128)(2,1)}, bf16[1024,1024]{1,0:T(8,128)(2,1)}, bf16[1024,1024]{1,0:T(8,128)(2,1)}), (bf16[1024,256]{1,0:T(8,128)(2,1)}, bf16[1024,1024]{1,0:T(8,128)(2,1)}, bf16[1024,1024]{1,0:T(8,128)(2,1)})) %all-reduce.12.cloned.1.call-update) | async-done | bytes 4718608 | tf_op jit(solution)/shard_map/psum | solution.py:467
  326.0 3.4 fusion.15
  330.4 6.1 %copy.68 = bf16[1024,1800]{1,0:T(8,128)(2,1)} copy(bf16[1024,1800]{0,1:T(8,128)(2,1)} %fusion.16) | data formatting | bytes 7372800
  338.7 6.6 %all-reduce.5 = (f32[1024]{0:T(1024)S(1)}, f32[256]{0:T(256)S(1)}) all-reduce(f32[1024]{0:T(1024)S(1)} %bitcast.88, f32[256]{0:T(256)S(1)} %bitcast.90), channel_id=1, replica_groups=mesh['shard'=16,'context'=2,'tensor'=4] {'tensor'}, use_global_device_ids=true, to_apply=%region_12.13 | all-reduce | flops 1280 | bytes 10240 | tf_op jit(solution)/shard_map/psum | solution.py:467
  346.1 5.2 fusion.8
  351.4 125.8 %all-reduce.4 = (f32[1024]{0:T(1024)S(1)}, f32[4376]{0:T(1024)S(1)}) all-reduce(f32[1024]{0:T(1024)S(1)} %get-tuple-element.98, f32[4376]{0:T(1024)S(1)} %concatenate.27), channel_id=1, replica_groups=mesh['shard'=16,'context'=2,'tensor'=4] {'shard','context'}, use_global_device_ids=true, to_apply=%region_9.10 | all-reduce | flops 5400 | bytes 43200 | tf_op jit(solution)/shard_map/psum | solution.py:484
  477.2 5.5 %fusion.5 = (bf16[1024,1024]{1,0:T(8,128)(2,1)}, bf16[1024,1024]{1,0:T(8,128)(2,1)}) fusion(bf16[1024,1024]{1,0:T(8,128)(2,1)S(1)} %copy-done, bf16[1024,1024]{1,0:T(8,128)(2,1)} %param.35, f32[1024,1024]{1,0:T(8,128)} %get-tuple-element.142, f32[1024]{0:T(1024)S(1)} %broadcast_multiply_fusion, f32[1024]{0:T(1024)S(1)} %get-tuple-element.131, ...), kind=kLoop, calls=%fused_computation.11 | loop fusion | flops 12582912 | bytes 14696448 | tf_op jit(solution)/shard_map/convert_element_type | solution.py:480
  488.3 27.3 %all-reduce.10.cloned.1.call-done = bf16[64,1800]{0,1:T(8,128)(2,1)} async-done(((bf16[64,1800]{0,1:T(8,128)(2,1)}), bf16[64,1800]{0,1:T(8,128)(2,1)}) %all-reduce.10.cloned.1.call-update) | async-done | bytes 230416 | tf_op jit(solution)/shard_map/psum | solution.py:483
  (139 shorter events, 55.4 us)
Async XLA Ops:
  7.2 103.2 %all-gather.5.cloned.1.call-start = ((), (), s32[]{:S(2)}) async-start(), calls=%async_computation.1 | async-start | bytes 1114112 | tf_op jit(solution)/shard_map/all_gather | solution.py:391
  7.9 102.5 %all-gather.7.cloned.1.call-start = ((), (), s32[]{:S(2)}) async-start(), calls=%async_computation.2 | async-start | bytes 1114112 | tf_op jit(solution)/shard_map/all_gather | solution.py:392
  8.7 144.0 %all-gather.9.cloned.1.call-start = ((), (), s32[]{:S(2)}) async-start(), calls=%async_computation.3 | async-start | bytes 1114112 | tf_op jit(solution)/shard_map/all_gather | solution.py:395
  9.5 96.2 %collective-permute-start.1 = (s32[16]{0:T(128)S(1)}, s32[16]{0:T(128)S(1)}, u32[]{:S(2)}, u32[]{:S(2)}) collective-permute-start(s32[16]{0:T(128)S(1)} %slice.81), channel_id=1, source_target_pairs={{0,4},{1,5},{2,6},{3,7},{8,12},{9,13},{10,14},{11,15},{16,20},{17,... | collective-permute-start | bytes 200 | tf_op jit(solution)/shard_map/ppermute | solution.py:339
  14.3 99.0 %collective-permute-start = (bf16[16,1024]{1,0:T(8,128)(2,1)S(1)}, bf16[16,1024]{1,0:T(8,128)(2,1)S(1)}, u32[]{:S(2)}, u32[]{:S(2)}) collective-permute-start(bf16[16,1024]{1,0:T(8,128)(2,1)S(1)} %slice.80), channel_id=1, source_target_pairs={{0,4},{1,5},{2,6},{3,7},{8,12},{9,13},{10,14},{11,15},{16,20},{17,... | collective-permute-start | bytes 98312 | tf_op jit(solution)/shard_map/ppermute | solution.py:339
  15.6 310.4 %all-reduce.12.cloned.1.call-start = ((), (), s32[]{:S(2)}) async-start(), calls=%async_computation.6 | async-start | bytes 9437184 | tf_op jit(solution)/shard_map/psum | solution.py:467
  81.3 31.9 %copy-start.14 = (f32[4,768]{1,0:T(4,128)}, f32[4,768]{1,0:T(4,128)S(1)}, u32[]{:S(2)}) copy-start(f32[4,768]{1,0:T(4,128)S(1)} %constant_dynamic-update-slice_fusion.cw) | copy-start | bytes 36868
  132.6 10.2 %collective-permute-start.2 = (f32[128,512]{1,0:T(8,128)}, f32[128,512]{1,0:T(8,128)S(1)}, u32[]{:S(2)}, u32[]{:S(2)}) collective-permute-start(f32[128,512]{1,0:T(8,128)} %get-tuple-element.36), channel_id=1, source_target_pairs={{0,4},{1,5},{2,6},{3,7},{8,12},{9,13},{10,14},{11,15},{16,20},{17,... | collective-permute-start | bytes 786440 | tf_op jit(solution)/shard_map/ppermute | solution.py:339
  136.6 6.1 %copy-start.10 = (bf16[1024,128]{1,0:T(8,128)(2,1)S(1)}, bf16[1024,128]{1,0:T(8,128)(2,1)}, u32[]{:S(2)}) copy-start(bf16[1024,128]{1,0:T(8,128)(2,1)} %get-tuple-element.35) | copy-start | bytes 786436
  138.6 14.1 %copy-start.19 = (f32[512]{0:T(512)S(1)}, f32[512]{0:T(512)}, u32[]{:S(2)}) copy-start(f32[512]{0:T(512)} %param.33) | copy-start | bytes 6148
  142.8 17.2 %copy-start.9 = (f32[128,512]{1,0:T(8,128)}, f32[128,512]{1,0:T(8,128)S(1)}, u32[]{:S(2)}) copy-start(f32[128,512]{1,0:T(8,128)S(1)} %collective-permute-done.2.st_in) | copy-start | bytes 786436
  174.6 2.6 copy-start.7
  175.9 5.7 %collective-permute-start.3 = (bf16[128,512]{1,0:T(8,128)(2,1)S(1)}, bf16[128,512]{1,0:T(8,128)(2,1)S(1)}, u32[]{:S(2)}, u32[]{:S(2)}) collective-permute-start(bf16[128,512]{1,0:T(8,128)(2,1)S(1)} %convolution_convert_fusion.5), channel_id=1, source_target_pairs={{4,0},{5,1},{6,2},{7,3},{12,8},{13,9},{14,10},{15,11},{20,16},{21,... | collective-permute-start | bytes 393224 | tf_op jit(solution)/shard_map/ppermute | solution.py:339
  212.2 6.3 %copy-start.15 = (f32[16,768]{1,0:T(8,128)S(1)}, f32[16,768]{1,0:T(8,128)}, u32[]{:S(2)}) copy-start(f32[16,768]{1,0:T(8,128)} %get-tuple-element.42) | copy-start | bytes 147460
  212.2 6.3 %copy-start.20 = (bf16[1024,512]{1,0:T(8,128)(2,1)S(1)}, bf16[1024,512]{1,0:T(8,128)(2,1)}, u32[]{:S(2)}) copy-start(bf16[1024,512]{1,0:T(8,128)(2,1)} %get-tuple-element.41) | copy-start | bytes 3145732
  212.2 6.3 %copy-start.11 = (f32[1024,256]{1,0:T(8,128)S(1)}, f32[1024,256]{1,0:T(8,128)}, u32[]{:S(2)}) copy-start(f32[1024,256]{1,0:T(8,128)} %get-tuple-element.45) | copy-start | bytes 3145732
  212.3 7.2 %copy-start.12 = (bf16[1024,512]{1,0:T(8,128)(2,1)S(1)}, bf16[1024,512]{1,0:T(8,128)(2,1)}, u32[]{:S(2)}) copy-start(bf16[1024,512]{1,0:T(8,128)(2,1)} %all-gather.7.cloned.1.call-done) | copy-start | bytes 3145732
  212.3 6.2 %collective-permute-start.4 = (f32[8,768]{1,0:T(8,128)}, f32[8,768]{1,0:T(8,128)S(1)}, u32[]{:S(2)}, u32[]{:S(2)}) collective-permute-start(f32[8,768]{1,0:T(8,128)} %get-tuple-element.43), channel_id=1, source_target_pairs={{4,0},{5,1},{6,2},{7,3},{12,8},{13,9},{14,10},{15,11},{20,16},{21,... | collective-permute-start | bytes 73736 | tf_op jit(solution)/shard_map/ppermute | solution.py:339
  223.0 259.7 %reduce-scatter.4.cloned.1.call-start = ((), (), s32[]{:S(2)}) async-start(), calls=%async_computation.5 | async-start | bytes 4177920
  224.2 4.1 copy-start.4
  224.2 4.1 copy-start.22
  326.0 3.4 copy-start.5
  336.5 9.6 %copy-start.23 = (bf16[1024,256]{1,0:T(8,128)(2,1)S(1)}, bf16[1024,256]{1,0:T(8,128)(2,1)}, u32[]{:S(2)}) copy-start(bf16[1024,256]{1,0:T(8,128)(2,1)} %get-tuple-element.106) | copy-start | bytes 1572868
  336.5 179.1 %all-reduce.10.cloned.1.call-start = ((), (), s32[]{:S(2)}) async-start(), calls=%async_computation.4 | async-start | bytes 921600 | tf_op jit(solution)/shard_map/psum | solution.py:483
  (11 other events, 19.9 us)
Sparse Core Ops, SparseCore 0:
  10.5 48.5 all-gather.4
  61.5 43.7 all-gather.6
  107.8 44.8 all-gather.8
  223.1 102.8 all-reduce.11
  336.6 77.4 reduce-scatter.3
  484.8 30.7 all-reduce.9

commit v2 on v1

--- a/solution.py
+++ b/solution.py
@@ -79,13 +79,14 @@
 
 
 def front_kernel(
-    tok, etok, gain, w, colm, segr, cw, cb, dtb, alog, dsk, ex,
-    xn_o, z_o, xbc_o, pre_o, dtr_o, y_o, er_o, c_o, st_o, xs,
+    tok, etok, w, colm, segr, cw, cb, dtb, alog, dsk, ex,
+    xn_o, z_o, xbc_o, pre_o, dtr_o, y_o, er_o, c_o, st_o, gain_o, xs,
 ):
     a_neg = -jnp.exp(alog[...])
     causal, _ = triangles()
     lower = as_low(causal)
-    gain_row = gain[...].astype(F32)
+    gain_row = w[:, 1280:1408].astype(F32).T[8:9]
+    gain_o[...] = gain_row
 
     def normed(block):
         plain = block.astype(F32)
@@ -157,7 +158,7 @@
 
 def back_kernel(
     dy, colm, segr, xbc, pre_r, dtr, st_in, g_in, cw, dtb, alog, dsk, ex, ext,
-    dx_o, dbc_o, tail_o, ret_o, ddt_o, gcw_o, gcb_o, gh_o,
+    dx_o, dbc_o, tail_o, ret_o, ddt_o, small_o,
     states, acts, dpre, grad, heads,
 ):
     a_neg = -jnp.exp(alog[...])
@@ -291,7 +292,8 @@
         return carry
 
     lax.fori_loop(0, 8, backward, 0)
-    gh_o[...] = heads[...]
+    small_o[...] = jnp.zeros_like(small_o)
+    small_o[24:32, 0:8] = heads[...]
 
     for c in range(6):
         lanes = slice(c * 128, c * 128 + 128)
@@ -328,9 +330,265 @@
 
         zero = jnp.zeros((1, 128), F32)
         sums = lax.fori_loop(0, 8, conv, (zero,) * 5)
-        gcb_o[:, lanes] = sums[0]
+        at = 16 + c if c < 4 else 36 + c
+        small_o[at : at + 1] = sums[0]
         for d in range(4):
-            gcw_o[3 - d : 4 - d, lanes] = sums[d + 1]
+            at = (3 - d) * 4 + c if c < 4 else 28 + (3 - d) * 2 + c
+            small_o[at : at + 1] = sums[d + 1]
+
+
+MESH = pl.DeviceIdType.MESH
+
+
+class Links:
+    def __init__(self, send, recv):
+        self.send, self.recv, self.count, self.started = send, recv, 0, []
+
+    def copy(self, src, dst, device):
+        made = pltpu.make_async_remote_copy(
+            src_ref=src,
+            dst_ref=dst,
+            send_sem=self.send.at[self.count],
+            recv_sem=self.recv.at[self.count],
+            device_id=device,
+            device_id_type=MESH,
+        )
+        self.count += 1
+        self.started.append(made)
+        made.start()
+        return made
+
+    def finish(self):
+        for made in self.started:
+            made.wait_send()
+
+
+def arrival(like, dst, links_recv, device):
+    return pltpu.make_async_remote_copy(
+        src_ref=dst, dst_ref=dst, send_sem=links_recv, recv_sem=links_recv, device_id=device, device_id_type=MESH
+    )
+
+
+def greet(devices):
+    barrier = pltpu.get_barrier_semaphore()
+    for device in devices:
+        pl.semaphore_signal(barrier, inc=1, device_id=device, device_id_type=MESH)
+    pl.semaphore_wait(barrier, len(devices))
+
+
+def places():
+    shard, context, tensor = (lax.axis_index(name) for name in ("shard", "context", "tensor"))
+    core, chip = lax.rem(shard, 2), lax.div(shard, 2)
+
+    def at(shard_to=None, context_to=None, tensor_to=None):
+        return (
+            shard if shard_to is None else shard_to,
+            context if context_to is None else context_to,
+            tensor if tensor_to is None else tensor_to,
+        )
+
+    chips = [None] + [lax.rem(chip + k, 8) for k in range(1, 8)]
+    sibling = at(shard_to=chip * 2 + (1 - core))
+    others = [None] + [at(shard_to=c * 2 + core) for c in chips[1:]]
+    partner = at(context_to=1 - context)
+    ranks = [None] + [lax.rem(tensor + k, 4) for k in range(1, 4)]
+    group = [None] + [at(tensor_to=t) for t in ranks[1:]]
+    return shard, context, tensor, core, chip, chips, sibling, others, partner, ranks, group
+
+
+def gather_kernel(wz, wx, wbc, wdt, norm, wo, etok, eseg, all_o, etok_o, eseg_o, mine, etok_b, send, recv):
+    shard, context, tensor, core, chip, chips, sibling, others, partner, ranks, group = places()
+    mine[:, 0:512] = wz[...]
+    mine[:, 512:1024] = wx[...]
+    mine[:, 1024:1280] = wbc[...]
+    mine[:, 1280:1408] = jnp.zeros((64, 128), BF)
+    mine[:, 1280:1288] = wdt[...]
+    mine[:, 1288:1289] = norm[...]
+    mine[:, 1408:1920] = wo[...]
+    greet([sibling, partner] + others[1:])
+    links = Links(send, recv)
+    tokens_in = links.copy(etok, etok_b, partner)
+    seg_in = links.copy(eseg, eseg_o, partner)
+    first = [None]
+    for k in range(1, 8):
+        first.append(links.copy(mine, all_o.at[shard], others[k]))
+    base = links.count
+    links.copy(mine, all_o.at[shard], sibling)
+    all_o[shard] = mine[...]
+    for k in (1, 7, 2, 6, 3, 5, 4):
+        source = lax.rem(chip + 8 - k, 8) * 2 + core
+        slot = all_o.at[source]
+        arrival(mine, slot, recv.at[1 + k], others[k]).wait_recv()
+        links.copy(slot, slot, sibling)
+    for n, k in enumerate((0, 1, 7, 2, 6, 3, 5, 4)):
+        source = lax.rem(chip + 8 - k, 8) * 2 + (1 - core)
+        arrival(mine, all_o.at[source], recv.at[base + n], sibling).wait_recv()
+    tokens_in.wait_recv()
+    seg_in.wait_recv()
+    links.finish()
+    etok_o[...] = jnp.where(context > 0, etok_b[...].astype(F32), 0.0).astype(BF)
+
+
+def tail_kernel(
+    part, branch, dbc, gz, gx, go, gd, small, gate, gain, tok, cot, xn, w,
+    out_o, dtok_o, oz, ox, oo, odt, obc, onorm, small_o,
+    rp, rbc, rb, sz, sx, so, sd, chunk, rg, cs, cr,
+    g2, s2, chunk2, rg2, c2s, c2r, t2,
+    sm, sm_s, sm_c, sm_x, sm_r, sm_t,
+    tok_r, cot_r, xn_r, wbc, send, recv, local_sem,
+):
+    shard, context, tensor, core, chip, chips, sibling, others, partner, ranks, group = places()
+    own = pl.ds(pl.multiple_of(tensor * 256, 256), 256)
+    fetch = [
+        pltpu.make_async_copy(tok.at[own], tok_r, local_sem.at[0]),
+        pltpu.make_async_copy(cot.at[own], cot_r, local_sem.at[1]),
+        pltpu.make_async_copy(xn.at[own], xn_r, local_sem.at[2]),
+        pltpu.make_async_copy(w.at[:, pl.ds(1024, 256)], wbc, local_sem.at[3]),
+    ]
+    for copy in fetch:
+        copy.start()
+    greet([sibling, partner] + others[1:] + group[1:])
+    links = Links(send, recv)
+    sm[...] = small[...]
+    sm[20:24] = gate[...]
+    rows = [None] + [pl.ds(pl.multiple_of(t * 256, 256), 256) for t in ranks[1:]]
+    dbc_in = [links.copy(dbc.at[rows[k]], rbc.at[k - 1], group[k]) for k in range(1, 4)]
+    part_in = [links.copy(part.at[rows[k]], rp.at[k - 1], group[k]) for k in range(1, 4)]
+    sib_in = [
+        links.copy(sm, sm_s, sibling),
+        links.copy(gz.at[:, 1 - core], sz, sibling),
+        links.copy(gx.at[:, 1 - core], sx, sibling),
+        links.copy(go.at[:, 1 - core], so, sibling),
+        links.copy(gd.at[:, 1 - core], sd, sibling),
+    ]
+    branch_in = [links.copy(branch.at[rows[k]], rb.at[k - 1], group[k]) for k in range(1, 4)]
+    for copy in sib_in:
+        copy.wait_recv()
+    sm_c[chip] = sm[...] + sm_s[...]
+    small_in = [links.copy(sm_c.at[chip], sm_c.at[chip], others[k]) for k in range(1, 8)]
+    small_base = links.count - 8
+
+    def merge(c, carry):
+        for mine, theirs, at in ((gz, sz, 0), (gx, sx, 512), (go, so, 1024)):
+            chunk[c, :, at : at + 512] = (mine[c, core].astype(F32) + theirs[c].astype(F32)).astype(BF)
+        chunk[c, :, 1536:1664] = (gd[c, core].astype(F32) + sd[c].astype(F32)).astype(BF)
+        return carry
+
+    lax.fori_loop(0, 8, merge, 0)
+    grads_in = [links.copy(chunk.at[chips[k]], rg.at[k - 1], others[k]) for k in range(1, 8)]
+
+    for copy in fetch:
+        copy.wait()
+    for copy in dbc_in + part_in:
+        copy.wait_recv()
+    ones = jnp.full((64, 128), 1.0, BF)
+
+    def slice_rows(i):
+        r = pl.ds(pl.multiple_of(i * 64, 64), 64)
+        rt = pl.ds(pl.multiple_of(tensor * 256 + i * 64, 64), 64)
+        return r, rt
+
+    def inner(i, carry):
+        r, rt = slice_rows(i)
+        d_bc = dbc[rt].astype(F32) + rbc[0, r].astype(F32) + rbc[1, r].astype(F32) + rbc[2, r].astype(F32)
+        d_bc_low = d_bc.astype(BF)
+        total = part[rt].astype(F32) + rp[0, r].astype(F32) + rp[1, r].astype(F32) + rp[2, r].astype(F32)
+        total = total + mm_nt(d_bc_low, wbc[...])
+        plain = tok_r[r].astype(F32)
+        root = lax.rsqrt(jnp.mean(plain * plain, axis=1, keepdims=True) + EPSILON)
+        stat = plain * root
+        d_plain = total * gain[...]
+        mean = jnp.mean(d_plain * plain, axis=1, keepdims=True)
+        dtok_o[rt] = (cot_r[r].astype(F32) + root * d_plain - stat * (root * root) * mean).astype(BF)
+        g_bc, g_norm = carry
+        g_bc = g_bc + mm_tn(xn_r[r], d_bc_low)
+        g_norm = g_norm + mm_tn((total * stat).astype(BF), ones)
+        return g_bc, g_norm
+
+    g_bc, g_norm = lax.fori_loop(0, 4, inner, (jnp.zeros((1024, 256), F32), jnp.zeros((1024, 128), F32)))
+    g2[:, :, :, 0:256] = g_bc.astype(BF).reshape(8, 2, 64, 256)
+    g2[:, :, :, 256:384] = g_norm.astype(BF).reshape(8, 2, 64, 128)
+    sib2_in = links.copy(g2.at[:, 1 - core], s2, sibling)
+    mine_rows = dtok_o.at[own]
+    dtok_base = links.count
+    for k in range(1, 4):
+        links.copy(mine_rows, mine_rows, group[k])
+    sib2_in.wait_recv()
+    for c in range(8):
+        chunk2[c] = (g2[c, core].astype(F32) + s2[c].astype(F32)).astype(BF)
+    grads2_in = [links.copy(chunk2.at[chips[k]], rg2.at[k - 1], others[k]) for k in range(1, 8)]
+
+    for copy in branch_in:
+        copy.wait_recv()
+
+    def finish_out(i, carry):
+        r, rt = slice_rows(i)
+        total = branch[rt].astype(F32) + rb[0, r].astype(F32) + rb[1, r].astype(F32) + rb[2, r].astype(F32)
+        out_o[rt] = (tok_r[r].astype(F32) + total).astype(BF)
+        return carry
+
+    lax.fori_loop(0, 4, finish_out, 0)
+    out_rows = out_o.at[own]
+    out_base = links.count
+    for k in range(1, 4):
+        links.copy(out_rows, out_rows, group[k])
+
+    for k in range(1, 8):
+        source = lax.rem(chip + 8 - k, 8)
+        arrival(None, sm_c.at[source], recv.at[small_base + k], others[k]).wait_recv()
+    total = sm_c[0]
+    for c in range(1, 8):
+        total = total + sm_c[c]
+    sm_x[...] = total
+    small_ctx = links.copy(sm_x, sm_r, partner)
+    for copy in grads_in:
+        copy.wait_recv()
+    for at in range(0, 1664, 128):
+        lanes = slice(at, at + 128)
+        acc = chunk[chip, :, lanes].astype(F32)
+        for k in range(7):
+            acc = acc + rg[k, :, lanes].astype(F32)
+        cs[:, lanes] = acc.astype(BF)
+    grads_ctx = links.copy(cs, cr, partner)
+    for copy in grads2_in:
+        copy.wait_recv()
+    for at in range(0, 384, 128):
+        lanes = slice(at, at + 128)
+        acc = chunk2[chip, :, lanes].astype(F32)
+        for k in range(7):
+            acc = acc + rg2[k, :, lanes].astype(F32)
+        c2s[:, lanes] = acc
+    grads2_ctx = links.copy(c2s, c2r, partner)
+    small_ctx.wait_recv()
+    sums = sm_x[...] + sm_r[...]
+    small_o[0:32] = sums[0:32]
+    sm_t[tensor] = sums[32:48]
+    small_t = links.count
+    for k in range(1, 4):
+        links.copy(sm_t.at[tensor], sm_t.at[tensor], group[k])
+    grads2_ctx.wait_recv()
+    t2[tensor] = c2s[...] + c2r[...]
+    grads2_t = links.count
+    for k in range(1, 4):
+        links.copy(t2.at[tensor], t2.at[tensor], group[k])
+    grads_ctx.wait_recv()
+    oz[...] = cs[:, 0:512].astype(F32) + cr[:, 0:512].astype(F32)
+    ox[...] = cs[:, 512:1024].astype(F32) + cr[:, 512:1024].astype(F32)
+    oo[...] = cs[:, 1024:1536].astype(F32) + cr[:, 1024:1536].astype(F32)
+    odt[...] = cs[:, 1536:1664].astype(F32) + cr[:, 1536:1664].astype(F32)
+    for k in range(1, 4):
+        source = lax.rem(tensor + 4 - k, 4)
+        arrival(None, sm_t.at[source], recv.at[small_t + k - 1], group[k]).wait_recv()
+        arrival(None, t2.at[source], recv.at[grads2_t + k - 1], group[k]).wait_recv()
+    small_o[32:48] = (sm_t[0] + sm_t[1]) + (sm_t[2] + sm_t[3])
+    both = (t2[0] + t2[1]) + (t2[2] + t2[3])
+    obc[...] = both[:, 0:256]
+    onorm[...] = both[:, 256:384]
+    for k in range(1, 4):
+        source = pl.ds(pl.multiple_of(lax.rem(tensor + 4 - k, 4) * 256, 256), 256)
+        arrival(None, dtok_o.at[source], recv.at[dtok_base + k - 1], group[k]).wait_recv()
+        arrival(None, out_o.at[source], recv.at[out_base + k - 1], group[k]).wait_recv()
+    links.finish()
 
 
 def passed_along(value, axis, by):
@@ -356,14 +614,15 @@
     return sigma * (1.0 + value * (1.0 - sigma))
 
 
-def call(kernel, out_shapes, scratch, *args):
+def call(kernel, out_shapes, scratch, *args, specs=None, collective_id=None):
     return pl.pallas_call(
         kernel,
         out_shape=[jax.ShapeDtypeStruct(s, d) for s, d in out_shapes],
-        in_specs=[pl.BlockSpec(memory_space=pltpu.VMEM)] * len(args),
+        in_specs=[pl.BlockSpec(memory_space=pl.ANY if n in (specs or ()) else pltpu.VMEM) for n in range(len(args))],
         out_specs=[pl.BlockSpec(memory_space=pltpu.VMEM)] * len(out_shapes),
-        scratch_shapes=[pltpu.VMEM(s, d) for s, d in scratch],
-        compiler_params=pltpu.CompilerParams(vmem_limit_bytes=VMEM_LIMIT),
+        scratch_shapes=[pltpu.SemaphoreType.DMA(s) if d is None else pltpu.VMEM(s, d) for s, d in scratch],
+        compiler_params=pltpu.CompilerParams(vmem_limit_bytes=VMEM_LIMIT, collective_id=collective_id, has_side_effects=collective_id is not None
+        ),
     )(*args)
 
 
@@ -386,22 +645,21 @@
     w_out,
     cotangent,
 ):
-    gain_all, z_all, x_all, dt_all, bc_all, out_all = (
-        lax.all_gather(norm_gain, "shard", axis=0, tiled=True),
-        lax.all_gather(w_z, "shard", axis=0, tiled=True),
-        lax.all_gather(w_x, "shard", axis=0, tiled=True),
-        lax.all_gather(w_dt, "shard", axis=0, tiled=True),
-        lax.all_gather(w_bc, "shard", axis=0, tiled=True),
-        lax.all_gather(w_out, "shard", axis=0, tiled=True),
-    )
     length = tokens.shape[0]
     head_count = dt_bias.shape[0]
     inner_width = head_count * HEADDIM
     bc_width = 2 * STATE
-    pad_dt = jnp.pad(dt_all, ((0, 0), (0, 120)))
-    w_in = jnp.concatenate([z_all, x_all, bc_all, pad_dt], axis=1)
-    edge_tokens, edge_ids = passed_along((tokens[length - EDGE :], segment[length - EDGE :]), "context", 1)
     seg = segment
+    w_all, edge_tokens, edge_segs = call(
+        gather_kernel,
+        [((16, 64, 1920), BF), ((EDGE, 1024), BF), ((8, 128), jnp.int32)],
+        [((64, 1920), BF), ((EDGE, 1024), BF), ((24,), None), ((24,), None)],
+        w_z, w_x, w_bc, w_dt, norm_gain[:, None], w_out, tokens[length - EDGE :], seg.reshape(8, 128),
+        collective_id=1,
+    )
+    w_all = w_all.reshape(1024, 1920)
+    out_all = w_all[:, 1408:]
+    edge_ids = jnp.where(lax.axis_index("context") > 0, edge_segs[7, 112:], 0)
     ext_ids = jnp.concatenate([edge_ids[-3:], seg])
     start_seg = jnp.where(edge_ids[-1] == seg[0], seg[0], -1)
     blocks = seg.reshape(length // Q, Q)
@@ -420,16 +678,13 @@
     expand = jnp.asarray(expand_np, BF)
     expand_t = jnp.asarray(expand_np.T, BF)
     wide = (length, inner_width)
-    x_normed, z_gate, xbc, pre, dt_raw, y_zero, enter_decay, c_act, state_local = call(
+    x_normed, z_gate, xbc, pre, dt_raw, y_zero, enter_decay, c_act, state_local, gain_row = call(
         front_kernel,
         [((length, 1024), BF), (wide, F32), ((length + EDGE, 768), BF), ((length, 768), F32), ((length, 8), F32),
-         (wide, F32), ((length, 8), F32), ((length, STATE), BF), ((STATE, inner_width), F32)],
+         (wide, F32), ((length, 8), F32), ((length, STATE), BF), ((STATE, inner_width), F32), ((1, 1024), F32)],
         [((length + EDGE, 768), F32)],
-        tokens, edge_tokens, gain_all[None], w_in, colm, segr, conv_w, conv_b, dt_bias[None], a_log[None], d_skip[None], expand,
-    )
-    plain = tokens.astype(F32)
-    root_inv = lax.rsqrt(jnp.mean(plain * plain, axis=1, keepdims=True) + EPSILON)
-    gain_float = gain_all.astype(F32)
+        tokens, edge_tokens, w_all, colm, segr, conv_w, conv_b, dt_bias[None], a_log[None], d_skip[None], expand,
+    )
     state_in = passed_along(state_local, "context", 1)
     decay_e = jnp.repeat(enter_decay, HEADDIM, axis=1)
     y_mixed = y_zero + decay_e * jnp.dot(c_act, state_in.astype(BF), preferred_element_type=F32)
@@ -448,10 +703,10 @@
     d_z = (d_gated * y_mixed * silu_slope(z_gate)).astype(BF)
     d_carry = over_rows(c_act, (d_y * decay_e).astype(BF)).astype(BF)
     d_state_out = passed_along(d_carry, "context", -1).astype(F32)
-    d_x_first, d_bc_first, tail_rows, back_rows, d_dt_raw, g_conv_w, g_conv_b, g_heads = call(
+    d_x_first, d_bc_first, tail_rows, back_rows, d_dt_raw, small = call(
         back_kernel,
         [(wide, BF), ((length, bc_width), F32), ((EDGE, 768), F32), ((8, 768), F32), ((length, 8), F32),
-         ((CONV, 768), F32), ((1, 768), F32), ((8, 8), F32)],
+         ((48, 128), F32)],
         [((8, STATE, inner_width), F32), ((length, 768), F32), ((length + 16, 768), F32), ((STATE, inner_width), F32), ((8, 8), F32)],
         d_y, colm, segr, xbc, pre, dt_raw, state_in, d_state_out, conv_w, dt_bias[None], a_log[None], d_skip[None], expand, expand_t,
     )
@@ -459,50 +714,47 @@
     tail_rows = tail_rows + jnp.pad(returned, ((EDGE - 8, 0), (0, 0)))
     d_x_low = lax.dynamic_update_slice(d_x_first, tail_rows[:, :inner_width].astype(BF), (length - EDGE, 0))
     d_bc = lax.dynamic_update_slice(d_bc_first, tail_rows[:, inner_width:], (length - EDGE, 0))
-    d_dt_low = d_dt_raw.astype(BF)
-    part_in = (against(d_z, z_all) + against(d_x_low, x_all) + against(d_dt_low, dt_all)).astype(BF)
+    d_bc = d_bc.astype(BF)
+    d_dt_low = jnp.pad(d_dt_raw.astype(BF), ((0, 0), (0, 120)))
+    gates = jnp.concatenate([d_z, d_x_low], axis=1)
+    part_in = (against(gates, w_all[:, :1024]) + against(d_dt_low, w_all[:, 1280:1408])).astype(BF)
     g_w_z = over_rows(x_normed, d_z).astype(BF)
     g_w_x = over_rows(x_normed, d_x_low).astype(BF)
     g_w_dt = over_rows(x_normed, d_dt_low).astype(BF)
-    in_sum, bc_sum, branch, conv_bc_sum, conv_bcb_sum = lax.psum(
-        (part_in, d_bc.astype(BF), branch_part, g_conv_w[:, inner_width:], g_conv_b[:, inner_width:]), "tensor"
-    )
-    output = (plain + branch).astype(BF)
-    d_bc_low = bc_sum.astype(BF)
-    d_x_normed = in_sum + against(d_bc_low, bc_all)
-    stat_rows = plain * root_inv
-    g_norm_gain = jnp.sum(d_x_normed * stat_rows, axis=0)
-    d_plain = d_x_normed * gain_float[None, :]
-    d_tokens = (
-        cotangent.astype(F32)
-        + root_inv * d_plain
-        - plain * root_inv**3 * jnp.mean(d_plain * plain, axis=1, keepdims=True)
-    ).astype(BF)
-    g_w_bc = over_rows(x_normed, d_bc_low).astype(BF)
-    whole = jnp.concatenate([g_w_z, g_w_x, g_w_out, g_w_bc, g_w_dt], axis=1)
-    owned = lax.psum(lax.psum_scatter(whole, "shard", scatter_dimension=0, tiled=True), "context").astype(F32)
-    small, gn = lax.psum((jnp.concatenate([g_conv_w[:, :inner_width].reshape(-1), g_conv_b[0, :inner_width], conv_bc_sum.reshape(-1),
-        conv_bcb_sum[0], g_heads[0], g_heads[1], g_heads[2], g_gate_gain]), g_norm_gain), ("shard", "context"))
-    own_norm = lax.dynamic_slice(gn, (lax.axis_index("shard") * 64,), (64,))
-    cuts = np.cumsum([2048, 512, 1024, 256, 8, 8, 8])
-    pieces = jnp.split(small, cuts)
+    grid = (8, 2, 64)
+    output, d_tokens, o_z, o_x, o_out, o_dt, o_bc, o_norm, total = call(
+        tail_kernel,
+        [((length, 1024), BF), ((length, 1024), BF), ((64, 512), F32), ((64, 512), F32), ((64, 512), F32), ((64, 128), F32),
+         ((64, 256), F32), ((64, 128), F32), ((48, 128), F32)],
+        [((3, 256, 1024), BF), ((3, 256, 256), BF), ((3, 256, 1024), BF),
+         ((8, 64, 512), BF), ((8, 64, 512), BF), ((8, 64, 512), BF), ((8, 64, 128), BF), ((8, 64, 1664), BF), ((7, 64, 1664), BF),
+         ((64, 1664), BF), ((64, 1664), BF),
+         ((8, 2, 64, 384), BF), ((8, 64, 384), BF), ((8, 64, 384), BF), ((7, 64, 384), BF),
+         ((64, 384), F32), ((64, 384), F32), ((4, 64, 384), F32),
+         ((48, 128), F32), ((48, 128), F32), ((8, 48, 128), F32), ((48, 128), F32), ((48, 128), F32), ((4, 16, 128), F32),
+         ((256, 1024), BF), ((256, 1024), BF), ((256, 1024), BF), ((1024, 256), BF),
+         ((64,), None), ((64,), None), ((4,), None)],
+        part_in, branch_part, d_bc, g_w_z.reshape(grid + (512,)), g_w_x.reshape(grid + (512,)), g_w_out.reshape(grid + (512,)),
+        g_w_dt.reshape(grid + (128,)), small, g_gate_gain.reshape(4, 128), gain_row, tokens, cotangent, x_normed, w_all,
+        specs=(10, 11, 12, 13), collective_id=2,
+    )
     return (
         output,
         d_tokens,
-        own_norm,
-        owned[:, 0:512],
-        owned[:, 512:1024],
-        owned[:, 1792:1800],
-        owned[:, 1536:1792],
-        pieces[0].reshape(CONV, inner_width),
-        pieces[1],
-        pieces[2].reshape(CONV, bc_width),
-        pieces[3],
-        pieces[4],
-        pieces[5],
-        pieces[6],
-        pieces[7],
-        owned[:, 1024:1536],
+        o_norm[:, 0],
+        o_z,
+        o_x,
+        o_dt[:, 0:8],
+        o_bc,
+        total[0:16].reshape(CONV, inner_width),
+        total[16:20].reshape(inner_width),
+        total[32:40].reshape(CONV, bc_width),
+        total[40:42].reshape(bc_width),
+        total[24, 0:8],
+        total[25, 0:8],
+        total[26, 0:8],
+        total[20:24].reshape(inner_width),
+        o_out,
     )
 
 

time: 530 us -> 295 us (0.56)
  blocking collectives: 222 us -> 9.96 us
  Pallas kernels: 48.6 us -> 199 us
  waiting for transfers between devices: 137 us -> 2.03 us
  between operations: 17.2 us -> 2.93 us
  matrix products: 37 us -> 25.7 us
  other arithmetic: 18.5 us -> 10 us
    pallas_call x2 -> x4, Pallas kernels: 48.6 us -> 199 us  [call(): pl.pallas_call(kernel, out_shape=[jax.ShapeDtypeStruct(s, d) for s, d in...]
    psum x2 -> x0, blocking collectives: 132 us -> none  [the longest x1 126 us: local(): lax.psum((jnp.concatenate([g_conv_w[:, :inner_width].reshape(-1), g_conv_...]
    psum x2 -> x0, waiting for transfers between devices: 120 us -> none  [the longest x1 92.9 us: local(): lax.psum((part_in, d_bc.astype(BF), branch_part, g_conv_w[:, inner_width:...]
    all_gather x2 -> x0, blocking collectives: 46.8 us -> none  [the longest x1 25.1 us: local(): lax.all_gather(w_dt, 'shard', axis=0, tiled=True)]
    unnamed x1 -> x0, blocking collectives: 32.7 us -> none
    all_gather x3 -> x0, waiting for transfers between devices: 8.21 us -> none  [the longest x1 8.21 us: local(): lax.all_gather(w_out, 'shard', axis=0, tiled=True)]
    dot_general x5 -> x3, matrix products: 14.4 us -> 8.3 us  [against(): lax.dot_general(left, right, (((1,), (1,)), ((), ())), preferred_element_...]
    convert_element_type x4 -> x2, other arithmetic: 7.37 us -> 1.9 us  [the longest x1 1.07 us: local(): d_dt_low = jnp.pad(d_dt_raw.astype(BF), ((0, 0), (0, 120)))]
  transfers between devices with their start and end apart: 11 -> 3, of which waited for: 5 -> 2; matrix products, arithmetic and copies ran while one was open for 10% -> 5% of each run, Pallas kernels for 4% -> 0%
where the time goes in v2:
time: 295 us; the launch traced here: 290 us
  Pallas kernels  199 us (67%)
  local copies, waits for them, and re-layouts  35.7 us (12%)
  matrix products  25.7 us (9%)
  other arithmetic  10 us (3%)
  blocking collectives  9.96 us (3%)
  starting transfers between devices  5.17 us (2%)
    pallas_call x4, Pallas kernels, call(): pl.pallas_call(kernel, out_shape=[jax.ShapeDtypeStruct(s, d) for s, d in...  199 us
    unnamed x61, local copies, waits for them, and re-layouts  13.7 us
    dot_general x5, matrix products, over_rows(): lax.dot_general(left, right, (((0,), (0,)), ((), ())), preferred_element_...  10.2 us
    psum x1, blocking collectives, local(): lax.psum(jnp.stack([jnp.sum(gated * gated, axis=1), jnp.sum(d_scaled * ga...  9.96 us
    dot_general x3, matrix products, against(): lax.dot_general(left, right, (((1,), (1,)), ((), ())), preferred_element_...  8.3 us
  transfers between devices with their start and end apart: 3, of which 2 were waited for; matrix products, arithmetic and copies ran while one was open for 5% of the time, Pallas kernels for 0%

profile of v2, /device:TPU:1, one launch (start us, length us, event | category | flops | bytes accessed | tf_op | source)
XLA Modules:
  0.0 290.3 jit_solution(8657218186786681775)
XLA Ops:
  6.3 1.4 copy.57.wdt
  7.7 1.4 slice.87.etok
  9.1 41.2 %shard_map.306 = (bf16[16,64,1920]{2,1,0:T(8,128)(2,1)}, bf16[16,1024]{1,0:T(8,128)(2,1)}, s32[8,128]{1,0:T(8,128)}) custom-call(bf16[64,512]{1,0:T(8,128)(2,1)} %wz.1, bf16[64,512]{1,0:T(8,128)(2,1)} %wx.1, bf16[64,256]{1,0:T(8,128)(2,1)} %wbc.1, bf16[64,8]{1,0:T(8,128)(2,1)} %copy.57.wdt, bf16[64,1]{1,0:T(8,128)(2,1)} %copy.58.norm, bf16[64,512]{1,0:T(8,128)(2,1)} %wo.1, ...), custom_call_target="tpu_custom_call" | custom-call | tf_op jit(solution)/shard_map/pallas_call | solution.py:618
  58.3 19.2 %shard_map.307 = (bf16[1024,1024]{1,0:T(8,128)(2,1)}, f32[1024,512]{1,0:T(8,128)}, bf16[1040,768]{1,0:T(8,128)(2,1)}, f32[1024,768]{1,0:T(8,128)}, f32[1024,8]{1...) custom-call(bf16[1024,1024]{1,0:T(8,128)(2,1)} %tok.3, ...), custom_call_target="tpu_custom_call" | custom-call | tf_op jit(solution)/shard_map/pallas_call | solution.py:618
  77.5 2.3 collective-permute-start
  81.0 1.6 broadcast_in_dim.40
  82.6 2.0 copy.61
  85.7 2.2 multiply_add_fusion
  88.6 5.0 %multiply_reduce_fusion.1 = (f32[1024]{0:T(1024)S(1)}, f32[1024]{0:T(1024)S(1)}, f32[1024,512]{1,0:T(8,128)}, f32[512,1024]{0,1:T(8,128)}) fusion(f32[512]{0:T(512)S(1)} %copy-done.24, f32[1024,512]{1,0:T(8,128)S(1)} %multiply_add_fusion, f32[1024,512]{1,0:T(8,128)S(1)} %copy-done.8, bf16[1024,1024]{1,0:T(8,128)(2,1)S(1)} %copy-done.6, ...), kind=kOutput, calls=%fused_computation.15 | convolution fusion | flops 1078982656 | bytes 11544576 | tf_op jit(solution)/shard_map/dot_general | solution.py:693
  93.6 10.0 %psum.7 = f32[2,1024]{1,0:T(2,128)S(1)} all-reduce(f32[2,1024]{1,0:T(2,128)S(1)} %pad_maximum_fusion), channel_id=1, replica_groups=mesh['shard'=16,'context'=2,'tensor'=4] {'tensor'}, use_global_device_ids=true, to_apply=%region_2.3 | all-reduce | flops 2048 | bytes 16384 | tf_op jit(solution)/shard_map/psum | solution.py:695
  103.7 3.7 %fusion.8 = bf16[1024,512]{0,1:T(8,128)(2,1)S(1)} fusion(bf16[1024,1024]{1,0:T(8,128)(2,1)} %cot.1, f32[1024,512]{1,0:T(8,128)} %get-tuple-element.122, f32[1024]{0:T(1024)S(1)} %bitcast.91, f32[512]{0:T(512)S(1)} %copy-done.24), kind=kOutput, calls=%fused_computation.23 | convolution fusion | flops 1075838976 | bytes 5249024 | tf_op jit(solution)/shard_map/dot_general | solution.py:607
  107.8 3.6 %multiply_convert_fusion.2 = (bf16[1024,512]{1,0:T(8,128)(2,1)S(1)}, f32[1024,512]{1,0:T(8,128)S(1)}, f32[512]{0:T(512)}) fusion(f32[1024,512]{1,0:T(8,128)S(1)} %copy-done.9, f32[1024,512]{1,0:T(8,128)S(1)} %copy-done.5, f32[1024]{0:T(1024)S(1)} %bitcast.95, f32[1024,512]{1,0:T(8,128)S(1)} %copy-done.10, f32[512,1024]{0,1:T(8,128)} %get-tuple-element.141, ...), kind=kLoop, calls=%fused_computation.12 | loop fusion | flops 10485248 | bytes 11550720 | tf_op jit(solution)/shard_map/convert_element_type | solution.py:703
  112.7 1.6 collective-permute-start.1
  114.3 2.3 convolution_convert_fusion.3
  116.6 3.9 %convolution_convert_fusion.branch = bf16[1024,1024]{1,0:T(8,128)(2,1)} fusion(bf16[1024,1920]{1,0:T(8,128)(2,1)} %bitcast.78, f32[1024,512]{1,0:T(8,128)S(1)} %copy-done.10, f32[1024]{0:T(1024)S(1)} %bitcast.93, f32[512]{0:T(512)S(1)} %copy-done.24), kind=kOutput, calls=%fused_computation.19 | convolution fusion | flops 1076363264 | bytes 5249024 | tf_op jit(solution)/shard_map/dot_general | solution.py:601
  122.6 30.0 %shard_map.308 = (bf16[1024,512]{1,0:T(8,128)(2,1)}, f32[1024,256]{1,0:T(8,128)}, f32[16,768]{1,0:T(8,128)}, f32[8,768]{1,0:T(8,128)}, f32[1024,8]{1,0:T(8,128)}, /*index=5*/f32[48,128]{1,0:T(8,128)}) custom-call(f32[1024,512]{1,0:T(8,128)} %copy-done, f32[1032,8]{1,0:T(8,128)} %pad.12.colm, f32[8,128]{1,0:T(8,128)} %get-tuple-element.136.segr, ...), custom_call_target="tpu_custom_call" | custom-call | tf_op jit(solution)/shard_map/pallas_call | solution.py:618
  154.9 1.5 convolution_convert_fusion.4
  157.4 2.3 convolution_convert_fusion.2
  160.2 2.4 fusion
  163.4 2.0 add_convert_fusion.part
  165.4 108.5 %shard_map.309 = (bf16[1024,1024]{1,0:T(8,128)(2,1)}, bf16[1024,1024]{1,0:T(8,128)(2,1)}, f32[64,512]{1,0:T(8,128)}, f32[64,512]{1,0:T(8,128)}, f32[64,512]{1,0:...) custom-call(bf16[1024,1024]{1,0:T(8,128)(2,1)} %add_convert_fusion.part, ...), custom_call_target="tpu_custom_call" | custom-call | tf_op jit(solution)/shard_map/pallas_call | solution.py:618
  279.1 1.4 slice_reduce_fusion
  280.5 1.4 copy.66
  283.1 3.2 %copy.78 = bf16[1024,1024]{1,0:T(8,128)(2,1)} copy(bf16[1024,1024]{1,0:T(8,128)(2,1)} %get-tuple-element.158) | data formatting | bytes 4194304
  (98 shorter events, 33.6 us)
Async XLA Ops:
  0.6 57.0 %copy-start.23 = (f32[4,256]{1,0:T(4,128)S(1)}, f32[4,256]{1,0:T(4,128)}, u32[]{:S(2)}) copy-start(f32[4,256]{1,0:T(4,128)} %param.28) | copy-start | bytes 12292
  77.5 8.2 %collective-permute-start = (f32[128,512]{1,0:T(8,128)}, f32[128,512]{1,0:T(8,128)S(1)}, u32[]{:S(2)}, u32[]{:S(2)}) collective-permute-start(f32[128,512]{1,0:T(8,128)} %get-tuple-element.50), channel_id=1, source_target_pairs={{0,4},{1,5},{2,6},{3,7},{8,12},{9,13},{10,14},{11,15},{16,20},{17,... | collective-permute-start | bytes 786440 | tf_op jit(solution)/shard_map/ppermute | solution.py:597
  82.6 3.1 %copy-start.15 = (bf16[1024,128]{1,0:T(8,128)(2,1)S(1)}, bf16[1024,128]{1,0:T(8,128)(2,1)}, u32[]{:S(2)}) copy-start(bf16[1024,128]{1,0:T(8,128)(2,1)} %get-tuple-element.49) | copy-start | bytes 786436
  85.7 2.3 copy-start.6
  85.7 2.9 %copy-start.8 = (f32[1024,512]{1,0:T(8,128)S(1)}, f32[1024,512]{1,0:T(8,128)}, u32[]{:S(2)}) copy-start(f32[1024,512]{1,0:T(8,128)} %get-tuple-element.51) | copy-start | bytes 6291460
  85.7 2.9 %copy-start.24 = (f32[512]{0:T(512)S(1)}, f32[512]{0:T(512)}, u32[]{:S(2)}) copy-start(f32[512]{0:T(512)} %param.33) | copy-start | bytes 6148
  87.8 5.8 %copy-start.4 = (f32[1024,512]{1,0:T(8,128)}, f32[1024,512]{1,0:T(8,128)S(1)}, u32[]{:S(2)}) copy-start(f32[1024,512]{1,0:T(8,128)S(1)} %multiply_add_fusion) | copy-start | bytes 6291460
  103.6 3.8 %copy-start.5 = (f32[1024,512]{1,0:T(8,128)S(1)}, f32[1024,512]{1,0:T(8,128)}, u32[]{:S(2)}) copy-start(f32[1024,512]{1,0:T(8,128)} %copy-done.4) | copy-start | bytes 6291460
  103.6 3.8 %copy-start.9 = (f32[1024,512]{1,0:T(8,128)S(1)}, f32[1024,512]{1,0:T(8,128)}, u32[]{:S(2)}) copy-start(f32[1024,512]{1,0:T(8,128)} %get-tuple-element.51) | copy-start | bytes 6291460
  103.6 4.1 %copy-start.10 = (f32[1024,512]{1,0:T(8,128)S(1)}, f32[1024,512]{1,0:T(8,128)}, u32[]{:S(2)}) copy-start(f32[1024,512]{1,0:T(8,128)} %get-tuple-element.122) | copy-start | bytes 6291460
  107.8 3.6 %copy-start.16 = (bf16[1024,128]{1,0:T(8,128)(2,1)S(1)}, bf16[1024,128]{1,0:T(8,128)(2,1)}, u32[]{:S(2)}) copy-start(bf16[1024,128]{1,0:T(8,128)(2,1)} %get-tuple-element.49) | copy-start | bytes 786436
  111.3 2.9 %copy-start.12 = (bf16[1024,512]{1,0:T(8,128)(2,1)}, bf16[1024,512]{1,0:T(8,128)(2,1)S(1)}, u32[]{:S(2)}) copy-start(bf16[1024,512]{1,0:T(8,128)(2,1)S(1)} %get-tuple-element.123) | copy-start | bytes 3145732
  111.3 2.9 %copy-start.2 = (bf16[1024,1024]{1,0:T(8,128)(2,1)S(1)}, bf16[1024,1024]{1,0:T(8,128)(2,1)}, u32[]{:S(2)}) copy-start(bf16[1024,1024]{1,0:T(8,128)(2,1)} %get-tuple-element.60.xn) | copy-start | bytes 6291460
  112.7 9.2 %collective-permute-start.1 = (bf16[128,512]{1,0:T(8,128)(2,1)S(1)}, bf16[128,512]{1,0:T(8,128)(2,1)S(1)}, u32[]{:S(2)}, u32[]{:S(2)}) collective-permute-start(bf16[128,512]{1,0:T(8,128)(2,1)S(1)} %convolution_convert_fusion.5), channel_id=1, source_target_pairs={{4,0},{5,1},{6,2},{7,3},{12,8},{13,9},{14,10},{15,11},{20,16},{21,... | collective-permute-start | bytes 393224 | tf_op jit(solution)/shard_map/ppermute | solution.py:597
  122.6 32.3 %copy-start.3 = (bf16[1024,1024]{1,0:T(8,128)(2,1)S(1)}, bf16[1024,1024]{1,0:T(8,128)(2,1)}, u32[]{:S(2)}) copy-start(bf16[1024,1024]{1,0:T(8,128)(2,1)} %get-tuple-element.60.xn) | copy-start | bytes 6291460
  152.5 4.8 %collective-permute-start.2 = (f32[8,768]{1,0:T(8,128)}, f32[8,768]{1,0:T(8,128)S(1)}, u32[]{:S(2)}, u32[]{:S(2)}) collective-permute-start(f32[8,768]{1,0:T(8,128)} %get-tuple-element.57), channel_id=1, source_target_pairs={{4,0},{5,1},{6,2},{7,3},{12,8},{13,9},{14,10},{15,11},{20,16},{21,... | collective-permute-start | bytes 73736 | tf_op jit(solution)/shard_map/ppermute | solution.py:597
  154.9 2.4 copy-start.22
  154.9 2.4 copy-start.25
  157.4 2.3 copy-start.1
  157.4 2.8 copy-start.13
  160.2 2.4 copy-start.11
  283.1 3.2 %copy-start.7 = (bf16[1024,1024]{1,0:T(8,128)(2,1)S(1)}, bf16[1024,1024]{1,0:T(8,128)(2,1)}, u32[]{:S(2)}) copy-start(bf16[1024,1024]{1,0:T(8,128)(2,1)} %get-tuple-element.159) | copy-start | bytes 6291460
  286.4 2.7 copy-start.21
  286.4 3.3 %copy-start.17 = (f32[64,512]{1,0:T(8,128)S(1)}, f32[64,512]{1,0:T(8,128)}, u32[]{:S(2)}) copy-start(f32[64,512]{1,0:T(8,128)} %get-tuple-element.173) | copy-start | bytes 393220
  (5 other events, 7.4 us)

commit v3 on v2

--- a/solution.py
+++ b/solution.py
@@ -157,10 +157,19 @@
 
 
 def back_kernel(
-    dy, colm, segr, xbc, pre_r, dtr, st_in, g_in, cw, dtb, alog, dsk, ex, ext,
-    dx_o, dbc_o, tail_o, ret_o, ddt_o, small_o,
-    states, acts, dpre, grad, heads,
+    dy, colm, segr, xbc, pre_r, dtr, st_in, g_send, cw, dtb, alog, dsk, ex, ext, branch, tok,
+    dx_o, dbc_o, ddt_o, small_o, out_o,
+    states, acts, dpre, grad, heads, g_in, tail_r, ret_s, ret_r, near, relay, from_d, from_u, tok_r, send, recv, local_sem,
 ):
+    shard, context, tensor, core, chip, chips, sibling, others, partner, ranks, group = places()
+    own = pl.ds(pl.multiple_of(tensor * 256, 256), 256)
+    fetch = pltpu.make_async_copy(tok.at[own], tok_r, local_sem.at[0])
+    fetch.start()
+    greet([partner, group[1], group[3]])
+    links = Links(send, recv)
+    carry_in = links.copy(g_send, g_in, partner)
+    ring = Ring(links, tensor, group)
+    ring.reduce_first(branch, near, from_d, from_u)
     a_neg = -jnp.exp(alog[...])
     causal, anti = triangles()
     lower = as_low(causal)
@@ -203,7 +212,8 @@
         lanes = slice(c * 128, c * 128 + 128)
         pre = pre_r[r7, lanes]
         acts[r7, lanes] = pre * sigmoid(pre)
-    grad[...] = g_in[...]
+    carry_in.wait_recv()
+    grad[...] = jnp.where(context == 0, g_in[...].astype(F32), 0.0)
     heads[...] = jnp.zeros_like(heads)
     dpre[0:8] = jnp.zeros((8, 768), F32)
     dpre[1032:1040] = jnp.zeros((8, 768), F32)
@@ -291,7 +301,22 @@
         heads[2:3] += head_sum(jnp.concatenate(k_terms, axis=1))
         return carry
 
-    lax.fori_loop(0, 8, backward, 0)
+    lax.fori_loop(0, 1, backward, 0)
+    ring.reduce_second(branch, near, relay, from_d, from_u)
+    lax.fori_loop(1, 4, backward, 0)
+    fetch.wait()
+    ring.reduce_wait()
+
+    def finish_out(i, carry):
+        r = pl.ds(pl.multiple_of(i * 64, 64), 64)
+        rt = pl.ds(pl.multiple_of(tensor * 256 + i * 64, 64), 64)
+        total = branch[rt].astype(F32) + from_d[r].astype(F32) + from_u[r].astype(F32)
+        out_o[rt] = (tok_r[r].astype(F32) + total).astype(BF)
+        return carry
+
+    lax.fori_loop(0, 4, finish_out, 0)
+    ring.gather_first(out_o)
+    lax.fori_loop(4, 8, backward, 0)
     small_o[...] = jnp.zeros_like(small_o)
     small_o[24:32, 0:8] = heads[...]
 
@@ -302,7 +327,11 @@
         total = jnp.zeros((8, 128), F32)
         for d in range(1, 4):
             total = total + cw[3 - d : 4 - d, lanes] * (first * flags[:, d : d + 1])[d : d + 8]
-        ret_o[:, lanes] = total
+        ret_s[:, lanes] = total
+    ret_in = links.copy(ret_s, ret_r, partner)
+    ring.gather_second(out_o)
+    for c in range(6):
+        lanes = slice(c * 128, c * 128 + 128)
 
         def conv(b, sums, lanes=lanes, c=c):
             r = pl.ds(pl.multiple_of(b * Q, Q), Q)
@@ -320,11 +349,11 @@
             if c < 4:
                 dx_o[r, lanes] = out.astype(BF)
             else:
-                dbc_o[r, slice(c * 128 - 512, c * 128 - 384)] = out
+                dbc_o[r, slice(c * 128 - 512, c * 128 - 384)] = out.astype(BF)
 
             @pl.when(b == 7)
             def _():
-                tail_o[:, lanes] = out[Q - EDGE :]
+                tail_r[:, lanes] = out[Q - EDGE :]
 
             return tuple(new)
 
@@ -335,6 +364,13 @@
         for d in range(4):
             at = (3 - d) * 4 + c if c < 4 else 28 + (3 - d) * 2 + c
             small_o[at : at + 1] = sums[d + 1]
+    ret_in.wait_recv()
+    returned = jnp.where(context == 0, ret_r[...], 0.0)
+    last = tail_r[...] + jnp.concatenate([jnp.zeros((EDGE - 8, 768), F32), returned], axis=0)
+    dx_o[1024 - EDGE : 1024] = last[:, 0:512].astype(BF)
+    dbc_o[1024 - EDGE : 1024] = last[:, 512:768].astype(BF)
+    ring.gather_wait(out_o)
+    links.finish()
 
 
 MESH = pl.DeviceIdType.MESH
@@ -394,6 +430,67 @@
     ranks = [None] + [lax.rem(tensor + k, 4) for k in range(1, 4)]
     group = [None] + [at(tensor_to=t) for t in ranks[1:]]
     return shard, context, tensor, core, chip, chips, sibling, others, partner, ranks, group
+
+
+class Ring:
+    def __init__(self, links, tensor, group):
+        self.links, self.tensor = links, tensor
+        self.up, self.down = group[1], group[3]
+        self.t_up, self.t_down, self.t_far = (lax.rem(tensor + k, 4) for k in (1, 3, 2))
+
+    def half(self, rank, which):
+        return pl.ds(pl.multiple_of(rank * 256 + which * 128, 128), 128)
+
+    def whole(self, rank):
+        return pl.ds(pl.multiple_of(rank * 256, 256), 256)
+
+    def reduce_first(self, src, near, from_down, from_up):
+        copy = self.links.copy
+        self.first = (
+            copy(src.at[self.half(self.t_far, 0)], near.at[0], self.up),
+            copy(src.at[self.half(self.t_far, 1)], near.at[1], self.down),
+        )
+        self.alone = (
+            copy(src.at[self.half(self.t_up, 1)], from_down.at[pl.ds(128, 128)], self.up),
+            copy(src.at[self.half(self.t_down, 0)], from_up.at[pl.ds(0, 128)], self.down),
+        )
+
+    def reduce_second(self, src, near, relay, from_down, from_up):
+        copy = self.links.copy
+        self.first[0].wait_recv()
+        relay[0] = (near[0].astype(F32) + src[self.half(self.t_up, 0)].astype(F32)).astype(BF)
+        up = copy(relay.at[0], from_down.at[pl.ds(0, 128)], self.up)
+        self.first[1].wait_recv()
+        relay[1] = (near[1].astype(F32) + src[self.half(self.t_down, 1)].astype(F32)).astype(BF)
+        down = copy(relay.at[1], from_up.at[pl.ds(128, 128)], self.down)
+        self.summed = (up, down)
+
+    def reduce_wait(self):
+        for made in self.alone + self.summed:
+            made.wait_recv()
+
+    def gather_first(self, ref):
+        mine = ref.at[self.whole(self.tensor)]
+        self.base = self.links.count
+        self.links.copy(mine, mine, self.up)
+        self.links.copy(mine, mine, self.down)
+
+    def landed(self, slot, which, device):
+        arrival(None, slot, self.links.recv.at[self.base + which], device).wait_recv()
+
+    def gather_second(self, ref):
+        self.landed(ref.at[self.whole(self.t_down)], 0, self.down)
+        self.base2 = self.links.count
+        up = ref.at[self.half(self.t_down, 0)]
+        self.links.copy(up, up, self.up)
+        self.landed(ref.at[self.whole(self.t_up)], 1, self.up)
+        down = ref.at[self.half(self.t_up, 1)]
+        self.links.copy(down, down, self.down)
+
+    def gather_wait(self, ref):
+        offset = self.base2 - self.base
+        self.landed(ref.at[self.half(self.t_far, 0)], offset, self.down)
+        self.landed(ref.at[self.half(self.t_far, 1)], offset + 1, self.up)
 
 
 def gather_kernel(wz, wx, wbc, wdt, norm, wo, etok, eseg, all_o, etok_o, eseg_o, mine, etok_b, send, recv):
@@ -430,9 +527,9 @@
 
 
 def tail_kernel(
-    part, branch, dbc, gz, gx, go, gd, small, gate, gain, tok, cot, xn, w,
-    out_o, dtok_o, oz, ox, oo, odt, obc, onorm, small_o,
-    rp, rbc, rb, sz, sx, so, sd, chunk, rg, cs, cr,
+    part, dbc, gz, gx, go, gd, small, gate, gain, tok, cot, xn, w,
+    dtok_o, oz, ox, oo, odt, obc, onorm, conv_o, convb_o, bc_o, bcb_o, gate_o, heads_o,
+    near, relay, from_d, from_u, near2, relay2, from_d2, from_u2, sz, sx, so, sd, chunk, rg, cs, cr,
     g2, s2, chunk2, rg2, c2s, c2r, t2,
     sm, sm_s, sm_c, sm_x, sm_r, sm_t,
     tok_r, cot_r, xn_r, wbc, send, recv, local_sem,
@@ -451,9 +548,9 @@
     links = Links(send, recv)
     sm[...] = small[...]
     sm[20:24] = gate[...]
-    rows = [None] + [pl.ds(pl.multiple_of(t * 256, 256), 256) for t in ranks[1:]]
-    dbc_in = [links.copy(dbc.at[rows[k]], rbc.at[k - 1], group[k]) for k in range(1, 4)]
-    part_in = [links.copy(part.at[rows[k]], rp.at[k - 1], group[k]) for k in range(1, 4)]
+    wide, thin = Ring(links, tensor, group), Ring(links, tensor, group)
+    thin.reduce_first(dbc, near2, from_d2, from_u2)
+    wide.reduce_first(part, near, from_d, from_u)
     sib_in = [
         links.copy(sm, sm_s, sibling),
         links.copy(gz.at[:, 1 - core], sz, sibling),
@@ -461,7 +558,7 @@
         links.copy(go.at[:, 1 - core], so, sibling),
         links.copy(gd.at[:, 1 - core], sd, sibling),
     ]
-    branch_in = [links.copy(branch.at[rows[k]], rb.at[k - 1], group[k]) for k in range(1, 4)]
+    thin.reduce_second(dbc, near2, relay2, from_d2, from_u2)
     for copy in sib_in:
         copy.wait_recv()
     sm_c[chip] = sm[...] + sm_s[...]
@@ -475,12 +572,13 @@
         return carry
 
     lax.fori_loop(0, 8, merge, 0)
+    wide.reduce_second(part, near, relay, from_d, from_u)
     grads_in = [links.copy(chunk.at[chips[k]], rg.at[k - 1], others[k]) for k in range(1, 8)]
 
     for copy in fetch:
         copy.wait()
-    for copy in dbc_in + part_in:
-        copy.wait_recv()
+    thin.reduce_wait()
+    wide.reduce_wait()
     ones = jnp.full((64, 128), 1.0, BF)
 
     def slice_rows(i):
@@ -490,9 +588,9 @@
 
     def inner(i, carry):
         r, rt = slice_rows(i)
-        d_bc = dbc[rt].astype(F32) + rbc[0, r].astype(F32) + rbc[1, r].astype(F32) + rbc[2, r].astype(F32)
+        d_bc = dbc[rt].astype(F32) + from_d2[r].astype(F32) + from_u2[r].astype(F32)
         d_bc_low = d_bc.astype(BF)
-        total = part[rt].astype(F32) + rp[0, r].astype(F32) + rp[1, r].astype(F32) + rp[2, r].astype(F32)
+        total = part[rt].astype(F32) + from_d[r].astype(F32) + from_u[r].astype(F32)
         total = total + mm_nt(d_bc_low, wbc[...])
         plain = tok_r[r].astype(F32)
         root = lax.rsqrt(jnp.mean(plain * plain, axis=1, keepdims=True) + EPSILON)
@@ -509,29 +607,11 @@
     g2[:, :, :, 0:256] = g_bc.astype(BF).reshape(8, 2, 64, 256)
     g2[:, :, :, 256:384] = g_norm.astype(BF).reshape(8, 2, 64, 128)
     sib2_in = links.copy(g2.at[:, 1 - core], s2, sibling)
-    mine_rows = dtok_o.at[own]
-    dtok_base = links.count
-    for k in range(1, 4):
-        links.copy(mine_rows, mine_rows, group[k])
+    wide.gather_first(dtok_o)
     sib2_in.wait_recv()
     for c in range(8):
         chunk2[c] = (g2[c, core].astype(F32) + s2[c].astype(F32)).astype(BF)
     grads2_in = [links.copy(chunk2.at[chips[k]], rg2.at[k - 1], others[k]) for k in range(1, 8)]
-
-    for copy in branch_in:
-        copy.wait_recv()
-
-    def finish_out(i, carry):
-        r, rt = slice_rows(i)
-        total = branch[rt].astype(F32) + rb[0, r].astype(F32) + rb[1, r].astype(F32) + rb[2, r].astype(F32)
-        out_o[rt] = (tok_r[r].astype(F32) + total).astype(BF)
-        return carry
-
-    lax.fori_loop(0, 4, finish_out, 0)
-    out_rows = out_o.at[own]
-    out_base = links.count
-    for k in range(1, 4):
-        links.copy(out_rows, out_rows, group[k])
 
     for k in range(1, 8):
         source = lax.rem(chip + 8 - k, 8)
@@ -550,6 +630,7 @@
             acc = acc + rg[k, :, lanes].astype(F32)
         cs[:, lanes] = acc.astype(BF)
     grads_ctx = links.copy(cs, cr, partner)
+    wide.gather_second(dtok_o)
     for copy in grads2_in:
         copy.wait_recv()
     for at in range(0, 384, 128):
@@ -561,7 +642,13 @@
     grads2_ctx = links.copy(c2s, c2r, partner)
     small_ctx.wait_recv()
     sums = sm_x[...] + sm_r[...]
-    small_o[0:32] = sums[0:32]
+    for k in range(4):
+        for p in range(4):
+            conv_o[k : k + 1, p * 128 : p * 128 + 128] = sums[k * 4 + p : k * 4 + p + 1]
+    for p in range(4):
+        convb_o[:, p * 128 : p * 128 + 128] = sums[16 + p : 17 + p]
+        gate_o[:, p * 128 : p * 128 + 128] = sums[20 + p : 21 + p]
+    heads_o[...] = sums[24:32]
     sm_t[tensor] = sums[32:48]
     small_t = links.count
     for k in range(1, 4):
@@ -580,14 +667,16 @@
         source = lax.rem(tensor + 4 - k, 4)
         arrival(None, sm_t.at[source], recv.at[small_t + k - 1], group[k]).wait_recv()
         arrival(None, t2.at[source], recv.at[grads2_t + k - 1], group[k]).wait_recv()
-    small_o[32:48] = (sm_t[0] + sm_t[1]) + (sm_t[2] + sm_t[3])
+    sums = (sm_t[0] + sm_t[1]) + (sm_t[2] + sm_t[3])
+    for k in range(4):
+        for p in range(2):
+            bc_o[k : k + 1, p * 128 : p * 128 + 128] = sums[k * 2 + p : k * 2 + p + 1]
+    for p in range(2):
+        bcb_o[:, p * 128 : p * 128 + 128] = sums[8 + p : 9 + p]
     both = (t2[0] + t2[1]) + (t2[2] + t2[3])
     obc[...] = both[:, 0:256]
     onorm[...] = both[:, 256:384]
-    for k in range(1, 4):
-        source = pl.ds(pl.multiple_of(lax.rem(tensor + 4 - k, 4) * 256, 256), 256)
-        arrival(None, dtok_o.at[source], recv.at[dtok_base + k - 1], group[k]).wait_recv()
-        arrival(None, out_o.at[source], recv.at[out_base + k - 1], group[k]).wait_recv()
+    wide.gather_wait(dtok_o)
     links.finish()
 
 
@@ -702,19 +791,17 @@
     d_y = d_gated * gate_act
     d_z = (d_gated * y_mixed * silu_slope(z_gate)).astype(BF)
     d_carry = over_rows(c_act, (d_y * decay_e).astype(BF)).astype(BF)
-    d_state_out = passed_along(d_carry, "context", -1).astype(F32)
-    d_x_first, d_bc_first, tail_rows, back_rows, d_dt_raw, small = call(
+    d_x_low, d_bc, d_dt_raw, small, output = call(
         back_kernel,
-        [(wide, BF), ((length, bc_width), F32), ((EDGE, 768), F32), ((8, 768), F32), ((length, 8), F32),
-         ((48, 128), F32)],
-        [((8, STATE, inner_width), F32), ((length, 768), F32), ((length + 16, 768), F32), ((STATE, inner_width), F32), ((8, 8), F32)],
-        d_y, colm, segr, xbc, pre, dt_raw, state_in, d_state_out, conv_w, dt_bias[None], a_log[None], d_skip[None], expand, expand_t,
-    )
-    returned = passed_along(back_rows, "context", -1)
-    tail_rows = tail_rows + jnp.pad(returned, ((EDGE - 8, 0), (0, 0)))
-    d_x_low = lax.dynamic_update_slice(d_x_first, tail_rows[:, :inner_width].astype(BF), (length - EDGE, 0))
-    d_bc = lax.dynamic_update_slice(d_bc_first, tail_rows[:, inner_width:], (length - EDGE, 0))
-    d_bc = d_bc.astype(BF)
+        [(wide, BF), ((length, bc_width), BF), ((length, 8), F32), ((48, 128), F32), ((length, 1024), BF)],
+        [((8, STATE, inner_width), F32), ((length, 768), F32), ((length + 16, 768), F32), ((STATE, inner_width), F32), ((8, 8), F32),
+         ((STATE, inner_width), BF), ((EDGE, 768), F32), ((8, 768), F32), ((8, 768), F32),
+         ((2, 128, 1024), BF), ((2, 128, 1024), BF), ((256, 1024), BF), ((256, 1024), BF), ((256, 1024), BF),
+         ((16,), None), ((16,), None), ((1,), None)],
+        d_y, colm, segr, xbc, pre, dt_raw, state_in, d_carry, conv_w, dt_bias[None], a_log[None], d_skip[None], expand, expand_t,
+        branch_part, tokens,
+        specs=(15,), collective_id=3,
+    )
     d_dt_low = jnp.pad(d_dt_raw.astype(BF), ((0, 0), (0, 120)))
     gates = jnp.concatenate([d_z, d_x_low], axis=1)
     part_in = (against(gates, w_all[:, :1024]) + against(d_dt_low, w_all[:, 1280:1408])).astype(BF)
@@ -722,11 +809,12 @@
     g_w_x = over_rows(x_normed, d_x_low).astype(BF)
     g_w_dt = over_rows(x_normed, d_dt_low).astype(BF)
     grid = (8, 2, 64)
-    output, d_tokens, o_z, o_x, o_out, o_dt, o_bc, o_norm, total = call(
+    d_tokens, o_z, o_x, o_out, o_dt, o_bc, o_norm, conv_o, convb_o, cbc_o, cbcb_o, gate_o, heads_o = call(
         tail_kernel,
-        [((length, 1024), BF), ((length, 1024), BF), ((64, 512), F32), ((64, 512), F32), ((64, 512), F32), ((64, 128), F32),
-         ((64, 256), F32), ((64, 128), F32), ((48, 128), F32)],
-        [((3, 256, 1024), BF), ((3, 256, 256), BF), ((3, 256, 1024), BF),
+        [((length, 1024), BF), ((64, 512), F32), ((64, 512), F32), ((64, 512), F32), ((64, 128), F32),
+         ((64, 256), F32), ((64, 128), F32), ((4, 512), F32), ((1, 512), F32), ((4, 256), F32), ((1, 256), F32), ((1, 512), F32), ((8, 128), F32)],
+        [((2, 128, 1024), BF), ((2, 128, 1024), BF), ((256, 1024), BF), ((256, 1024), BF),
+         ((2, 128, 256), BF), ((2, 128, 256), BF), ((256, 256), BF), ((256, 256), BF),
          ((8, 64, 512), BF), ((8, 64, 512), BF), ((8, 64, 512), BF), ((8, 64, 128), BF), ((8, 64, 1664), BF), ((7, 64, 1664), BF),
          ((64, 1664), BF), ((64, 1664), BF),
          ((8, 2, 64, 384), BF), ((8, 64, 384), BF), ((8, 64, 384), BF), ((7, 64, 384), BF),
@@ -734,9 +822,9 @@
          ((48, 128), F32), ((48, 128), F32), ((8, 48, 128), F32), ((48, 128), F32), ((48, 128), F32), ((4, 16, 128), F32),
          ((256, 1024), BF), ((256, 1024), BF), ((256, 1024), BF), ((1024, 256), BF),
          ((64,), None), ((64,), None), ((4,), None)],
-        part_in, branch_part, d_bc, g_w_z.reshape(grid + (512,)), g_w_x.reshape(grid + (512,)), g_w_out.reshape(grid + (512,)),
+        part_in, d_bc, g_w_z.reshape(grid + (512,)), g_w_x.reshape(grid + (512,)), g_w_out.reshape(grid + (512,)),
         g_w_dt.reshape(grid + (128,)), small, g_gate_gain.reshape(4, 128), gain_row, tokens, cotangent, x_normed, w_all,
-        specs=(10, 11, 12, 13), collective_id=2,
+        specs=(9, 10, 11, 12), collective_id=2,
     )
     return (
         output,
@@ -746,14 +834,14 @@
         o_x,
         o_dt[:, 0:8],
         o_bc,
-        total[0:16].reshape(CONV, inner_width),
-        total[16:20].reshape(inner_width),
-        total[32:40].reshape(CONV, bc_width),
-        total[40:42].reshape(bc_width),
-        total[24, 0:8],
-        total[25, 0:8],
-        total[26, 0:8],
-        total[20:24].reshape(inner_width),
+        conv_o,
+        convb_o[0],
+        cbc_o,
+        cbcb_o[0],
+        heads_o[0, 0:8],
+        heads_o[1, 0:8],
+        heads_o[2, 0:8],
+        gate_o[0],
         o_out,
     )
 

time: 295 us -> 252 us (0.85)
  Pallas kernels: 199 us -> 161 us
  matrix products: 25.7 us -> 32.8 us
  local copies, waits for them, and re-layouts: 35.7 us -> 31 us
    pallas_call x4, Pallas kernels: 199 us -> 161 us  [call(): pl.pallas_call(kernel, out_shape=[jax.ShapeDtypeStruct(s, d) for s, d in...]
    dot_general x3, matrix products: 8.3 us -> 13 us  [against(): lax.dot_general(left, right, (((1,), (1,)), ((), ())), preferred_element_...]
    reshape x4 -> x0, local copies, waits for them, and re-layouts: 3.75 us -> none  [the longest x1 1.32 us: local(): total[20:24].reshape(inner_width)]
    unnamed x61 -> x72, local copies, waits for them, and re-layouts: 13.7 us -> 14.2 us
  transfers between devices with their start and end apart: 3 -> 1, of which waited for: 2 -> 1; matrix products, arithmetic and copies ran while one was open for 5% -> 2% of each run, Pallas kernels for 0% -> 0%
where the time goes in v3:
time: 252 us; the launch traced here: 248 us
  Pallas kernels  161 us (64%)
  matrix products  32.8 us (13%)
  local copies, waits for them, and re-layouts  31 us (12%)
  blocking collectives  9.85 us (4%)
  other arithmetic  7.39 us (3%)
  between operations  2.88 us (1%)
    pallas_call x4, Pallas kernels, call(): pl.pallas_call(kernel, out_shape=[jax.ShapeDtypeStruct(s, d) for s, d in...  161 us
    unnamed x72, local copies, waits for them, and re-layouts  14.2 us
    dot_general x3, matrix products, against(): lax.dot_general(left, right, (((1,), (1,)), ((), ())), preferred_element_...  13 us
    dot_general x5, matrix products, over_rows(): lax.dot_general(left, right, (((0,), (0,)), ((), ())), preferred_element_...  12.6 us
    psum x1, blocking collectives, local(): lax.psum(jnp.stack([jnp.sum(gated * gated, axis=1), jnp.sum(d_scaled * ga...  9.85 us
  transfers between devices with their start and end apart: 1, of which 1 were waited for; matrix products, arithmetic and copies ran while one was open for 2% of the time, Pallas kernels for 0%

profile of v3, /device:TPU:1, one launch (start us, length us, event | category | flops | bytes accessed | tf_op | source)
XLA Modules:
  0.0 248.2 jit_solution(8317436946730857384)
XLA Ops:
  3.6 1.4 bitcast_convert_fusion
  6.3 1.4 copy.57.wdt
  7.7 1.4 slice.65.etok
  9.1 41.2 %shard_map.306 = (bf16[16,64,1920]{2,1,0:T(8,128)(2,1)}, bf16[16,1024]{1,0:T(8,128)(2,1)}, s32[8,128]{1,0:T(8,128)}) custom-call(bf16[64,512]{1,0:T(8,128)(2,1)} %wz.1, bf16[64,512]{1,0:T(8,128)(2,1)} %wx.1, bf16[64,256]{1,0:T(8,128)(2,1)} %wbc.1, bf16[64,8]{1,0:T(8,128)(2,1)} %copy.57.wdt, bf16[64,1]{1,0:T(8,128)(2,1)} %copy.58.norm, bf16[64,512]{1,0:T(8,128)(2,1)} %wo.1, ...), custom_call_target="tpu_custom_call" | custom-call | tf_op jit(solution)/shard_map/pallas_call | solution.py:707
  58.3 19.2 %shard_map.307 = (bf16[1024,1024]{1,0:T(8,128)(2,1)}, f32[1024,512]{1,0:T(8,128)}, bf16[1040,768]{1,0:T(8,128)(2,1)}, f32[1024,768]{1,0:T(8,128)}, f32[1024,8]{1...) custom-call(bf16[1024,1024]{1,0:T(8,128)(2,1)} %tok.5, ...), custom_call_target="tpu_custom_call" | custom-call | tf_op jit(solution)/shard_map/pallas_call | solution.py:707
  77.5 2.3 collective-permute-start
  81.1 1.6 broadcast_in_dim.40
  82.6 2.0 copy.61
  85.8 2.2 multiply_add_fusion
  88.8 5.0 %multiply_reduce_fusion.1 = (f32[1024]{0:T(1024)S(1)}, f32[1024]{0:T(1024)S(1)}, f32[1024,512]{1,0:T(8,128)}, f32[512,1024]{0,1:T(8,128)}) fusion(f32[512]{0:T(512)S(1)} %copy-done.27, f32[1024,512]{1,0:T(8,128)S(1)} %multiply_add_fusion, f32[1024,512]{1,0:T(8,128)S(1)} %copy-done.8, bf16[1024,1024]{1,0:T(8,128)(2,1)S(1)} %copy-done.12, ...), kind=kOutput, calls=%fused_computation.15 | convolution fusion | flops 1078982656 | bytes 11544576 | tf_op jit(solution)/shard_map/dot_general | solution.py:782
  93.8 9.9 %psum.7 = f32[2,1024]{1,0:T(2,128)S(1)} all-reduce(f32[2,1024]{1,0:T(2,128)S(1)} %pad_maximum_fusion), channel_id=1, replica_groups=mesh['shard'=16,'context'=2,'tensor'=4] {'tensor'}, use_global_device_ids=true, to_apply=%region_2.3 | all-reduce | flops 2048 | bytes 16384 | tf_op jit(solution)/shard_map/psum | solution.py:784
  103.7 3.7 %fusion.12 = bf16[1024,512]{0,1:T(8,128)(2,1)S(1)} fusion(bf16[1024,1024]{1,0:T(8,128)(2,1)} %cot.1, f32[1024,512]{1,0:T(8,128)} %get-tuple-element.128, f32[1024]{0:T(1024)S(1)} %bitcast.88, f32[512]{0:T(512)S(1)} %copy-done.27), kind=kOutput, calls=%fused_computation.23 | convolution fusion | flops 1075838976 | bytes 5249024 | tf_op jit(solution)/shard_map/dot_general | solution.py:696
  107.4 4.0 %convolution_convert_fusion.branch = bf16[1024,1024]{1,0:T(8,128)(2,1)} fusion(bf16[1024,1920]{1,0:T(8,128)(2,1)} %bitcast.75, f32[1024,512]{1,0:T(8,128)S(1)} %copy-done.10, f32[1024]{0:T(1024)S(1)} %bitcast.89, f32[512]{0:T(512)S(1)} %copy-done.27), kind=kOutput, calls=%fused_computation.19 | convolution fusion | flops 1076363264 | bytes 5249024 | tf_op jit(solution)/shard_map/dot_general | solution.py:690
  111.5 2.5 %multiply_convert_fusion = (bf16[1024,512]{1,0:T(8,128)(2,1)S(1)}, f32[1024,512]{1,0:T(8,128)S(1)}, f32[512]{0:T(512)}) fusion(f32[1024,512]{1,0:T(8,128)S(1)} %copy-done.9, f32[1024,512]{1,0:T(8,128)S(1)} %copy-done.4, f32[1024]{0:T(1024)S(1)} %bitcast.92, f32[1024,512]{1,0:T(8,128)S(1)} %copy-done.10, f32[512,1024]{0,1:T(8,128)S(1)} %copy-done.11, ...), kind=kLoop, calls=%fused_computation.10 | loop fusion | flops 10485248 | bytes 11550720 | tf_op jit(solution)/shard_map/convert_element_type | solution.py:792
  114.0 1.5 convolution_convert_fusion.5.g_send
  115.5 41.2 %shard_map.308 = (bf16[1024,512]{1,0:T(8,128)(2,1)}, bf16[1024,256]{1,0:T(8,128)(2,1)}, f32[1024,8]{1,0:T(8,128)}, f32[48,128]{1,0:T(8,128)}, bf16[1024,1024]{1,0:T(8,128)(2,1)}) custom-call(f32[1024,512]{1,0:T(8,128)} %copy-done, f32[1032,8]{1,0:T(8,128)} %pad.8.colm, f32[8,128]{1,0:T(8,128)} %get-tuple-element.140.segr, ...), custom_call_target="tpu_custom_call" | custom-call | tf_op jit(solution)/shard_map/pallas_call | solution.py:707
  157.8 3.8 %fusion.18 = f32[1024,1024]{1,0:T(8,128)} fusion(bf16[1024,1920]{1,0:T(8,128)(2,1)} %bitcast.76, bf16[1024,8]{1,0:T(8,128)(2,1)S(1)} %convert_element_type.79), kind=kOutput, calls=%fused_computation.31 | convolution fusion | flops 268435456 | bytes 4472832 | tf_op jit(solution)/shard_map/dot_general | solution.py:690
  161.6 1.5 convolution_convert_fusion.4
  163.0 2.3 convolution_convert_fusion.3
  166.7 3.6 %convolution_convert_fusion.2 = bf16[1024,512]{1,0:T(8,128)(2,1)} fusion(bf16[1024,1024]{1,0:T(8,128)(2,1)S(1)} %copy-done.2, bf16[1024,512]{1,0:T(8,128)(2,1)} %get-tuple-element.59), kind=kOutput, calls=%fused_computation.21 | convolution fusion | flops 1074266112 | bytes 4194304 | tf_op jit(solution)/shard_map/dot_general | solution.py:696
  170.4 5.3 %add_convert_fusion.part = bf16[1024,1024]{1,0:T(8,128)(2,1)} fusion(f32[1024,1024]{1,0:T(8,128)S(1)} %copy-done.5, bf16[1024,1920]{1,0:T(8,128)(2,1)S(1)} %bitcast.78, bf16[1024,512]{1,0:T(8,128)(2,1)} %get-tuple-element.59, bf16[1024,512]{1,0:T(8,128)(2,1)} %copy-done.13), kind=kOutput, calls=%fused_computation | convolution fusion | flops 2153775104 | bytes 10485760 | tf_op jit(solution)/shard_map/dot_general | solution.py:690
  175.7 59.1 %shard_map.309 = (bf16[1024,1024]{1,0:T(8,128)(2,1)}, f32[64,512]{1,0:T(8,128)}, f32[64,512]{1,0:T(8,128)}, f32[64,512]{1,0:T(8,128)}, f32[64,128]{1,0:T(8,128)}...) custom-call(bf16[1024,1024]{1,0:T(8,128)(2,1)} %add_convert_fusion.p, ...), custom_call_target="tpu_custom_call" | custom-call | tf_op jit(solution)/shard_map/pallas_call | solution.py:707
  234.8 1.4 slice_reduce_fusion
  237.5 1.4 copy.66
  (94 shorter events, 26.7 us)
Async XLA Ops:
  0.6 57.0 %copy-start.23 = (f32[4,256]{1,0:T(4,128)S(1)}, f32[4,256]{1,0:T(4,128)}, u32[]{:S(2)}) copy-start(f32[4,256]{1,0:T(4,128)} %param.28) | copy-start | bytes 12292
  77.5 8.3 %collective-permute-start = (f32[128,512]{1,0:T(8,128)}, f32[128,512]{1,0:T(8,128)S(1)}, u32[]{:S(2)}, u32[]{:S(2)}) collective-permute-start(f32[128,512]{1,0:T(8,128)} %get-tuple-element.53), channel_id=1, source_target_pairs={{0,4},{1,5},{2,6},{3,7},{8,12},{9,13},{10,14},{11,15},{16,20},{17,... | collective-permute-start | bytes 786440 | tf_op jit(solution)/shard_map/ppermute | solution.py:686
  82.6 3.2 %copy-start.15 = (bf16[1024,128]{1,0:T(8,128)(2,1)S(1)}, bf16[1024,128]{1,0:T(8,128)(2,1)}, u32[]{:S(2)}) copy-start(bf16[1024,128]{1,0:T(8,128)(2,1)} %get-tuple-element.52) | copy-start | bytes 786436
  85.8 2.9 %copy-start.12 = (bf16[1024,1024]{1,0:T(8,128)(2,1)S(1)}, bf16[1024,1024]{1,0:T(8,128)(2,1)}, u32[]{:S(2)}) copy-start(bf16[1024,1024]{1,0:T(8,128)(2,1)} %cot.1) | copy-start | bytes 6291460
  85.8 2.9 %copy-start.27 = (f32[512]{0:T(512)S(1)}, f32[512]{0:T(512)}, u32[]{:S(2)}) copy-start(f32[512]{0:T(512)} %param.33) | copy-start | bytes 6148
  88.0 5.7 %copy-start.3 = (f32[1024,512]{1,0:T(8,128)}, f32[1024,512]{1,0:T(8,128)S(1)}, u32[]{:S(2)}) copy-start(f32[1024,512]{1,0:T(8,128)S(1)} %multiply_add_fusion) | copy-start | bytes 6291460
  103.7 3.8 %copy-start.10 = (f32[1024,512]{1,0:T(8,128)S(1)}, f32[1024,512]{1,0:T(8,128)}, u32[]{:S(2)}) copy-start(f32[1024,512]{1,0:T(8,128)} %get-tuple-element.128) | copy-start | bytes 6291460
  103.7 7.8 %copy-start.11 = (f32[512,1024]{0,1:T(8,128)S(1)}, f32[512,1024]{0,1:T(8,128)}, u32[]{:S(2)}) copy-start(f32[512,1024]{0,1:T(8,128)} %get-tuple-element.145) | copy-start | bytes 6291460
  107.4 4.0 %copy-start.4 = (f32[1024,512]{1,0:T(8,128)S(1)}, f32[1024,512]{1,0:T(8,128)}, u32[]{:S(2)}) copy-start(f32[1024,512]{1,0:T(8,128)} %copy-done.3) | copy-start | bytes 6291460
  107.4 4.0 %copy-start.9 = (f32[1024,512]{1,0:T(8,128)S(1)}, f32[1024,512]{1,0:T(8,128)}, u32[]{:S(2)}) copy-start(f32[1024,512]{1,0:T(8,128)} %get-tuple-element.54) | copy-start | bytes 6291460
  111.5 2.5 %copy-start.16 = (bf16[1024,128]{1,0:T(8,128)(2,1)S(1)}, bf16[1024,128]{1,0:T(8,128)(2,1)}, u32[]{:S(2)}) copy-start(bf16[1024,128]{1,0:T(8,128)(2,1)} %get-tuple-element.52) | copy-start | bytes 786436
  114.0 49.1 %copy-start.13 = (bf16[1024,512]{1,0:T(8,128)(2,1)}, bf16[1024,512]{1,0:T(8,128)(2,1)S(1)}, u32[]{:S(2)}) copy-start(bf16[1024,512]{1,0:T(8,128)(2,1)S(1)} %get-tuple-element.129) | copy-start | bytes 3145732
  157.8 3.8 %copy-start.2 = (bf16[1024,1024]{1,0:T(8,128)(2,1)S(1)}, bf16[1024,1024]{1,0:T(8,128)(2,1)}, u32[]{:S(2)}) copy-start(bf16[1024,1024]{1,0:T(8,128)(2,1)} %get-tuple-element.62.xn) | copy-start | bytes 6291460
  166.7 3.6 %copy-start.1 = (bf16[16,64,1920]{2,1,0:T(8,128)(2,1)S(1)}, bf16[16,64,1920]{2,1,0:T(8,128)(2,1)}, u32[]{:S(2)}) copy-start(bf16[16,64,1920]{2,1,0:T(8,128)(2,1)} %get-tuple-element.48) | copy-start | bytes 11796484
  166.7 3.7 %copy-start.5 = (f32[1024,1024]{1,0:T(8,128)S(1)}, f32[1024,1024]{1,0:T(8,128)}, u32[]{:S(2)}) copy-start(f32[1024,1024]{1,0:T(8,128)} %fusion.18) | copy-start | bytes 12582916
  175.7 63.3 %copy-start.6 = (bf16[1024,1024]{1,0:T(8,128)(2,1)S(1)}, bf16[1024,1024]{1,0:T(8,128)(2,1)}, u32[]{:S(2)}) copy-start(bf16[1024,1024]{1,0:T(8,128)(2,1)} %get-tuple-element.162) | copy-start | bytes 6291460
  238.9 2.3 copy-start.7
  241.3 2.7 %copy-start.21 = (f32[64,256]{1,0:T(8,128)S(1)}, f32[64,256]{1,0:T(8,128)}, u32[]{:S(2)}) copy-start(f32[64,256]{1,0:T(8,128)} %get-tuple-element.168) | copy-start | bytes 196612
  241.3 3.3 %copy-start.22 = (f32[4,512]{1,0:T(4,128)S(1)}, f32[4,512]{1,0:T(4,128)}, u32[]{:S(2)}) copy-start(f32[4,512]{1,0:T(4,128)} %get-tuple-element.169) | copy-start | bytes 24580
  241.3 3.9 %copy-start.26 = (f32[1,512]{1,0:T(1,128)S(1)}, f32[1,512]{1,0:T(1,128)}, u32[]{:S(2)}) copy-start(f32[1,512]{1,0:T(1,128)} %get-tuple-element.72) | copy-start | bytes 6148
  241.3 4.5 %copy-start.24 = (f32[4,256]{1,0:T(4,128)S(1)}, f32[4,256]{1,0:T(4,128)}, u32[]{:S(2)}) copy-start(f32[4,256]{1,0:T(4,128)} %get-tuple-element.171) | copy-start | bytes 12292
  241.3 5.1 %copy-start.28 = (f32[1,256]{1,0:T(1,128)S(1)}, f32[1,256]{1,0:T(1,128)}, u32[]{:S(2)}) copy-start(f32[1,256]{1,0:T(1,128)} %get-tuple-element.74) | copy-start | bytes 3076
  241.3 5.6 %copy-start.25 = (f32[1,512]{1,0:T(1,128)S(1)}, f32[1,512]{1,0:T(1,128)}, u32[]{:S(2)}) copy-start(f32[1,512]{1,0:T(1,128)} %get-tuple-element.76) | copy-start | bytes 6148
  241.3 6.2 %copy-start.17 = (f32[64,512]{1,0:T(8,128)S(1)}, f32[64,512]{1,0:T(8,128)}, u32[]{:S(2)}) copy-start(f32[64,512]{1,0:T(8,128)} %get-tuple-element.177) | copy-start | bytes 393220
  (6 other events, 10.1 us)

commit v4 on v3

--- a/solution.py
+++ b/solution.py
@@ -76,84 +76,6 @@
     first = jnp.where(lane < HEADDIM, slab, zero)
     second = jnp.where(lane >= HEADDIM, slab, zero)
     return jnp.concatenate([first, second], axis=0)
-
-
-def front_kernel(
-    tok, etok, w, colm, segr, cw, cb, dtb, alog, dsk, ex,
-    xn_o, z_o, xbc_o, pre_o, dtr_o, y_o, er_o, c_o, st_o, gain_o, xs,
-):
-    a_neg = -jnp.exp(alog[...])
-    causal, _ = triangles()
-    lower = as_low(causal)
-    gain_row = w[:, 1280:1408].astype(F32).T[8:9]
-    gain_o[...] = gain_row
-
-    def normed(block):
-        plain = block.astype(F32)
-        root = lax.rsqrt(jnp.mean(plain * plain, axis=1, keepdims=True) + EPSILON)
-        return (plain * root * gain_row).astype(BF)
-
-    edge = mm(normed(etok[...]), w[:, 512:1280]).astype(BF)
-    xbc_o[0:EDGE] = edge
-    xs[0:EDGE] = edge.astype(F32)
-    st_o[...] = jnp.zeros_like(st_o)
-    expand = ex[...]
-    dsk_e = mm2(dsk[...], expand)
-
-    def body(b, run):
-        r = pl.ds(pl.multiple_of(b * Q, Q), Q)
-        rn = pl.ds(pl.multiple_of(b * Q + EDGE, EDGE), Q)
-        xn = normed(tok[r])
-        xn_o[r] = xn
-        z_o[r] = mm(xn, w[:, 0:512])
-        xb = mm(xn, w[:, 512:1280]).astype(BF)
-        xbc_o[rn] = xb
-        xs[rn] = xb.astype(F32)
-        raw = mm(xn, w[:, 1280:1408])[:, 0:8]
-        dtr_o[r] = raw
-        marks = colm[r]
-        acts = []
-        for c in range(6):
-            lanes = slice(c * 128, c * 128 + 128)
-            slab = xs[pl.ds(pl.multiple_of(b * Q, Q), Q + EDGE), lanes]
-            pre = cb[:, lanes] + cw[3:4, lanes] * slab[EDGE:]
-            for d in range(1, 4):
-                pre = pre + (cw[3 - d : 4 - d, lanes] * slab[EDGE - d : Q + EDGE - d]) * marks[:, d : d + 1]
-            pre_o[r, lanes] = pre
-            acts.append(pre * sigmoid(pre))
-        b_low = acts[4].astype(BF)
-        c_low = acts[5].astype(BF)
-        c_o[r] = c_low
-        dt = softplus(raw + dtb[...])
-        cum = mm3_left(lower, dt * a_neg)
-        er_o[r] = jnp.exp(run + cum) * marks[:, 4:5]
-        cum_t = cum.T
-        last = cum[Q - 1 : Q]
-        enter = jnp.exp(cum) * marks[:, 5:6]
-        tail = jnp.exp(last - cum) * marks[:, 6:7]
-        dt_e = mm2(dt, expand)
-        enter_e = mm2(enter, expand)
-        tail_e = mm2(tail, expand)
-        mask = causal & (marks[:, 0:1] == segr[pl.ds(b, 1), :])
-        scores = jnp.where(mask, mm_nt(c_low, b_low), 0.0)
-        state = st_o[...]
-        inter = mm(c_low, state.astype(BF))
-        pieces = []
-        for p in range(4):
-            lanes = slice(p * 128, p * 128 + 128)
-            xdt = acts[p] * dt_e[:, lanes]
-            pieces.append((xdt * tail_e[:, lanes]).astype(BF))
-            ws = []
-            for h in (2 * p, 2 * p + 1):
-                decay = jnp.exp(jnp.minimum(cum[:, h : h + 1] - cum_t[h : h + 1, :], 0.0))
-                ws.append((decay * scores).astype(BF))
-            intra = mm(jnp.concatenate(ws, axis=1), halves(xdt.astype(BF)))
-            y_o[r, lanes] = intra + enter_e[:, lanes] * inter[:, lanes] + dsk_e[:, lanes] * acts[p]
-        fresh = mm_tn(b_low, jnp.concatenate(pieces, axis=1))
-        st_o[...] = enter_e[Q - 1 : Q] * state + fresh
-        return run + last
-
-    lax.fori_loop(0, 8, body, jnp.zeros((1, 8), F32))
 
 
 def back_kernel(
@@ -493,37 +415,234 @@
         self.landed(ref.at[self.half(self.t_far, 1)], offset + 1, self.up)
 
 
-def gather_kernel(wz, wx, wbc, wdt, norm, wo, etok, eseg, all_o, etok_o, eseg_o, mine, etok_b, send, recv):
+def forward_kernel(
+    wz, wx, wbc, wdt, norm, wo, etok, tok, cot, seg, cwx, cwb, cbx, cbb, dtb, alog, dsk, gg, ex, ext,
+    in_o, zo_o, xn_o, xbc_o, pre_o, dtr_o, colm_o, gain_o, st_o, dy_o, dz_o, yn_o, branch_o, carry_o, gate_o,
+    mine1, mine2, etok_b, eseg, xs, st, st_low, st_in, y_s, er_s, c_s, z_s, dn_s, row_s, row_r, send, recv,
+):
     shard, context, tensor, core, chip, chips, sibling, others, partner, ranks, group = places()
-    mine[:, 0:512] = wz[...]
-    mine[:, 512:1024] = wx[...]
-    mine[:, 1024:1280] = wbc[...]
-    mine[:, 1280:1408] = jnp.zeros((64, 128), BF)
-    mine[:, 1280:1288] = wdt[...]
-    mine[:, 1288:1289] = norm[...]
-    mine[:, 1408:1920] = wo[...]
-    greet([sibling, partner] + others[1:])
+    mine1[:, 0:512] = wx[...]
+    mine1[:, 512:768] = wbc[...]
+    mine1[:, 768:896] = jnp.zeros((64, 128), BF)
+    mine1[:, 768:776] = wdt[...]
+    mine1[:, 776:777] = norm[...]
+    mine2[:, 0:512] = wz[...]
+    mine2[:, 512:1024] = wo[...]
+    greet([sibling, partner] + others[1:] + group[1:])
     links = Links(send, recv)
+
+    def slot(ref, owner):
+        return ref.at[pl.ds(pl.multiple_of(owner * 64, 64), 64)]
+
+    seg_in = links.copy(seg, eseg, partner)
+    first = links.count - 1
+    for k in range(1, 8):
+        links.copy(mine1, slot(in_o, shard), others[k])
+    passed = links.count
+    links.copy(mine1, slot(in_o, shard), sibling)
     tokens_in = links.copy(etok, etok_b, partner)
-    seg_in = links.copy(eseg, eseg_o, partner)
-    first = [None]
+    second = links.count - 1
     for k in range(1, 8):
-        first.append(links.copy(mine, all_o.at[shard], others[k]))
-    base = links.count
-    links.copy(mine, all_o.at[shard], sibling)
-    all_o[shard] = mine[...]
+        links.copy(mine2, slot(zo_o, shard), others[k])
+    passed2 = links.count + 7
+    links.copy(mine2, slot(zo_o, shard), sibling)
+    mine_slot = pl.ds(pl.multiple_of(shard * 64, 64), 64)
+    in_o[mine_slot] = mine1[...]
+    zo_o[mine_slot] = mine2[...]
+
+    seg_in.wait_recv()
+    seg_t = seg[...].astype(F32).T
+    edge_t = jnp.where(context > 0, eseg[...].astype(F32).T, 0.0)
+    edge_col = edge_t[120:128, 7:8]
+    start = jnp.where(edge_col[7:8] == seg_t[0:1, 0:1], seg_t[0:1, 0:1], -1.0)
+    colm_o[1024:1032] = jnp.zeros((8, 8), F32)
+    for b in range(8):
+        col = seg_t[:, b : b + 1]
+        before = edge_col if b == 0 else seg_t[120:128, b - 1 : b]
+        longer = jnp.concatenate([before, col], axis=0)
+        entering = start if b == 0 else before[7:8]
+        marks = [col]
+        for d in range(1, 4):
+            marks.append(jnp.where(longer[8 - d : 136 - d] == col, 1.0, 0.0))
+        for value in (start, entering, col[127:128]):
+            marks.append(jnp.where(col == value, 1.0, 0.0))
+        marks.append(jnp.zeros_like(col))
+        colm_o[b * Q : b * Q + Q] = jnp.concatenate(marks, axis=1)
+
     for k in (1, 7, 2, 6, 3, 5, 4):
         source = lax.rem(chip + 8 - k, 8) * 2 + core
-        slot = all_o.at[source]
-        arrival(mine, slot, recv.at[1 + k], others[k]).wait_recv()
-        links.copy(slot, slot, sibling)
-    for n, k in enumerate((0, 1, 7, 2, 6, 3, 5, 4)):
+        arrival(None, slot(in_o, source), recv.at[first + k], others[k]).wait_recv()
+        made = pltpu.make_async_remote_copy(
+            src_ref=slot(in_o, source), dst_ref=slot(in_o, source), send_sem=send.at[24 + k], recv_sem=recv.at[24 + k],
+            device_id=sibling, device_id_type=MESH,
+        )
+        made.start()
+        links.started.append(made)
+    for k in range(8):
         source = lax.rem(chip + 8 - k, 8) * 2 + (1 - core)
-        arrival(mine, all_o.at[source], recv.at[base + n], sibling).wait_recv()
+        sem = recv.at[passed] if k == 0 else recv.at[24 + k]
+        arrival(None, slot(in_o, source), sem, sibling).wait_recv()
     tokens_in.wait_recv()
-    seg_in.wait_recv()
+
+    a_neg = -jnp.exp(alog[...])
+    causal, _ = triangles()
+    lower = as_low(causal)
+    gain_row = in_o[:, 768:896].astype(F32).T[8:9]
+    gain_o[...] = gain_row
+
+    def normed(block):
+        plain = block.astype(F32)
+        root = lax.rsqrt(jnp.mean(plain * plain, axis=1, keepdims=True) + EPSILON)
+        return (plain * root * gain_row).astype(BF)
+
+    edge_tokens = jnp.where(context > 0, etok_b[...].astype(F32), 0.0)
+    edge = mm(normed(edge_tokens), in_o[:, 0:768]).astype(BF)
+    xbc_o[0:EDGE] = edge
+    xs[0:EDGE] = edge.astype(F32)
+    st[...] = jnp.zeros_like(st)
+    expand = ex[...]
+    dsk_e = mm2(dsk[...], expand)
+
+    def forwarding(k):
+        source = lax.rem(chip + 8 - k, 8) * 2 + core
+        return pltpu.make_async_remote_copy(
+            src_ref=slot(zo_o, source), dst_ref=slot(zo_o, source), send_sem=send.at[32 + k], recv_sem=recv.at[32 + k],
+            device_id=sibling, device_id_type=MESH,
+        )
+
+    def body(b, run):
+        r = pl.ds(pl.multiple_of(b * Q, Q), Q)
+        rn = pl.ds(pl.multiple_of(b * Q + EDGE, EDGE), Q)
+        xn = normed(tok[r])
+        xn_o[r] = xn
+        both = mm(xn, in_o[...])
+        xb = both[:, 0:768].astype(BF)
+        xbc_o[rn] = xb
+        xs[rn] = xb.astype(F32)
+        raw = both[:, 768:776]
+        dtr_o[r] = raw
+        marks = colm_o[r]
+        acts = []
+        for c in range(6):
+            lanes = slice(c * 128, c * 128 + 128)
+            cw, cb, at = (cwx, cbx, lanes) if c < 4 else (cwb, cbb, slice(c * 128 - 512, c * 128 - 384))
+            slab = xs[pl.ds(pl.multiple_of(b * Q, Q), Q + EDGE), lanes]
+            pre = cb[:, at] + cw[3:4, at] * slab[EDGE:]
+            for d in range(1, 4):
+                pre = pre + (cw[3 - d : 4 - d, at] * slab[EDGE - d : Q + EDGE - d]) * marks[:, d : d + 1]
+            pre_o[r, lanes] = pre
+            acts.append(pre * sigmoid(pre))
+        b_low = acts[4].astype(BF)
+        c_low = acts[5].astype(BF)
+        c_s[r] = c_low
+        dt = softplus(raw + dtb[...])
+        cum = mm3_left(lower, dt * a_neg)
+        er_s[r] = jnp.exp(run + cum) * marks[:, 4:5]
+        cum_t = cum.T
+        last = cum[Q - 1 : Q]
+        enter = jnp.exp(cum) * marks[:, 5:6]
+        tail = jnp.exp(last - cum) * marks[:, 6:7]
+        dt_e = mm2(dt, expand)
+        enter_e = mm2(enter, expand)
+        tail_e = mm2(tail, expand)
+        mask = causal & (marks[:, 0:1] == seg[pl.ds(b, 1), :].astype(F32))
+        scores = jnp.where(mask, mm_nt(c_low, b_low), 0.0)
+        state = st[...]
+        inter = mm(c_low, state.astype(BF))
+        pieces = []
+        for p in range(4):
+            lanes = slice(p * 128, p * 128 + 128)
+            xdt = acts[p] * dt_e[:, lanes]
+            pieces.append((xdt * tail_e[:, lanes]).astype(BF))
+            ws = []
+            for h in (2 * p, 2 * p + 1):
+                decay = jnp.exp(jnp.minimum(cum[:, h : h + 1] - cum_t[h : h + 1, :], 0.0))
+                ws.append((decay * scores).astype(BF))
+            intra = mm(jnp.concatenate(ws, axis=1), halves(xdt.astype(BF)))
+            y_s[r, lanes] = intra + enter_e[:, lanes] * inter[:, lanes] + dsk_e[:, lanes] * acts[p]
+        fresh = mm_tn(b_low, jnp.concatenate(pieces, axis=1))
+        st[...] = enter_e[Q - 1 : Q] * state + fresh
+
+        @pl.when(b < 7)
+        def _():
+            k = b + 1
+            source = lax.rem(chip + 8 - k, 8) * 2 + core
+            arrival(None, slot(zo_o, source), recv.at[second + k], sibling).wait_recv()
+            forwarding(k).start()
+
+        return run + last
+
+    lax.fori_loop(0, 8, body, jnp.zeros((1, 8), F32))
+    st_low[...] = st[...].astype(BF)
+    links.count = 40
+    state_in = links.copy(st_low, st_in, partner)
+    for k in range(8):
+        source = lax.rem(chip + 8 - k, 8) * 2 + (1 - core)
+        sem = recv.at[passed2 - 7] if k == 0 else recv.at[32 + k]
+        arrival(None, slot(zo_o, source), sem, sibling).wait_recv()
+
+    def project(b, carry):
+        r = pl.ds(pl.multiple_of(b * Q, Q), Q)
+        z_s[r] = mm(xn_o[r], zo_o[:, 0:512])
+        dn_s[r] = mm(cot[r], zo_o[:, 512:1024])
+        return carry
+
+    lax.fori_loop(0, 8, project, 0)
+    state_in.wait_recv()
+    st_o[...] = jnp.where(context > 0, st_in[...].astype(F32), 0.0)
+
+    def sums(b, carry):
+        r = pl.ds(pl.multiple_of(b * Q, Q), Q)
+        y = y_s[r] + mm2(er_s[r], expand) * mm(c_s[r], st_o[...].astype(BF))
+        y_s[r] = y
+        z = z_s[r]
+        gated = y * (z * sigmoid(z))
+        first_sum = jnp.sum(gated * gated, axis=1, keepdims=True)
+        second_sum = jnp.sum(dn_s[r] * gg[...] * gated, axis=1, keepdims=True)
+        row_s[b] = jnp.concatenate([first_sum, second_sum, jnp.zeros((Q, 6), F32)], axis=1).T
+        return carry
+
+    lax.fori_loop(0, 8, sums, 0)
+    rows_in = [links.copy(row_s, row_r.at[k - 1], group[k]) for k in range(1, 4)]
+    for copy in rows_in:
+        copy.wait_recv()
+    gate_o[...] = jnp.zeros_like(gate_o)
+    st[...] = jnp.zeros_like(st)
+
+    def finish(b, carry):
+        r = pl.ds(pl.multiple_of(b * Q, Q), Q)
+        total = (row_s[b] + row_r[0, b] + row_r[1, b] + row_r[2, b]).T
+        root = lax.rsqrt(total[:, 0:1] * (1.0 / INNER) + EPSILON)
+        cross = (root * root * root) * (total[:, 1:2] * (1.0 / INNER))
+        er_e = mm2(er_s[r], expand)
+        normals, carries = [], []
+        for p in range(4):
+            lanes = slice(p * 128, p * 128 + 128)
+            y = y_s[r, lanes]
+            z = z_s[r, lanes]
+            dn = dn_s[r, lanes]
+            sig = sigmoid(z)
+            gate = z * sig
+            gated = y * gate
+            scaled = gated * root
+            normals.append((scaled * gg[:, lanes]).astype(BF))
+            gate_o[p : p + 1] += jnp.sum(dn * scaled, axis=0, keepdims=True)
+            d_gated = root * (dn * gg[:, lanes]) - gated * cross
+            d_y = d_gated * gate
+            dy_o[r, lanes] = d_y
+            dz_o[r, lanes] = (d_gated * y * (sig * (1.0 + z * (1.0 - sig)))).astype(BF)
+            carries.append((d_y * er_e[:, lanes]).astype(BF))
+        low = jnp.concatenate(normals, axis=1)
+        yn_o[r] = low
+        branch_o[r] = mm_nt(low, zo_o[:, 512:1024]).astype(BF)
+        st[...] += mm_tn(c_s[r], jnp.concatenate(carries, axis=1))
+        return carry
+
+    lax.fori_loop(0, 8, finish, 0)
+    carry_o[...] = st[...].astype(BF)
     links.finish()
-    etok_o[...] = jnp.where(context > 0, etok_b[...].astype(F32), 0.0).astype(BF)
+    for k in range(1, 8):
+        forwarding(k).wait_send()
 
 
 def tail_kernel(
@@ -540,7 +659,7 @@
         pltpu.make_async_copy(tok.at[own], tok_r, local_sem.at[0]),
         pltpu.make_async_copy(cot.at[own], cot_r, local_sem.at[1]),
         pltpu.make_async_copy(xn.at[own], xn_r, local_sem.at[2]),
-        pltpu.make_async_copy(w.at[:, pl.ds(1024, 256)], wbc, local_sem.at[3]),
+        pltpu.make_async_copy(w.at[:, pl.ds(512, 256)], wbc, local_sem.at[3]),
     ]
     for copy in fetch:
         copy.start()
@@ -680,12 +799,6 @@
     links.finish()
 
 
-def passed_along(value, axis, by):
-    count = lax.axis_size(axis)
-    pairs = [(i, i + by) for i in range(count) if 0 <= i + by < count]
-    return lax.ppermute(value, axis, pairs)
-
-
 def against(left, right):
     return lax.dot_general(
         left, right, (((1,), (1,)), ((), ())), preferred_element_type=jnp.float32
@@ -696,11 +809,6 @@
     return lax.dot_general(
         left, right, (((0,), (0,)), ((), ())), preferred_element_type=jnp.float32
     )
-
-
-def silu_slope(value):
-    sigma = jax.nn.sigmoid(value)
-    return sigma * (1.0 + value * (1.0 - sigma))
 
 
 def call(kernel, out_shapes, scratch, *args, specs=None, collective_id=None):
@@ -738,59 +846,27 @@
     head_count = dt_bias.shape[0]
     inner_width = head_count * HEADDIM
     bc_width = 2 * STATE
-    seg = segment
-    w_all, edge_tokens, edge_segs = call(
-        gather_kernel,
-        [((16, 64, 1920), BF), ((EDGE, 1024), BF), ((8, 128), jnp.int32)],
-        [((64, 1920), BF), ((EDGE, 1024), BF), ((24,), None), ((24,), None)],
-        w_z, w_x, w_bc, w_dt, norm_gain[:, None], w_out, tokens[length - EDGE :], seg.reshape(8, 128),
-        collective_id=1,
-    )
-    w_all = w_all.reshape(1024, 1920)
-    out_all = w_all[:, 1408:]
-    edge_ids = jnp.where(lax.axis_index("context") > 0, edge_segs[7, 112:], 0)
-    ext_ids = jnp.concatenate([edge_ids[-3:], seg])
-    start_seg = jnp.where(edge_ids[-1] == seg[0], seg[0], -1)
-    blocks = seg.reshape(length // Q, Q)
-    before = jnp.concatenate([start_seg[None], blocks[:-1, -1]])
-    marks = [seg.astype(F32)]
-    marks += [(ext_ids[3 - d : 3 - d + length] == seg).astype(F32) for d in (1, 2, 3)]
-    marks += [(seg == start_seg).astype(F32)]
-    marks += [(blocks == before[:, None]).astype(F32).reshape(-1)]
-    marks += [(blocks == blocks[:, -1:]).astype(F32).reshape(-1)]
-    marks += [jnp.zeros((length,), F32)]
-    colm = jnp.pad(jnp.stack(marks, axis=1), ((0, 8), (0, 0)))
-    segr = blocks.astype(F32)
-    conv_w = jnp.concatenate([conv_x, conv_bc], axis=1)
-    conv_b = jnp.concatenate([conv_xb, conv_bcb])[None]
+    seg = segment.reshape(8, 128)
+    segr = seg.astype(F32)
     expand_np = np.kron(np.eye(8), np.ones((1, HEADDIM)))
     expand = jnp.asarray(expand_np, BF)
     expand_t = jnp.asarray(expand_np.T, BF)
     wide = (length, inner_width)
-    x_normed, z_gate, xbc, pre, dt_raw, y_zero, enter_decay, c_act, state_local, gain_row = call(
-        front_kernel,
-        [((length, 1024), BF), (wide, F32), ((length + EDGE, 768), BF), ((length, 768), F32), ((length, 8), F32),
-         (wide, F32), ((length, 8), F32), ((length, STATE), BF), ((STATE, inner_width), F32), ((1, 1024), F32)],
-        [((length + EDGE, 768), F32)],
-        tokens, edge_tokens, w_all, colm, segr, conv_w, conv_b, dt_bias[None], a_log[None], d_skip[None], expand,
+    state = (STATE, inner_width)
+    heads = (dt_bias[None], a_log[None], d_skip[None])
+    (w_in, w_zo, x_normed, xbc, pre, dt_raw, colm, gain_row, state_in, d_y, d_z, y_normed, branch_part, d_carry, g_gate_gain) = call(
+        forward_kernel,
+        [((1024, 896), BF), ((1024, 1024), BF), ((length, 1024), BF), ((length + EDGE, 768), BF), ((length, 768), F32), ((length, 8), F32),
+         ((length + 8, 8), F32), ((1, 1024), F32), (state, F32), (wide, F32), (wide, BF), (wide, BF), ((length, 1024), BF), (state, BF), ((4, 128), F32)],
+        [((64, 896), BF), ((64, 1024), BF), ((EDGE, 1024), BF), ((8, 128), jnp.int32), ((length + EDGE, 768), F32), (state, F32), (state, BF), (state, BF),
+         (wide, F32), ((length, 8), F32), ((length, STATE), BF), (wide, F32), (wide, F32), ((8, 8, 128), F32), ((3, 8, 8, 128), F32),
+         ((48,), None), ((48,), None)],
+        w_z, w_x, w_bc, w_dt, norm_gain[:, None], w_out, tokens[length - EDGE :], tokens, cotangent, seg,
+        conv_x, conv_bc, conv_xb[None], conv_bcb[None], *heads, gate_gain[None], expand, expand_t,
+        collective_id=1,
     )
-    state_in = passed_along(state_local, "context", 1)
-    decay_e = jnp.repeat(enter_decay, HEADDIM, axis=1)
-    y_mixed = y_zero + decay_e * jnp.dot(c_act, state_in.astype(BF), preferred_element_type=F32)
-    gate_act = jax.nn.silu(z_gate)
-    gated = y_mixed * gate_act
-    d_y_normed = jnp.dot(cotangent, out_all, preferred_element_type=F32)
-    d_scaled = d_y_normed * gate_gain[None, :]
-    sums = lax.psum(jnp.stack([jnp.sum(gated * gated, axis=1), jnp.sum(d_scaled * gated, axis=1)]), "tensor")
-    gate_root = lax.rsqrt(sums[0] / INNER + EPSILON)[:, None]
-    y_normed = (gated * gate_root * gate_gain[None, :]).astype(BF)
-    branch_part = against(y_normed, out_all).astype(BF)
+    conv_w = jnp.concatenate([conv_x, conv_bc], axis=1)
     g_w_out = over_rows(cotangent, y_normed).astype(BF)
-    g_gate_gain = jnp.sum(d_y_normed * gated * gate_root, axis=0)
-    d_gated = gate_root * d_scaled - gated * gate_root**3 * (sums[1] / INNER)[:, None]
-    d_y = d_gated * gate_act
-    d_z = (d_gated * y_mixed * silu_slope(z_gate)).astype(BF)
-    d_carry = over_rows(c_act, (d_y * decay_e).astype(BF)).astype(BF)
     d_x_low, d_bc, d_dt_raw, small, output = call(
         back_kernel,
         [(wide, BF), ((length, bc_width), BF), ((length, 8), F32), ((48, 128), F32), ((length, 1024), BF)],
@@ -798,13 +874,12 @@
          ((STATE, inner_width), BF), ((EDGE, 768), F32), ((8, 768), F32), ((8, 768), F32),
          ((2, 128, 1024), BF), ((2, 128, 1024), BF), ((256, 1024), BF), ((256, 1024), BF), ((256, 1024), BF),
          ((16,), None), ((16,), None), ((1,), None)],
-        d_y, colm, segr, xbc, pre, dt_raw, state_in, d_carry, conv_w, dt_bias[None], a_log[None], d_skip[None], expand, expand_t,
+        d_y, colm, segr, xbc, pre, dt_raw, state_in, d_carry, conv_w, *heads, expand, expand_t,
         branch_part, tokens,
         specs=(15,), collective_id=3,
     )
     d_dt_low = jnp.pad(d_dt_raw.astype(BF), ((0, 0), (0, 120)))
-    gates = jnp.concatenate([d_z, d_x_low], axis=1)
-    part_in = (against(gates, w_all[:, :1024]) + against(d_dt_low, w_all[:, 1280:1408])).astype(BF)
+    part_in = (against(d_z, w_zo[:, :512]) + against(d_x_low, w_in[:, :512]) + against(d_dt_low, w_in[:, 768:])).astype(BF)
     g_w_z = over_rows(x_normed, d_z).astype(BF)
     g_w_x = over_rows(x_normed, d_x_low).astype(BF)
     g_w_dt = over_rows(x_normed, d_dt_low).astype(BF)
@@ -823,7 +898,7 @@
          ((256, 1024), BF), ((256, 1024), BF), ((256, 1024), BF), ((1024, 256), BF),
          ((64,), None), ((64,), None), ((4,), None)],
         part_in, d_bc, g_w_z.reshape(grid + (512,)), g_w_x.reshape(grid + (512,)), g_w_out.reshape(grid + (512,)),
-        g_w_dt.reshape(grid + (128,)), small, g_gate_gain.reshape(4, 128), gain_row, tokens, cotangent, x_normed, w_all,
+        g_w_dt.reshape(grid + (128,)), small, g_gate_gain, gain_row, tokens, cotangent, x_normed, w_in,
         specs=(9, 10, 11, 12), collective_id=2,
     )
     return (

time: 252 us -> 210 us (0.83)
  matrix products: 32.8 us -> 13.2 us
  local copies, waits for them, and re-layouts: 31 us -> 20.1 us
  blocking collectives: 9.85 us -> 0 us
  Pallas kernels: 161 us -> 169 us
  other arithmetic: 7.39 us -> 3.67 us
    psum x1 -> x0, blocking collectives: 9.85 us -> none  [local(): lax.psum(jnp.stack([jnp.sum(gated * gated, axis=1), jnp.sum(d_scaled * ga...]
    dot_general x3, matrix products: 13 us -> 4.59 us  [against(): lax.dot_general(left, right, (((1,), (1,)), ((), ())), preferred_element_...]
    pallas_call x4 -> x3, Pallas kernels: 161 us -> 169 us  [call(): pl.pallas_call(kernel, out_shape=[jax.ShapeDtypeStruct(s, d) for s, d in...]
    dot_general x2 -> x0, matrix products: 7.14 us -> none  [the longest x1 4.98 us: local(): d_y_normed = jnp.dot(cotangent, out_all, preferred_element_type=F32)]
    dot_general x5 -> x4, matrix products: 12.6 us -> 8.63 us  [over_rows(): lax.dot_general(left, right, (((0,), (0,)), ((), ())), preferred_element_...]
    slice x5 -> x0, local copies, waits for them, and re-layouts: 3.59 us -> none  [the longest x2 1.78 us: local(): start_seg = jnp.where(edge_ids[-1] == seg[0], seg[0], -1)]
    convert_element_type x2 -> x1, other arithmetic: 3.84 us -> 1.28 us  [local(): segr = seg.astype(F32)]
    unnamed x72 -> x53, local copies, waits for them, and re-layouts: 14.2 us -> 13.4 us
  transfers between devices with their start and end apart: 1 -> 0, of which waited for: 1 -> 0; matrix products, arithmetic and copies ran while one was open for 2% -> 0% of each run, Pallas kernels for 0% -> 0%
where the time goes in v4:
time: 210 us; the launch traced here: 207 us
  Pallas kernels  169 us (80%)
  local copies, waits for them, and re-layouts  20.1 us (10%)
  matrix products  13.2 us (6%)
  other arithmetic  3.67 us (2%)
    pallas_call x3, Pallas kernels, call(): pl.pallas_call(kernel, out_shape=[jax.ShapeDtypeStruct(s, d) for s, d in...  169 us
    unnamed x53, local copies, waits for them, and re-layouts  13.4 us
    dot_general x4, matrix products, over_rows(): lax.dot_general(left, right, (((0,), (0,)), ((), ())), preferred_element_...  8.63 us
    dot_general x3, matrix products, against(): lax.dot_general(left, right, (((1,), (1,)), ((), ())), preferred_element_...  4.59 us

profile of v4, /device:TPU:1, one launch (start us, length us, event | category | flops | bytes accessed | tf_op | source)
XLA Modules:
  0.0 206.8 jit_solution(6611426474249846896)
XLA Ops:
  0.6 1.3 bitcast_convert_fusion.segr
  1.9 1.3 pad_maximum_fusion.cw
  3.2 1.4 copy.40.norm
  4.6 1.4 copy.39.wdt
  6.0 1.4 slice.27.etok
  7.3 69.6 %shard_map.306 = (bf16[1024,896]{1,0:T(8,128)(2,1)}, bf16[1024,1024]{1,0:T(8,128)(2,1)}, bf16[1024,1024]{1,0:T(8,128)(2,1)}, bf16[1040,768]{1,0:T(8,128)(2,1)}, ...) custom-call(bf16[64,512]{1,0:T(8,128)(2,1)} %wz.1, ...), custom_call_target="tpu_custom_call" | custom-call | tf_op jit(solution)/shard_map/pallas_call | solution.py:815
  76.9 43.5 %shard_map.307 = (bf16[1024,512]{1,0:T(8,128)(2,1)}, bf16[1024,256]{1,0:T(8,128)(2,1)}, f32[1024,8]{1,0:T(8,128)}, f32[48,128]{1,0:T(8,128)}, bf16[1024,1024]{1,0:T(8,128)(2,1)}) custom-call(f32[1024,512]{1,0:T(8,128)} %get-tuple-element.49.dy, f32[1032,8]{1,0:T(8,128)} %get-tuple-element.50.colm, f32[8,128]{1,0:T(8,128)} %bitcast_convert_fusion.segr, ...), custom_call_target="tpu_custom_call" | custom-call | tf_op jit(solution)/shard_map/pallas_call | solution.py:815
  120.4 1.1 convert_element_type.27
  121.5 1.5 convolution_convert_fusion.3
  122.9 2.3 %convolution_convert_fusion.1 = bf16[1024,512]{1,0:T(8,128)(2,1)} fusion(bf16[1024,1024]{1,0:T(8,128)(2,1)S(1)} %copy-done.1, bf16[1024,512]{1,0:T(8,128)(2,1)S(1)} %copy-done.6), kind=kOutput, calls=%fused_computation.2 | convolution fusion | flops 1074266112 | bytes 4194304 | tf_op jit(solution)/shard_map/dot_general | solution.py:809
  125.2 1.3 fusion
  126.5 1.4 copy.41
  128.5 3.6 %convolution_convert_fusion.2 = bf16[1024,512]{1,0:T(8,128)(2,1)} fusion(bf16[1024,1024]{1,0:T(8,128)(2,1)S(1)} %copy-done.2, bf16[1024,512]{1,0:T(8,128)(2,1)} %get-tuple-element.58), kind=kOutput, calls=%fused_computation.3 | convolution fusion | flops 1074266112 | bytes 4194304 | tf_op jit(solution)/shard_map/dot_general | solution.py:809
  132.1 1.3 fusion.2
  133.6 0.7 fusion.4
  134.8 2.6 %add_convert_fusion.part = bf16[1024,1024]{1,0:T(8,128)(2,1)} fusion(f32[1024,1024]{1,0:T(8,128)S(1)} %fusion.4, f32[1024,1024]{1,0:T(8,128)S(1)} %fusion.2, bf16[1024,512]{1,0:T(8,128)(2,1)S(1)} %copy-done.7, bf16[1024,896]{1,0:T(8,128)(2,1)S(1)} %copy-done.3), kind=kOutput, calls=%fused_computation | convolution fusion | flops 1076887552 | bytes 12582912 | tf_op jit(solution)/shard_map/dot_general | solution.py:803
  137.4 56.0 %shard_map.308 = (bf16[1024,1024]{1,0:T(8,128)(2,1)}, f32[64,512]{1,0:T(8,128)}, f32[64,512]{1,0:T(8,128)}, f32[64,512]{1,0:T(8,128)}, f32[64,128]{1,0:T(8,128)}...) custom-call(bf16[1024,1024]{1,0:T(8,128)(2,1)} %add_convert_fusion.p, ...), custom_call_target="tpu_custom_call" | custom-call | tf_op jit(solution)/shard_map/pallas_call | solution.py:815
  193.4 1.4 slice_reduce_fusion
  194.8 1.3 slice_bitcast_fusion
  196.1 1.4 copy.42
  197.5 1.3 copy.54
  198.8 1.0 copy-done.5
  199.9 1.3 copy.55
  201.3 0.7 copy.56
  (47 shorter events, 6.2 us)
Async XLA Ops:
  76.9 44.5 %copy-start.1 = (bf16[1024,1024]{1,0:T(8,128)(2,1)S(1)}, bf16[1024,1024]{1,0:T(8,128)(2,1)}, u32[]{:S(2)}) copy-start(bf16[1024,1024]{1,0:T(8,128)(2,1)} %get-tuple-element.64.xn) | copy-start | bytes 6291460
  121.5 1.5 copy-start.6
  122.9 2.3 %copy-start = (bf16[1024,1024]{1,0:T(8,128)(2,1)S(1)}, bf16[1024,1024]{1,0:T(8,128)(2,1)}, u32[]{:S(2)}) copy-start(bf16[1024,1024]{1,0:T(8,128)(2,1)} %cot.3) | copy-start | bytes 6291460
  122.9 2.3 %copy-start.8 = (bf16[1024,512]{1,0:T(8,128)(2,1)S(1)}, bf16[1024,512]{1,0:T(8,128)(2,1)}, u32[]{:S(2)}) copy-start(bf16[1024,512]{1,0:T(8,128)(2,1)} %get-tuple-element.65) | copy-start | bytes 3145732
  126.5 2.0 copy-start.2
  128.5 3.6 %copy-start.18 = (bf16[1024,1024]{1,0:T(8,128)(2,1)S(1)}, bf16[1024,1024]{1,0:T(8,128)(2,1)}, u32[]{:S(2)}) copy-start(bf16[1024,1024]{1,0:T(8,128)(2,1)} %get-tuple-element.59) | copy-start | bytes 6291460
  128.5 3.6 %copy-start.19 = (bf16[1024,512]{1,0:T(8,128)(2,1)S(1)}, bf16[1024,512]{1,0:T(8,128)(2,1)}, u32[]{:S(2)}) copy-start(bf16[1024,512]{1,0:T(8,128)(2,1)} %get-tuple-element.58) | copy-start | bytes 3145732
  132.1 1.5 copy-start.3
  133.6 1.2 copy-start.7
  137.4 60.1 %copy-start.4 = (bf16[1024,1024]{1,0:T(8,128)(2,1)S(1)}, bf16[1024,1024]{1,0:T(8,128)(2,1)}, u32[]{:S(2)}) copy-start(bf16[1024,1024]{1,0:T(8,128)(2,1)} %get-tuple-element.133) | copy-start | bytes 6291460
  197.5 2.3 %copy-start.5 = (bf16[1024,1024]{1,0:T(8,128)(2,1)S(1)}, bf16[1024,1024]{1,0:T(8,128)(2,1)}, u32[]{:S(2)}) copy-start(bf16[1024,1024]{1,0:T(8,128)(2,1)} %get-tuple-element.134) | copy-start | bytes 6291460
  199.9 1.4 copy-start.11
  199.9 2.0 copy-start.10
  199.9 2.7 %copy-start.12 = (f32[64,256]{1,0:T(8,128)S(1)}, f32[64,256]{1,0:T(8,128)}, u32[]{:S(2)}) copy-start(f32[64,256]{1,0:T(8,128)} %get-tuple-element.139) | copy-start | bytes 196612
  199.9 3.3 %copy-start.13 = (f32[4,512]{1,0:T(4,128)S(1)}, f32[4,512]{1,0:T(4,128)}, u32[]{:S(2)}) copy-start(f32[4,512]{1,0:T(4,128)} %get-tuple-element.140) | copy-start | bytes 24580
  199.9 3.9 %copy-start.16 = (f32[1,512]{1,0:T(1,128)S(1)}, f32[1,512]{1,0:T(1,128)}, u32[]{:S(2)}) copy-start(f32[1,512]{1,0:T(1,128)} %get-tuple-element.76) | copy-start | bytes 6148
  199.9 4.5 %copy-start.14 = (f32[4,256]{1,0:T(4,128)S(1)}, f32[4,256]{1,0:T(4,128)}, u32[]{:S(2)}) copy-start(f32[4,256]{1,0:T(4,128)} %get-tuple-element.142) | copy-start | bytes 12292
  199.9 5.1 %copy-start.17 = (f32[1,256]{1,0:T(1,128)S(1)}, f32[1,256]{1,0:T(1,128)}, u32[]{:S(2)}) copy-start(f32[1,256]{1,0:T(1,128)} %get-tuple-element.78) | copy-start | bytes 3076
  199.9 5.6 %copy-start.15 = (f32[1,512]{1,0:T(1,128)S(1)}, f32[1,512]{1,0:T(1,128)}, u32[]{:S(2)}) copy-start(f32[1,512]{1,0:T(1,128)} %get-tuple-element.80) | copy-start | bytes 6148
  199.9 6.2 %copy-start.9 = (f32[64,512]{1,0:T(8,128)S(1)}, f32[64,512]{1,0:T(8,128)}, u32[]{:S(2)}) copy-start(f32[64,512]{1,0:T(8,128)} %get-tuple-element.148) | copy-start | bytes 393220

commit v5 on v4

--- a/solution.py
+++ b/solution.py
@@ -79,19 +79,21 @@
 
 
 def back_kernel(
-    dy, colm, segr, xbc, pre_r, dtr, st_in, g_send, cw, dtb, alog, dsk, ex, ext, branch, tok,
-    dx_o, dbc_o, ddt_o, small_o, out_o,
-    states, acts, dpre, grad, heads, g_in, tail_r, ret_s, ret_r, near, relay, from_d, from_u, tok_r, send, recv, local_sem,
+    dy, colm, seg, xbc, pre_r, dtr, st_in, g_send, cwx, cwb, dtb, alog, dsk, ex, ext, branch, gz, go, tok,
+    dx_o, dbc_o, ddt_o, small_o, out_o, oz, oo,
+    states, acts, dpre, grad, heads, g_in, tail_r, ret_s, ret_r, near, relay, from_d, from_u, tok_r,
+    sz, so, chunk, rg, cs, cr, send, recv, local_sem,
 ):
-    shard, context, tensor, core, chip, chips, sibling, others, partner, ranks, group = places()
+    shard, context, tensor, core, chip, chips, sibling, others, partner, ranks, group, at = places()
     own = pl.ds(pl.multiple_of(tensor * 256, 256), 256)
     fetch = pltpu.make_async_copy(tok.at[own], tok_r, local_sem.at[0])
     fetch.start()
-    greet([partner, group[1], group[3]])
+    greet([partner, sibling, group[1], group[3]] + others[1:])
     links = Links(send, recv)
     carry_in = links.copy(g_send, g_in, partner)
     ring = Ring(links, tensor, group)
     ring.reduce_first(branch, near, from_d, from_u)
+    sib_in = (links.copy(gz.at[:, 1 - core], sz, sibling), links.copy(go.at[:, 1 - core], so, sibling))
     a_neg = -jnp.exp(alog[...])
     causal, anti = triangles()
     lower = as_low(causal)
@@ -134,6 +136,16 @@
         lanes = slice(c * 128, c * 128 + 128)
         pre = pre_r[r7, lanes]
         acts[r7, lanes] = pre * sigmoid(pre)
+    for copy in sib_in:
+        copy.wait_recv()
+
+    def merge(c, carry):
+        for mine, theirs, at in ((gz, sz, 0), (go, so, 512)):
+            chunk[c, :, at : at + 512] = (mine[c, core].astype(F32) + theirs[c].astype(F32)).astype(BF)
+        return carry
+
+    lax.fori_loop(0, 8, merge, 0)
+    grads_in = [links.copy(chunk.at[chips[k]], rg.at[k - 1], others[k]) for k in range(1, 8)]
     carry_in.wait_recv()
     grad[...] = jnp.where(context == 0, g_in[...].astype(F32), 0.0)
     heads[...] = jnp.zeros_like(heads)
@@ -164,7 +176,7 @@
         g_low = g_now.astype(BF)
         inter = mm(c_low, state_low)
         back = mm(b_low, g_low)
-        mask = causal & (marks[:, 0:1] == segr[pl.ds(b, 1), :])
+        mask = causal & (marks[:, 0:1] == seg[pl.ds(b, 1), :].astype(F32))
         scores = jnp.where(mask, mm_nt(c_low, b_low), 0.0)
         kept = jnp.sum(state * g_now, axis=0, keepdims=True) * keep_e
         entered, tailed, e_terms, q_terms, x_terms, k_terms = [], [], [], [], [], []
@@ -217,7 +229,7 @@
         d_log = mm3_left(upper, d_cum) + head_sum(jnp.concatenate(q_terms, axis=1))
         d_dt = d_log * a_neg + head_sum(jnp.concatenate(x_terms, axis=1))
         d_raw = d_dt * sigmoid(raw)
-        ddt_o[r] = d_raw
+        ddt_o[r] = jnp.concatenate([d_raw, jnp.zeros((Q, 120), F32)], axis=1).astype(BF)
         heads[0:1] += jnp.sum(d_raw, axis=0, keepdims=True)
         heads[1:2] += jnp.sum(d_log * dt, axis=0, keepdims=True) * a_neg
         heads[2:3] += head_sum(jnp.concatenate(k_terms, axis=1))
@@ -245,28 +257,36 @@
     for c in range(6):
         lanes = slice(c * 128, c * 128 + 128)
         first = dpre[0:16, lanes]
+        cw, wl = (cwx, lanes) if c < 4 else (cwb, slice(c * 128 - 512, c * 128 - 384))
         flags = jnp.concatenate([jnp.zeros((8, 8), F32), colm[0:8]], axis=0)
         total = jnp.zeros((8, 128), F32)
         for d in range(1, 4):
-            total = total + cw[3 - d : 4 - d, lanes] * (first * flags[:, d : d + 1])[d : d + 8]
+            total = total + cw[3 - d : 4 - d, wl] * (first * flags[:, d : d + 1])[d : d + 8]
         ret_s[:, lanes] = total
     ret_in = links.copy(ret_s, ret_r, partner)
     ring.gather_second(out_o)
+    for copy in grads_in:
+        copy.wait_recv()
+    for at in range(0, 1024, 128):
+        lanes = slice(at, at + 128)
+        cs[:, lanes] = add_slots(chunk[chip, :, lanes].astype(F32), rg, lanes).astype(BF)
+    grads_ctx = links.copy(cs, cr, partner)
     for c in range(6):
         lanes = slice(c * 128, c * 128 + 128)
-
-        def conv(b, sums, lanes=lanes, c=c):
+        cw, wl = (cwx, lanes) if c < 4 else (cwb, slice(c * 128 - 512, c * 128 - 384))
+
+        def conv(b, sums, lanes=lanes, c=c, cw=cw, wl=wl):
             r = pl.ds(pl.multiple_of(b * Q, Q), Q)
             slab = dpre[pl.ds(pl.multiple_of(b * Q + 8, 8), Q + 8), lanes]
             marks = colm[pl.ds(pl.multiple_of(b * Q, Q), Q + 8)]
             xin = xbc[pl.ds(pl.multiple_of(b * Q, Q), Q + EDGE), lanes].astype(F32)
             main = slab[0:Q]
-            out = cw[3:4, lanes] * main
+            out = cw[3:4, wl] * main
             new = [sums[0] + jnp.sum(main, axis=0, keepdims=True),
                    sums[1] + jnp.sum(main * xin[EDGE:], axis=0, keepdims=True)]
             for d in range(1, 4):
                 masked = slab * marks[:, d : d + 1]
-                out = out + cw[3 - d : 4 - d, lanes] * masked[d : d + Q]
+                out = out + cw[3 - d : 4 - d, wl] * masked[d : d + Q]
                 new.append(sums[d + 1] + jnp.sum(masked[0:Q] * xin[EDGE - d : Q + EDGE - d], axis=0, keepdims=True))
             if c < 4:
                 dx_o[r, lanes] = out.astype(BF)
@@ -291,6 +311,9 @@
     last = tail_r[...] + jnp.concatenate([jnp.zeros((EDGE - 8, 768), F32), returned], axis=0)
     dx_o[1024 - EDGE : 1024] = last[:, 0:512].astype(BF)
     dbc_o[1024 - EDGE : 1024] = last[:, 512:768].astype(BF)
+    grads_ctx.wait_recv()
+    oz[...] = cs[:, 0:512].astype(F32) + cr[:, 0:512].astype(F32)
+    oo[...] = cs[:, 512:1024].astype(F32) + cr[:, 512:1024].astype(F32)
     ring.gather_wait(out_o)
     links.finish()
 
@@ -351,7 +374,7 @@
     partner = at(context_to=1 - context)
     ranks = [None] + [lax.rem(tensor + k, 4) for k in range(1, 4)]
     group = [None] + [at(tensor_to=t) for t in ranks[1:]]
-    return shard, context, tensor, core, chip, chips, sibling, others, partner, ranks, group
+    return shard, context, tensor, core, chip, chips, sibling, others, partner, ranks, group, at
 
 
 class Ring:
@@ -366,15 +389,17 @@
     def whole(self, rank):
         return pl.ds(pl.multiple_of(rank * 256, 256), 256)
 
-    def reduce_first(self, src, near, from_down, from_up):
-        copy = self.links.copy
-        self.first = (
-            copy(src.at[self.half(self.t_far, 0)], near.at[0], self.up),
-            copy(src.at[self.half(self.t_far, 1)], near.at[1], self.down),
-        )
+    def reduce_first(self, src, near, from_down, from_up, make=None):
+        def send(rank, which, dst, device):
+            rows = self.half(rank, which)
+            if make is not None:
+                make(rows)
+            return self.links.copy(src.at[rows], dst, device)
+
+        self.first = (send(self.t_far, 0, near.at[0], self.up), send(self.t_far, 1, near.at[1], self.down))
         self.alone = (
-            copy(src.at[self.half(self.t_up, 1)], from_down.at[pl.ds(128, 128)], self.up),
-            copy(src.at[self.half(self.t_down, 0)], from_up.at[pl.ds(0, 128)], self.down),
+            send(self.t_up, 1, from_down.at[pl.ds(128, 128)], self.up),
+            send(self.t_down, 0, from_up.at[pl.ds(0, 128)], self.down),
         )
 
     def reduce_second(self, src, near, relay, from_down, from_up):
@@ -415,41 +440,94 @@
         self.landed(ref.at[self.half(self.t_far, 1)], offset + 1, self.up)
 
 
+class Spread:
+    def __init__(self, mine, out, base, send, recv, core, chip, at):
+        self.mine, self.out, self.base, self.send, self.recv, self.core, self.chip = mine, out, base, send, recv, core, chip
+        x = lax.rem(chip, 4)
+        right, left, far = (chip - x + lax.rem(x + k, 4) for k in (1, 3, 2))
+        over = lax.rem(chip + 4, 8)
+        o_right, o_left, o_far = (lax.rem(c + 4, 8) for c in (right, left, far))
+        there = [at(shard_to=c * 2 + core) for c in (over, right, left)]
+        sibling = at(shard_to=chip * 2 + (1 - core))
+        to_over, to_right, to_left = there
+        self.copies = [
+            (None, None, to_over), (None, None, to_right), (None, None, to_left), (None, None, sibling),
+            (over, None, to_right), (over, None, to_left),
+            (left, 0, to_right), (right, 1, to_left), (o_left, 0, to_right), (o_right, 1, to_left),
+        ]
+        owners = [over, left, right, o_left, o_right, far, o_far]
+        self.copies += [(owner, None, sibling) for owner in owners]
+        self.arrivals = [
+            (over, None, core), (left, None, core), (right, None, core), (chip, None, 1 - core), (o_left, None, core), (o_right, None, core),
+            (far, 0, core), (far, 1, core), (o_far, 0, core), (o_far, 1, core),
+        ]
+        self.arrivals += [(owner, None, 1 - core) for owner in owners]
+
+    def slot(self, owner, core, half):
+        start = (owner * 2 + core) * 64
+        if half is None:
+            return self.out.at[pl.ds(pl.multiple_of(start, 64), 64)]
+        return self.out.at[pl.ds(pl.multiple_of(start + half * 32, 32), 32)]
+
+    def copy(self, i):
+        owner, half, device = self.copies[i]
+        dst = self.slot(self.chip if owner is None else owner, self.core, half)
+        src = self.mine if owner is None else dst
+        return pltpu.make_async_remote_copy(
+            src_ref=src, dst_ref=dst, send_sem=self.send.at[self.base + i], recv_sem=self.recv.at[self.base + i],
+            device_id=device, device_id_type=MESH,
+        )
+
+    def wait(self, i):
+        owner, half, core = self.arrivals[i]
+        arrival(None, self.slot(owner, core, half), self.recv.at[self.base + i], self.copies[i][2]).wait_recv()
+
+    def begin(self):
+        for i in (0, 1, 2, 3):
+            self.copy(i).start()
+        self.out[pl.ds(pl.multiple_of((self.chip * 2 + self.core) * 64, 64), 64)] = self.mine[...]
+
+    def event(self, n):
+        waits, starts = (
+            ((1,), (6, 11)), ((2,), (7, 12)), ((0,), (4, 5, 10)), ((6, 7), (15,)),
+            ((4,), (8, 13)), ((5,), (9, 14)), ((8, 9), (16,)),
+        )[n]
+        for i in waits:
+            self.wait(i)
+        for i in starts:
+            self.copy(i).start()
+
+    def collect(self):
+        for i in (3,) + tuple(range(10, 17)):
+            self.wait(i)
+
+    def sent(self):
+        for i in range(17):
+            self.copy(i).wait_send()
+
+
 def forward_kernel(
-    wz, wx, wbc, wdt, norm, wo, etok, tok, cot, seg, cwx, cwb, cbx, cbb, dtb, alog, dsk, gg, ex, ext,
-    in_o, zo_o, xn_o, xbc_o, pre_o, dtr_o, colm_o, gain_o, st_o, dy_o, dz_o, yn_o, branch_o, carry_o, gate_o,
-    mine1, mine2, etok_b, eseg, xs, st, st_low, st_in, y_s, er_s, c_s, z_s, dn_s, row_s, row_r, send, recv,
+    wz, wx, wbc, wdt, norm, wo, tok, cot, seg, cwx, cwb, cbx, cbb, dtb, alog, dsk, gg, ex, ext,
+    in_o, zo_o, xn_o, xbc_o, pre_o, dtr_o, colm_o, gain_o, st_o, dy_o, dz_o, branch_o, carry_o, gate_o, gz_o, go_o,
+    mine1, mine2, etok_b, eseg, xs, st, st_low, st_in, y_s, er_s, c_s, z_s, dn_s, row_s, row_r, yn_o, send, recv,
 ):
-    shard, context, tensor, core, chip, chips, sibling, others, partner, ranks, group = places()
+    shard, context, tensor, core, chip, chips, sibling, others, partner, ranks, group, at = places()
     mine1[:, 0:512] = wx[...]
     mine1[:, 512:768] = wbc[...]
     mine1[:, 768:896] = jnp.zeros((64, 128), BF)
     mine1[:, 768:776] = wdt[...]
-    mine1[:, 776:777] = norm[...]
+    mine1[:, 776:777] = jnp.broadcast_to(norm[...].astype(F32), (8, 64)).T[:, 0:1].astype(BF)
     mine2[:, 0:512] = wz[...]
     mine2[:, 512:1024] = wo[...]
     greet([sibling, partner] + others[1:] + group[1:])
     links = Links(send, recv)
 
-    def slot(ref, owner):
-        return ref.at[pl.ds(pl.multiple_of(owner * 64, 64), 64)]
-
+    links.count = 34
     seg_in = links.copy(seg, eseg, partner)
-    first = links.count - 1
-    for k in range(1, 8):
-        links.copy(mine1, slot(in_o, shard), others[k])
-    passed = links.count
-    links.copy(mine1, slot(in_o, shard), sibling)
-    tokens_in = links.copy(etok, etok_b, partner)
-    second = links.count - 1
-    for k in range(1, 8):
-        links.copy(mine2, slot(zo_o, shard), others[k])
-    passed2 = links.count + 7
-    links.copy(mine2, slot(zo_o, shard), sibling)
-    mine_slot = pl.ds(pl.multiple_of(shard * 64, 64), 64)
-    in_o[mine_slot] = mine1[...]
-    zo_o[mine_slot] = mine2[...]
-
+    tokens_in = links.copy(tok.at[pl.ds(1024 - EDGE, EDGE)], etok_b, partner)
+    spread1 = Spread(mine1, in_o, 0, send, recv, core, chip, at)
+    spread2 = Spread(mine2, zo_o, 17, send, recv, core, chip, at)
+    spread1.begin()
     seg_in.wait_recv()
     seg_t = seg[...].astype(F32).T
     edge_t = jnp.where(context > 0, eseg[...].astype(F32).T, 0.0)
@@ -469,19 +547,10 @@
         marks.append(jnp.zeros_like(col))
         colm_o[b * Q : b * Q + Q] = jnp.concatenate(marks, axis=1)
 
-    for k in (1, 7, 2, 6, 3, 5, 4):
-        source = lax.rem(chip + 8 - k, 8) * 2 + core
-        arrival(None, slot(in_o, source), recv.at[first + k], others[k]).wait_recv()
-        made = pltpu.make_async_remote_copy(
-            src_ref=slot(in_o, source), dst_ref=slot(in_o, source), send_sem=send.at[24 + k], recv_sem=recv.at[24 + k],
-            device_id=sibling, device_id_type=MESH,
-        )
-        made.start()
-        links.started.append(made)
-    for k in range(8):
-        source = lax.rem(chip + 8 - k, 8) * 2 + (1 - core)
-        sem = recv.at[passed] if k == 0 else recv.at[24 + k]
-        arrival(None, slot(in_o, source), sem, sibling).wait_recv()
+    for n in range(7):
+        spread1.event(n)
+    spread2.begin()
+    spread1.collect()
     tokens_in.wait_recv()
 
     a_neg = -jnp.exp(alog[...])
@@ -502,13 +571,6 @@
     st[...] = jnp.zeros_like(st)
     expand = ex[...]
     dsk_e = mm2(dsk[...], expand)
-
-    def forwarding(k):
-        source = lax.rem(chip + 8 - k, 8) * 2 + core
-        return pltpu.make_async_remote_copy(
-            src_ref=slot(zo_o, source), dst_ref=slot(zo_o, source), send_sem=send.at[32 + k], recv_sem=recv.at[32 + k],
-            device_id=sibling, device_id_type=MESH,
-        )
 
     def body(b, run):
         r = pl.ds(pl.multiple_of(b * Q, Q), Q)
@@ -563,23 +625,15 @@
         fresh = mm_tn(b_low, jnp.concatenate(pieces, axis=1))
         st[...] = enter_e[Q - 1 : Q] * state + fresh
 
-        @pl.when(b < 7)
-        def _():
-            k = b + 1
-            source = lax.rem(chip + 8 - k, 8) * 2 + core
-            arrival(None, slot(zo_o, source), recv.at[second + k], sibling).wait_recv()
-            forwarding(k).start()
+        for n in range(7):
+            pl.when(b == n)(partial(spread2.event, n))
 
         return run + last
 
     lax.fori_loop(0, 8, body, jnp.zeros((1, 8), F32))
     st_low[...] = st[...].astype(BF)
-    links.count = 40
     state_in = links.copy(st_low, st_in, partner)
-    for k in range(8):
-        source = lax.rem(chip + 8 - k, 8) * 2 + (1 - core)
-        sem = recv.at[passed2 - 7] if k == 0 else recv.at[32 + k]
-        arrival(None, slot(zo_o, source), sem, sibling).wait_recv()
+    spread2.collect()
 
     def project(b, carry):
         r = pl.ds(pl.multiple_of(b * Q, Q), Q)
@@ -640,26 +694,32 @@
 
     lax.fori_loop(0, 8, finish, 0)
     carry_o[...] = st[...].astype(BF)
+    for m in range(8):
+        lanes = slice(m * 128, m * 128 + 128)
+        gz_o[m] = mm_tn(xn_o[:, lanes], dz_o[...]).astype(BF).reshape(2, 64, 512)
+        go_o[m] = mm_tn(cot[:, lanes], yn_o[...]).astype(BF).reshape(2, 64, 512)
     links.finish()
-    for k in range(1, 8):
-        forwarding(k).wait_send()
+    spread1.sent()
+    spread2.sent()
+
+
+def add_slots(total, slots, lanes):
+    for k in range(7):
+        total = total + slots[k, :, lanes].astype(F32)
+    return total
 
 
 def tail_kernel(
-    part, dbc, gz, gx, go, gd, small, gate, gain, tok, cot, xn, w,
-    dtok_o, oz, ox, oo, odt, obc, onorm, conv_o, convb_o, bc_o, bcb_o, gate_o, heads_o,
-    near, relay, from_d, from_u, near2, relay2, from_d2, from_u2, sz, sx, so, sd, chunk, rg, cs, cr,
-    g2, s2, chunk2, rg2, c2s, c2r, t2,
-    sm, sm_s, sm_c, sm_x, sm_r, sm_t,
-    tok_r, cot_r, xn_r, wbc, send, recv, local_sem,
+    dz, dx, ddt, dbc, small, gate, gain, w_in, w_zo, xn, tok, cot,
+    dtok_o, ox, odt, obc, onorm, conv_o, convb_o, bc_o, bcb_o, gate_o, dtb_o, alog_o, dsk_o,
+    part, gx, near, relay, from_d, from_u, sx, chunk, rg, cs, cr, t2,
+    sm, sm_s, sm_c, sm_x, sm_r, sm_t, nm, nm_s, nm_c, nm_x, nm_r, nm_t, tok_r, cot_r, send, recv, local_sem,
 ):
-    shard, context, tensor, core, chip, chips, sibling, others, partner, ranks, group = places()
+    shard, context, tensor, core, chip, chips, sibling, others, partner, ranks, group, at = places()
     own = pl.ds(pl.multiple_of(tensor * 256, 256), 256)
     fetch = [
         pltpu.make_async_copy(tok.at[own], tok_r, local_sem.at[0]),
         pltpu.make_async_copy(cot.at[own], cot_r, local_sem.at[1]),
-        pltpu.make_async_copy(xn.at[own], xn_r, local_sem.at[2]),
-        pltpu.make_async_copy(w.at[:, pl.ds(512, 256)], wbc, local_sem.at[3]),
     ]
     for copy in fetch:
         copy.start()
@@ -667,70 +727,66 @@
     links = Links(send, recv)
     sm[...] = small[...]
     sm[20:24] = gate[...]
-    wide, thin = Ring(links, tensor, group), Ring(links, tensor, group)
-    thin.reduce_first(dbc, near2, from_d2, from_u2)
-    wide.reduce_first(part, near, from_d, from_u)
-    sib_in = [
-        links.copy(sm, sm_s, sibling),
-        links.copy(gz.at[:, 1 - core], sz, sibling),
-        links.copy(gx.at[:, 1 - core], sx, sibling),
-        links.copy(go.at[:, 1 - core], so, sibling),
-        links.copy(gd.at[:, 1 - core], sd, sibling),
-    ]
-    thin.reduce_second(dbc, near2, relay2, from_d2, from_u2)
-    for copy in sib_in:
-        copy.wait_recv()
+    wide = Ring(links, tensor, group)
+
+    def make(r):
+        total = mm_nt(dz[r], w_zo[:, 0:512]) + mm_nt(dx[r], w_in[:, 0:512]) + mm_nt(ddt[r], w_in[:, 768:896]) + mm_nt(dbc[r], w_in[:, 512:768])
+        part[r] = total.astype(BF)
+
+    wide.reduce_first(part, near, from_d, from_u, make)
+    small_in = links.copy(sm, sm_s, sibling)
+
+    def outer(m):
+        block = xn[:, m * 128 : m * 128 + 128]
+        gx[m, :, :, 0:512] = mm_tn(block, dx[...]).astype(BF).reshape(2, 64, 512)
+        gx[m, :, :, 512:640] = mm_tn(block, ddt[...]).astype(BF).reshape(2, 64, 128)
+        gx[m, :, :, 640:896] = mm_tn(block, dbc[...]).astype(BF).reshape(2, 64, 256)
+
+    make(wide.half(wide.t_up, 0))
+    make(wide.half(wide.t_down, 1))
+    for m in range(4):
+        outer(m)
+    wide.reduce_second(part, near, relay, from_d, from_u)
+    for m in range(4, 8):
+        outer(m)
+    sib_in = links.copy(gx.at[:, 1 - core], sx, sibling)
+    small_in.wait_recv()
     sm_c[chip] = sm[...] + sm_s[...]
-    small_in = [links.copy(sm_c.at[chip], sm_c.at[chip], others[k]) for k in range(1, 8)]
-    small_base = links.count - 8
+    small_base = links.count - 1
+    for k in range(1, 8):
+        links.copy(sm_c.at[chip], sm_c.at[chip], others[k])
+    make(wide.half(tensor, 0))
+    make(wide.half(tensor, 1))
+    sib_in.wait_recv()
 
     def merge(c, carry):
-        for mine, theirs, at in ((gz, sz, 0), (gx, sx, 512), (go, so, 1024)):
-            chunk[c, :, at : at + 512] = (mine[c, core].astype(F32) + theirs[c].astype(F32)).astype(BF)
-        chunk[c, :, 1536:1664] = (gd[c, core].astype(F32) + sd[c].astype(F32)).astype(BF)
+        chunk[c] = (gx[c, core].astype(F32) + sx[c].astype(F32)).astype(BF)
         return carry
 
     lax.fori_loop(0, 8, merge, 0)
-    wide.reduce_second(part, near, relay, from_d, from_u)
     grads_in = [links.copy(chunk.at[chips[k]], rg.at[k - 1], others[k]) for k in range(1, 8)]
 
     for copy in fetch:
         copy.wait()
-    thin.reduce_wait()
     wide.reduce_wait()
-    ones = jnp.full((64, 128), 1.0, BF)
-
-    def slice_rows(i):
+
+    def inner(i, g_norm):
         r = pl.ds(pl.multiple_of(i * 64, 64), 64)
         rt = pl.ds(pl.multiple_of(tensor * 256 + i * 64, 64), 64)
-        return r, rt
-
-    def inner(i, carry):
-        r, rt = slice_rows(i)
-        d_bc = dbc[rt].astype(F32) + from_d2[r].astype(F32) + from_u2[r].astype(F32)
-        d_bc_low = d_bc.astype(BF)
         total = part[rt].astype(F32) + from_d[r].astype(F32) + from_u[r].astype(F32)
-        total = total + mm_nt(d_bc_low, wbc[...])
         plain = tok_r[r].astype(F32)
         root = lax.rsqrt(jnp.mean(plain * plain, axis=1, keepdims=True) + EPSILON)
         stat = plain * root
         d_plain = total * gain[...]
         mean = jnp.mean(d_plain * plain, axis=1, keepdims=True)
         dtok_o[rt] = (cot_r[r].astype(F32) + root * d_plain - stat * (root * root) * mean).astype(BF)
-        g_bc, g_norm = carry
-        g_bc = g_bc + mm_tn(xn_r[r], d_bc_low)
-        g_norm = g_norm + mm_tn((total * stat).astype(BF), ones)
-        return g_bc, g_norm
-
-    g_bc, g_norm = lax.fori_loop(0, 4, inner, (jnp.zeros((1024, 256), F32), jnp.zeros((1024, 128), F32)))
-    g2[:, :, :, 0:256] = g_bc.astype(BF).reshape(8, 2, 64, 256)
-    g2[:, :, :, 256:384] = g_norm.astype(BF).reshape(8, 2, 64, 128)
-    sib2_in = links.copy(g2.at[:, 1 - core], s2, sibling)
+        return g_norm + jnp.sum(total * stat, axis=0, keepdims=True)
+
+    g_norm = lax.fori_loop(0, 4, inner, jnp.zeros((1, 1024), F32))
     wide.gather_first(dtok_o)
-    sib2_in.wait_recv()
     for c in range(8):
-        chunk2[c] = (g2[c, core].astype(F32) + s2[c].astype(F32)).astype(BF)
-    grads2_in = [links.copy(chunk2.at[chips[k]], rg2.at[k - 1], others[k]) for k in range(1, 8)]
+        nm[c : c + 1] = g_norm[:, c * 128 : c * 128 + 128]
+    norm_sib = links.copy(nm, nm_s, sibling)
 
     for k in range(1, 8):
         source = lax.rem(chip + 8 - k, 8)
@@ -740,25 +796,26 @@
         total = total + sm_c[c]
     sm_x[...] = total
     small_ctx = links.copy(sm_x, sm_r, partner)
+    norm_sib.wait_recv()
+    nm_c[chip] = nm[...] + nm_s[...]
+    norm_base = links.count - 1
+    for k in range(1, 8):
+        links.copy(nm_c.at[chip], nm_c.at[chip], others[k])
     for copy in grads_in:
         copy.wait_recv()
-    for at in range(0, 1664, 128):
-        lanes = slice(at, at + 128)
-        acc = chunk[chip, :, lanes].astype(F32)
-        for k in range(7):
-            acc = acc + rg[k, :, lanes].astype(F32)
-        cs[:, lanes] = acc.astype(BF)
+    for col in range(0, 896, 128):
+        lanes = slice(col, col + 128)
+        cs[:, lanes] = add_slots(chunk[chip, :, lanes].astype(F32), rg, lanes).astype(BF)
     grads_ctx = links.copy(cs, cr, partner)
     wide.gather_second(dtok_o)
-    for copy in grads2_in:
-        copy.wait_recv()
-    for at in range(0, 384, 128):
-        lanes = slice(at, at + 128)
-        acc = chunk2[chip, :, lanes].astype(F32)
-        for k in range(7):
-            acc = acc + rg2[k, :, lanes].astype(F32)
-        c2s[:, lanes] = acc
-    grads2_ctx = links.copy(c2s, c2r, partner)
+    for k in range(1, 8):
+        source = lax.rem(chip + 8 - k, 8)
+        arrival(None, nm_c.at[source], recv.at[norm_base + k], others[k]).wait_recv()
+    total = nm_c[0]
+    for c in range(1, 8):
+        total = total + nm_c[c]
+    nm_x[...] = total
+    norm_ctx = links.copy(nm_x, nm_r, partner)
     small_ctx.wait_recv()
     sums = sm_x[...] + sm_r[...]
     for k in range(4):
@@ -767,24 +824,29 @@
     for p in range(4):
         convb_o[:, p * 128 : p * 128 + 128] = sums[16 + p : 17 + p]
         gate_o[:, p * 128 : p * 128 + 128] = sums[20 + p : 21 + p]
-    heads_o[...] = sums[24:32]
+    dtb_o[...] = sums[24:25, 0:8]
+    alog_o[...] = sums[25:26, 0:8]
+    dsk_o[...] = sums[26:27, 0:8]
     sm_t[tensor] = sums[32:48]
     small_t = links.count
     for k in range(1, 4):
         links.copy(sm_t.at[tensor], sm_t.at[tensor], group[k])
-    grads2_ctx.wait_recv()
-    t2[tensor] = c2s[...] + c2r[...]
+    norm_ctx.wait_recv()
+    nm_t[tensor] = nm_x[...] + nm_r[...]
+    norm_t = links.count
+    for k in range(1, 4):
+        links.copy(nm_t.at[tensor], nm_t.at[tensor], group[k])
+    grads_ctx.wait_recv()
+    ox[...] = cs[:, 0:512].astype(F32) + cr[:, 0:512].astype(F32)
+    t2[tensor] = cs[:, 640:896].astype(F32) + cr[:, 640:896].astype(F32)
     grads2_t = links.count
     for k in range(1, 4):
         links.copy(t2.at[tensor], t2.at[tensor], group[k])
-    grads_ctx.wait_recv()
-    oz[...] = cs[:, 0:512].astype(F32) + cr[:, 0:512].astype(F32)
-    ox[...] = cs[:, 512:1024].astype(F32) + cr[:, 512:1024].astype(F32)
-    oo[...] = cs[:, 1024:1536].astype(F32) + cr[:, 1024:1536].astype(F32)
-    odt[...] = cs[:, 1536:1664].astype(F32) + cr[:, 1536:1664].astype(F32)
+    odt[...] = (cs[:, 512:640].astype(F32) + cr[:, 512:640].astype(F32))[:, 0:8]
     for k in range(1, 4):
         source = lax.rem(tensor + 4 - k, 4)
         arrival(None, sm_t.at[source], recv.at[small_t + k - 1], group[k]).wait_recv()
+        arrival(None, nm_t.at[source], recv.at[norm_t + k - 1], group[k]).wait_recv()
         arrival(None, t2.at[source], recv.at[grads2_t + k - 1], group[k]).wait_recv()
     sums = (sm_t[0] + sm_t[1]) + (sm_t[2] + sm_t[3])
     for k in range(4):
@@ -792,23 +854,12 @@
             bc_o[k : k + 1, p * 128 : p * 128 + 128] = sums[k * 2 + p : k * 2 + p + 1]
     for p in range(2):
         bcb_o[:, p * 128 : p * 128 + 128] = sums[8 + p : 9 + p]
-    both = (t2[0] + t2[1]) + (t2[2] + t2[3])
-    obc[...] = both[:, 0:256]
-    onorm[...] = both[:, 256:384]
+    obc[...] = (t2[0] + t2[1]) + (t2[2] + t2[3])
+    nm_s[...] = (nm_t[0] + nm_t[1]) + (nm_t[2] + nm_t[3])
+    row = nm_s[pl.ds(chip, 1), :]
+    onorm[...] = jnp.where(core == 0, row[:, 0:64], row[:, 64:128])
     wide.gather_wait(dtok_o)
     links.finish()
-
-
-def against(left, right):
-    return lax.dot_general(
-        left, right, (((1,), (1,)), ((), ())), preferred_element_type=jnp.float32
-    )
-
-
-def over_rows(left, right):
-    return lax.dot_general(
-        left, right, (((0,), (0,)), ((), ())), preferred_element_type=jnp.float32
-    )
 
 
 def call(kernel, out_shapes, scratch, *args, specs=None, collective_id=None):
@@ -847,77 +898,57 @@
     inner_width = head_count * HEADDIM
     bc_width = 2 * STATE
     seg = segment.reshape(8, 128)
-    segr = seg.astype(F32)
     expand_np = np.kron(np.eye(8), np.ones((1, HEADDIM)))
     expand = jnp.asarray(expand_np, BF)
     expand_t = jnp.asarray(expand_np.T, BF)
     wide = (length, inner_width)
     state = (STATE, inner_width)
+    grid = (8, 2, 64, 512)
     heads = (dt_bias[None], a_log[None], d_skip[None])
-    (w_in, w_zo, x_normed, xbc, pre, dt_raw, colm, gain_row, state_in, d_y, d_z, y_normed, branch_part, d_carry, g_gate_gain) = call(
+    (w_in, w_zo, x_normed, xbc, pre, dt_raw, colm, gain_row, state_in, d_y, d_z, branch_part, d_carry, g_gate_gain, g_w_z, g_w_out) = call(
         forward_kernel,
         [((1024, 896), BF), ((1024, 1024), BF), ((length, 1024), BF), ((length + EDGE, 768), BF), ((length, 768), F32), ((length, 8), F32),
-         ((length + 8, 8), F32), ((1, 1024), F32), (state, F32), (wide, F32), (wide, BF), (wide, BF), ((length, 1024), BF), (state, BF), ((4, 128), F32)],
+         ((length + 8, 8), F32), ((1, 1024), F32), (state, F32), (wide, F32), (wide, BF), ((length, 1024), BF), (state, BF), ((4, 128), F32), (grid, BF), (grid, BF)],
         [((64, 896), BF), ((64, 1024), BF), ((EDGE, 1024), BF), ((8, 128), jnp.int32), ((length + EDGE, 768), F32), (state, F32), (state, BF), (state, BF),
-         (wide, F32), ((length, 8), F32), ((length, STATE), BF), (wide, F32), (wide, F32), ((8, 8, 128), F32), ((3, 8, 8, 128), F32),
+         (wide, F32), ((length, 8), F32), ((length, STATE), BF), (wide, F32), (wide, F32), ((8, 8, 128), F32), ((3, 8, 8, 128), F32), (wide, BF),
          ((48,), None), ((48,), None)],
-        w_z, w_x, w_bc, w_dt, norm_gain[:, None], w_out, tokens[length - EDGE :], tokens, cotangent, seg,
+        w_z, w_x, w_bc, w_dt, norm_gain[None], w_out, tokens, cotangent, seg,
         conv_x, conv_bc, conv_xb[None], conv_bcb[None], *heads, gate_gain[None], expand, expand_t,
         collective_id=1,
     )
-    conv_w = jnp.concatenate([conv_x, conv_bc], axis=1)
-    g_w_out = over_rows(cotangent, y_normed).astype(BF)
-    d_x_low, d_bc, d_dt_raw, small, output = call(
+    own = (64, 512)
+
+    def vector(shape, last):
+        return [(s, F32) for s in (shape, shape, (8,) + shape, shape, shape, last)]
+
+    half = ((2, 128, 1024), BF)
+    rows = ((256, 1024), BF)
+    d_x_low, d_bc, d_dt_low, small, output, o_z, o_out = call(
         back_kernel,
-        [(wide, BF), ((length, bc_width), BF), ((length, 8), F32), ((48, 128), F32), ((length, 1024), BF)],
-        [((8, STATE, inner_width), F32), ((length, 768), F32), ((length + 16, 768), F32), ((STATE, inner_width), F32), ((8, 8), F32),
-         ((STATE, inner_width), BF), ((EDGE, 768), F32), ((8, 768), F32), ((8, 768), F32),
-         ((2, 128, 1024), BF), ((2, 128, 1024), BF), ((256, 1024), BF), ((256, 1024), BF), ((256, 1024), BF),
-         ((16,), None), ((16,), None), ((1,), None)],
-        d_y, colm, segr, xbc, pre, dt_raw, state_in, d_carry, conv_w, *heads, expand, expand_t,
-        branch_part, tokens,
-        specs=(15,), collective_id=3,
+        [(wide, BF), ((length, 2 * STATE), BF), ((length, 128), BF), ((48, 128), F32), ((length, 1024), BF), (own, F32), (own, F32)],
+        [((8, STATE, inner_width), F32), ((length, 768), F32), ((length + 16, 768), F32), (state, F32), ((8, 8), F32),
+         (state, BF), ((EDGE, 768), F32), ((8, 768), F32), ((8, 768), F32),
+         half, half, rows, rows, rows,
+         ((8, 64, 512), BF), ((8, 64, 512), BF), ((8, 64, 1024), BF), ((7, 64, 1024), BF), ((64, 1024), BF), ((64, 1024), BF),
+         ((32,), None), ((32,), None), ((1,), None)],
+        d_y, colm, seg, xbc, pre, dt_raw, state_in, d_carry, conv_x, conv_bc, *heads, expand, expand_t,
+        branch_part, g_w_z, g_w_out, tokens,
+        specs=(18,), collective_id=3,
     )
-    d_dt_low = jnp.pad(d_dt_raw.astype(BF), ((0, 0), (0, 120)))
-    part_in = (against(d_z, w_zo[:, :512]) + against(d_x_low, w_in[:, :512]) + against(d_dt_low, w_in[:, 768:])).astype(BF)
-    g_w_z = over_rows(x_normed, d_z).astype(BF)
-    g_w_x = over_rows(x_normed, d_x_low).astype(BF)
-    g_w_dt = over_rows(x_normed, d_dt_low).astype(BF)
-    grid = (8, 2, 64)
-    d_tokens, o_z, o_x, o_out, o_dt, o_bc, o_norm, conv_o, convb_o, cbc_o, cbcb_o, gate_o, heads_o = call(
+    d_tokens, o_x, o_dt, o_bc, o_norm, conv_o, convb_o, cbc_o, cbcb_o, gate_o, dtb_o, alog_o, dsk_o = call(
         tail_kernel,
-        [((length, 1024), BF), ((64, 512), F32), ((64, 512), F32), ((64, 512), F32), ((64, 128), F32),
-         ((64, 256), F32), ((64, 128), F32), ((4, 512), F32), ((1, 512), F32), ((4, 256), F32), ((1, 256), F32), ((1, 512), F32), ((8, 128), F32)],
-        [((2, 128, 1024), BF), ((2, 128, 1024), BF), ((256, 1024), BF), ((256, 1024), BF),
-         ((2, 128, 256), BF), ((2, 128, 256), BF), ((256, 256), BF), ((256, 256), BF),
-         ((8, 64, 512), BF), ((8, 64, 512), BF), ((8, 64, 512), BF), ((8, 64, 128), BF), ((8, 64, 1664), BF), ((7, 64, 1664), BF),
-         ((64, 1664), BF), ((64, 1664), BF),
-         ((8, 2, 64, 384), BF), ((8, 64, 384), BF), ((8, 64, 384), BF), ((7, 64, 384), BF),
-         ((64, 384), F32), ((64, 384), F32), ((4, 64, 384), F32),
-         ((48, 128), F32), ((48, 128), F32), ((8, 48, 128), F32), ((48, 128), F32), ((48, 128), F32), ((4, 16, 128), F32),
-         ((256, 1024), BF), ((256, 1024), BF), ((256, 1024), BF), ((1024, 256), BF),
-         ((64,), None), ((64,), None), ((4,), None)],
-        part_in, d_bc, g_w_z.reshape(grid + (512,)), g_w_x.reshape(grid + (512,)), g_w_out.reshape(grid + (512,)),
-        g_w_dt.reshape(grid + (128,)), small, g_gate_gain, gain_row, tokens, cotangent, x_normed, w_in,
-        specs=(9, 10, 11, 12), collective_id=2,
+        [((length, 1024), BF), (own, F32), ((64, 8), F32), ((64, 256), F32), ((1, 64), F32),
+         ((4, 512), F32), ((1, 512), F32), ((4, 256), F32), ((1, 256), F32), ((1, 512), F32), ((1, 8), F32), ((1, 8), F32), ((1, 8), F32)],
+        [((length, 1024), BF), ((8, 2, 64, 896), BF), half, half, rows, rows,
+         ((8, 64, 896), BF), ((8, 64, 896), BF), ((7, 64, 896), BF), ((64, 896), BF), ((64, 896), BF), ((4, 64, 256), F32),
+         *vector((48, 128), (4, 16, 128)), *vector((8, 128), (4, 8, 128)),
+         rows, rows, ((64,), None), ((64,), None), ((2,), None)],
+        d_z, d_x_low, d_dt_low, d_bc, small, g_gate_gain, gain_row, w_in, w_zo, x_normed, tokens, cotangent,
+        specs=(10, 11), collective_id=2,
     )
     return (
-        output,
-        d_tokens,
-        o_norm[:, 0],
-        o_z,
-        o_x,
-        o_dt[:, 0:8],
-        o_bc,
-        conv_o,
-        convb_o[0],
-        cbc_o,
-        cbcb_o[0],
-        heads_o[0, 0:8],
-        heads_o[1, 0:8],
-        heads_o[2, 0:8],
-        gate_o[0],
-        o_out,
+        output, d_tokens, o_norm[0], o_z, o_x, o_dt, o_bc, conv_o, convb_o[0], cbc_o, cbcb_o[0],
+        dtb_o[0], alog_o[0], dsk_o[0], gate_o[0], o_out,
     )
 
 

time: 210 us -> 184 us (0.88); the launches traced: 207 us -> 184 us
  matrix products: 13.2 us -> 0 us
  local copies, waits for them, and re-layouts: 20.1 us -> 14.1 us
  other arithmetic: 3.67 us -> 0 us
    dot_general x7 -> x0, matrix products: 13.2 us -> none  [the longest x4 8.63 us: over_rows(): lax.dot_general(left, right, (((0,), (0,)), ((), ())), preferred_element_...]
    slice x2 -> x0, local copies, waits for them, and re-layouts: 2.76 us -> none  [the longest x1 1.38 us: local(): o_norm[:, 0]]
    convert_element_type x2 -> x0, other arithmetic: 2.35 us -> none  [the longest x1 1.28 us: local(): segr = seg.astype(F32)]
    unnamed x53 -> x47, local copies, waits for them, and re-layouts: 13.4 us -> 14.1 us
where the time goes in v5:
time: 184 us
  Pallas kernels  169 us (92%)
  local copies, waits for them, and re-layouts  14.1 us (8%)
    pallas_call x3, Pallas kernels, call(): pl.pallas_call(kernel, out_shape=[jax.ShapeDtypeStruct(s, d) for s, d in...  169 us
    unnamed x47, local copies, waits for them, and re-layouts  14.1 us

profile of v5, /device:TPU:1, one launch (start us, length us, event | category | flops | bytes accessed | tf_op | source)
XLA Modules:
  0.0 183.9 jit_solution(5417913762534275115)
XLA Ops:
  0.6 1.4 copy.35.wdt
  2.0 69.1 %shard_map.306 = (bf16[1024,896]{1,0:T(8,128)(2,1)}, bf16[1024,1024]{1,0:T(8,128)(2,1)}, bf16[1024,1024]{1,0:T(8,128)(2,1)}, bf16[1040,768]{1,0:T(8,128)(2,1)}, ...) custom-call(bf16[64,512]{1,0:T(8,128)(2,1)} %wz.1, ...), custom_call_target="tpu_custom_call" | custom-call | tf_op jit(solution)/shard_map/pallas_call | solution.py:866
  71.2 45.1 %shard_map.307 = (bf16[1024,512]{1,0:T(8,128)(2,1)}, bf16[1024,256]{1,0:T(8,128)(2,1)}, bf16[1024,128]{1,0:T(8,128)(2,1)}, f32[48,128]{1,0:T(8,128)}, bf16[1024,...) custom-call(f32[1024,512]{1,0:T(8,128)} %get-tuple-element.52.dy, f32[1032,8]{1,0:T(8,128)} %get-tuple-element.53.colm, ...), custom_call_target="tpu_custom_call" | custom-call | tf_op jit(solution)/shard_map/pallas_call | solution.py:866
  116.3 54.9 %shard_map.308 = (bf16[1024,1024]{1,0:T(8,128)(2,1)}, f32[64,512]{1,0:T(8,128)}, f32[64,8]{1,0:T(8,128)}, f32[64,256]{1,0:T(8,128)}, f32[1,64]{1,0:T(1,128)}, /*...) custom-call(bf16[1024,512]{1,0:T(8,128)(2,1)} %get-tuple-element.63., ...), custom_call_target="tpu_custom_call" | custom-call | tf_op jit(solution)/shard_map/pallas_call | solution.py:866
  171.1 1.4 copy.36
  172.6 1.3 copy.52
  173.9 1.0 copy-done.1
  174.9 0.0 copy-start.6
  174.9 0.0 copy-start.9
  174.9 0.0 copy-start.7
  175.0 1.3 copy.53
  176.3 0.5 copy.54
  176.9 0.7 copy.55
  177.5 0.7 copy.56
  178.2 0.6 copy.57
  178.8 0.6 copy.58
  179.4 0.6 copy.59
  180.0 0.6 copy.60
  180.6 0.6 copy.61
  181.2 0.5 copy.62
  181.7 0.5 copy.63
  182.2 0.5 copy.64
  182.7 0.6 copy.65
  183.3 0.7 copy.66
  (26 shorter events, 0.1 us)
Async XLA Ops:
  116.3 56.3 %copy-start = (bf16[1024,1024]{1,0:T(8,128)(2,1)S(1)}, bf16[1024,1024]{1,0:T(8,128)(2,1)}, u32[]{:S(2)}) copy-start(bf16[1024,1024]{1,0:T(8,128)(2,1)} %get-tuple-element.120) | copy-start | bytes 6291460
  172.6 2.3 %copy-start.1 = (bf16[1024,1024]{1,0:T(8,128)(2,1)S(1)}, bf16[1024,1024]{1,0:T(8,128)(2,1)}, u32[]{:S(2)}) copy-start(bf16[1024,1024]{1,0:T(8,128)(2,1)} %get-tuple-element.121) | copy-start | bytes 6291460
  174.9 1.4 copy-start.14
  174.9 1.9 %copy-start.3 = (f32[64,512]{1,0:T(8,128)S(1)}, f32[64,512]{1,0:T(8,128)}, u32[]{:S(2)}) copy-start(f32[64,512]{1,0:T(8,128)} %get-tuple-element.123) | copy-start | bytes 393220
  174.9 2.6 %copy-start.4 = (f32[64,512]{1,0:T(8,128)S(1)}, f32[64,512]{1,0:T(8,128)}, u32[]{:S(2)}) copy-start(f32[64,512]{1,0:T(8,128)} %get-tuple-element.124) | copy-start | bytes 393220
  174.9 3.3 %copy-start.5 = (f32[64,256]{1,0:T(8,128)S(1)}, f32[64,256]{1,0:T(8,128)}, u32[]{:S(2)}) copy-start(f32[64,256]{1,0:T(8,128)} %get-tuple-element.126) | copy-start | bytes 196612
  174.9 3.9 %copy-start.6 = (f32[4,512]{1,0:T(4,128)S(1)}, f32[4,512]{1,0:T(4,128)}, u32[]{:S(2)}) copy-start(f32[4,512]{1,0:T(4,128)} %get-tuple-element.127) | copy-start | bytes 24580
  174.9 4.5 %copy-start.9 = (f32[1,512]{1,0:T(1,128)S(1)}, f32[1,512]{1,0:T(1,128)}, u32[]{:S(2)}) copy-start(f32[1,512]{1,0:T(1,128)} %get-tuple-element.80) | copy-start | bytes 6148
  174.9 5.0 %copy-start.7 = (f32[4,256]{1,0:T(4,128)S(1)}, f32[4,256]{1,0:T(4,128)}, u32[]{:S(2)}) copy-start(f32[4,256]{1,0:T(4,128)} %get-tuple-element.129) | copy-start | bytes 12292
  175.0 5.6 %copy-start.10 = (f32[1,256]{1,0:T(1,128)S(1)}, f32[1,256]{1,0:T(1,128)}, u32[]{:S(2)}) copy-start(f32[1,256]{1,0:T(1,128)} %get-tuple-element.82) | copy-start | bytes 3076
  175.0 6.2 %copy-start.13 = (f32[1,8]{1,0:T(1,128)S(1)}, f32[1,8]{1,0:T(1,128)}, u32[]{:S(2)}) copy-start(f32[1,8]{1,0:T(1,128)} %get-tuple-element.83) | copy-start | bytes 100
  175.0 6.7 %copy-start.12 = (f32[1,8]{1,0:T(1,128)S(1)}, f32[1,8]{1,0:T(1,128)}, u32[]{:S(2)}) copy-start(f32[1,8]{1,0:T(1,128)} %get-tuple-element.84) | copy-start | bytes 100
  175.0 7.2 %copy-start.11 = (f32[1,8]{1,0:T(1,128)S(1)}, f32[1,8]{1,0:T(1,128)}, u32[]{:S(2)}) copy-start(f32[1,8]{1,0:T(1,128)} %get-tuple-element.85) | copy-start | bytes 100
  175.0 7.7 %copy-start.8 = (f32[1,512]{1,0:T(1,128)S(1)}, f32[1,512]{1,0:T(1,128)}, u32[]{:S(2)}) copy-start(f32[1,512]{1,0:T(1,128)} %get-tuple-element.86) | copy-start | bytes 6148
  175.0 8.3 %copy-start.2 = (f32[64,512]{1,0:T(8,128)S(1)}, f32[64,512]{1,0:T(8,128)}, u32[]{:S(2)}) copy-start(f32[64,512]{1,0:T(8,128)} %get-tuple-element.135) | copy-start | bytes 393220

commit v6 on v5

--- a/solution.py
+++ b/solution.py
@@ -76,246 +76,6 @@
     first = jnp.where(lane < HEADDIM, slab, zero)
     second = jnp.where(lane >= HEADDIM, slab, zero)
     return jnp.concatenate([first, second], axis=0)
-
-
-def back_kernel(
-    dy, colm, seg, xbc, pre_r, dtr, st_in, g_send, cwx, cwb, dtb, alog, dsk, ex, ext, branch, gz, go, tok,
-    dx_o, dbc_o, ddt_o, small_o, out_o, oz, oo,
-    states, acts, dpre, grad, heads, g_in, tail_r, ret_s, ret_r, near, relay, from_d, from_u, tok_r,
-    sz, so, chunk, rg, cs, cr, send, recv, local_sem,
-):
-    shard, context, tensor, core, chip, chips, sibling, others, partner, ranks, group, at = places()
-    own = pl.ds(pl.multiple_of(tensor * 256, 256), 256)
-    fetch = pltpu.make_async_copy(tok.at[own], tok_r, local_sem.at[0])
-    fetch.start()
-    greet([partner, sibling, group[1], group[3]] + others[1:])
-    links = Links(send, recv)
-    carry_in = links.copy(g_send, g_in, partner)
-    ring = Ring(links, tensor, group)
-    ring.reduce_first(branch, near, from_d, from_u)
-    sib_in = (links.copy(gz.at[:, 1 - core], sz, sibling), links.copy(go.at[:, 1 - core], so, sibling))
-    a_neg = -jnp.exp(alog[...])
-    causal, anti = triangles()
-    lower = as_low(causal)
-    upper = as_low(anti)
-    expand = ex[...]
-    expand_t = ext[...]
-    dsk_e = mm2(dsk[...], expand)
-
-    def head_sum(v):
-        return mm2(v, expand_t)
-
-    states[0] = st_in[...]
-
-    def forward(b, carry):
-        r = pl.ds(pl.multiple_of(b * Q, Q), Q)
-        marks = colm[r]
-        dt = softplus(dtr[r] + dtb[...])
-        cum = mm3_left(lower, dt * a_neg)
-        last = cum[Q - 1 : Q]
-        tail = jnp.exp(last - cum) * marks[:, 6:7] * dt
-        keep_e = mm2(jnp.exp(last) * marks[Q - 1 : Q, 5:6], expand)
-        tail_e = mm2(tail, expand)
-        pieces = []
-        for c in range(6):
-            lanes = slice(c * 128, c * 128 + 128)
-            pre = pre_r[r, lanes]
-            act = pre * sigmoid(pre)
-            acts[r, lanes] = act
-            if c < 4:
-                pieces.append((act * tail_e[:, lanes]).astype(BF))
-            if c == 4:
-                b_low = act.astype(BF)
-        fresh = mm_tn(b_low, jnp.concatenate(pieces, axis=1))
-        states[b + 1] = keep_e * states[b] + fresh
-        return carry
-
-    lax.fori_loop(0, 7, forward, 0)
-    r7 = slice(7 * Q, 8 * Q)
-    for c in range(6):
-        lanes = slice(c * 128, c * 128 + 128)
-        pre = pre_r[r7, lanes]
-        acts[r7, lanes] = pre * sigmoid(pre)
-    for copy in sib_in:
-        copy.wait_recv()
-
-    def merge(c, carry):
-        for mine, theirs, at in ((gz, sz, 0), (go, so, 512)):
-            chunk[c, :, at : at + 512] = (mine[c, core].astype(F32) + theirs[c].astype(F32)).astype(BF)
-        return carry
-
-    lax.fori_loop(0, 8, merge, 0)
-    grads_in = [links.copy(chunk.at[chips[k]], rg.at[k - 1], others[k]) for k in range(1, 8)]
-    carry_in.wait_recv()
-    grad[...] = jnp.where(context == 0, g_in[...].astype(F32), 0.0)
-    heads[...] = jnp.zeros_like(heads)
-    dpre[0:8] = jnp.zeros((8, 768), F32)
-    dpre[1032:1040] = jnp.zeros((8, 768), F32)
-
-    def backward(i, carry):
-        b = 7 - i
-        r = pl.ds(pl.multiple_of(b * Q, Q), Q)
-        rp = pl.ds(pl.multiple_of(b * Q + 8, 8), Q)
-        marks = colm[r]
-        raw = dtr[r] + dtb[...]
-        dt = softplus(raw)
-        cum = mm3_left(lower, dt * a_neg)
-        cum_t = cum.T
-        last = cum[Q - 1 : Q]
-        enter = jnp.exp(cum) * marks[:, 5:6]
-        tail = jnp.exp(last - cum) * marks[:, 6:7]
-        dt_e = mm2(dt, expand)
-        enter_e = mm2(enter, expand)
-        tail_e = mm2(tail, expand)
-        keep_e = enter_e[Q - 1 : Q]
-        b_low = acts[r, 512:640].astype(BF)
-        c_low = acts[r, 640:768].astype(BF)
-        state = states[b]
-        state_low = state.astype(BF)
-        g_now = grad[...]
-        g_low = g_now.astype(BF)
-        inter = mm(c_low, state_low)
-        back = mm(b_low, g_low)
-        mask = causal & (marks[:, 0:1] == seg[pl.ds(b, 1), :].astype(F32))
-        scores = jnp.where(mask, mm_nt(c_low, b_low), 0.0)
-        kept = jnp.sum(state * g_now, axis=0, keepdims=True) * keep_e
-        entered, tailed, e_terms, q_terms, x_terms, k_terms = [], [], [], [], [], []
-        rows, cols = [], []
-        d_scores = jnp.zeros((Q, Q), F32)
-        for p in range(4):
-            lanes = slice(p * 128, p * 128 + 128)
-            x = acts[r, lanes]
-            dys = dy[r, lanes]
-            xdt = x * dt_e[:, lanes]
-            xdt_low = xdt.astype(BF)
-            ed = enter_e[:, lanes] * dys
-            tx = tail_e[:, lanes] * xdt
-            entered.append(ed.astype(BF))
-            tailed.append(tx.astype(BF))
-            dy_two = halves(dys.astype(BF))
-            dw_two = mm_nt(dy_two, xdt_low)
-            ws = []
-            for k in range(2):
-                h = 2 * p + k
-                decay = jnp.exp(jnp.minimum(cum[:, h : h + 1] - cum_t[h : h + 1, :], 0.0))
-                weight = decay * scores
-                dw = dw_two[k * Q : k * Q + Q]
-                d_scores = d_scores + decay * dw
-                both = weight * dw
-                rows.append(jnp.sum(both, axis=1, keepdims=True))
-                cols.append(jnp.sum(both, axis=0, keepdims=True))
-                ws.append(weight.astype(BF))
-            dxdt = mm_tn(jnp.concatenate(ws, axis=0), dy_two) + tail_e[:, lanes] * back[:, lanes]
-            e_terms.append(ed * inter[:, lanes] - tx * back[:, lanes])
-            q_terms.append(jnp.sum(tx * back[:, lanes], axis=0, keepdims=True) + kept[:, lanes])
-            x_terms.append(dxdt * x)
-            k_terms.append(jnp.sum(dys * x, axis=0, keepdims=True))
-            pre = pre_r[r, lanes]
-            sig = sigmoid(pre)
-            dpre[rp, lanes] = (dxdt * dt_e[:, lanes] + dsk_e[:, lanes] * dys) * (sig * (1.0 + pre * (1.0 - sig)))
-        entered = jnp.concatenate(entered, axis=1)
-        tailed = jnp.concatenate(tailed, axis=1)
-        ds_low = jnp.where(mask, d_scores, 0.0).astype(BF)
-        d_c = mm_nt(entered, state_low) + mm(ds_low, b_low)
-        d_b = mm_nt(tailed, g_low) + mm_tn(ds_low, c_low)
-        grad[...] = keep_e * g_now + mm_tn(c_low, entered)
-        for c, value in ((4, d_b), (5, d_c)):
-            lanes = slice(c * 128, c * 128 + 128)
-            pre = pre_r[r, lanes]
-            sig = sigmoid(pre)
-            dpre[rp, lanes] = value * (sig * (1.0 + pre * (1.0 - sig)))
-        d_cum = jnp.concatenate(rows, axis=1) - jnp.concatenate(cols, axis=0).T
-        d_cum = d_cum + head_sum(jnp.concatenate(e_terms, axis=1))
-        d_log = mm3_left(upper, d_cum) + head_sum(jnp.concatenate(q_terms, axis=1))
-        d_dt = d_log * a_neg + head_sum(jnp.concatenate(x_terms, axis=1))
-        d_raw = d_dt * sigmoid(raw)
-        ddt_o[r] = jnp.concatenate([d_raw, jnp.zeros((Q, 120), F32)], axis=1).astype(BF)
-        heads[0:1] += jnp.sum(d_raw, axis=0, keepdims=True)
-        heads[1:2] += jnp.sum(d_log * dt, axis=0, keepdims=True) * a_neg
-        heads[2:3] += head_sum(jnp.concatenate(k_terms, axis=1))
-        return carry
-
-    lax.fori_loop(0, 1, backward, 0)
-    ring.reduce_second(branch, near, relay, from_d, from_u)
-    lax.fori_loop(1, 4, backward, 0)
-    fetch.wait()
-    ring.reduce_wait()
-
-    def finish_out(i, carry):
-        r = pl.ds(pl.multiple_of(i * 64, 64), 64)
-        rt = pl.ds(pl.multiple_of(tensor * 256 + i * 64, 64), 64)
-        total = branch[rt].astype(F32) + from_d[r].astype(F32) + from_u[r].astype(F32)
-        out_o[rt] = (tok_r[r].astype(F32) + total).astype(BF)
-        return carry
-
-    lax.fori_loop(0, 4, finish_out, 0)
-    ring.gather_first(out_o)
-    lax.fori_loop(4, 8, backward, 0)
-    small_o[...] = jnp.zeros_like(small_o)
-    small_o[24:32, 0:8] = heads[...]
-
-    for c in range(6):
-        lanes = slice(c * 128, c * 128 + 128)
-        first = dpre[0:16, lanes]
-        cw, wl = (cwx, lanes) if c < 4 else (cwb, slice(c * 128 - 512, c * 128 - 384))
-        flags = jnp.concatenate([jnp.zeros((8, 8), F32), colm[0:8]], axis=0)
-        total = jnp.zeros((8, 128), F32)
-        for d in range(1, 4):
-            total = total + cw[3 - d : 4 - d, wl] * (first * flags[:, d : d + 1])[d : d + 8]
-        ret_s[:, lanes] = total
-    ret_in = links.copy(ret_s, ret_r, partner)
-    ring.gather_second(out_o)
-    for copy in grads_in:
-        copy.wait_recv()
-    for at in range(0, 1024, 128):
-        lanes = slice(at, at + 128)
-        cs[:, lanes] = add_slots(chunk[chip, :, lanes].astype(F32), rg, lanes).astype(BF)
-    grads_ctx = links.copy(cs, cr, partner)
-    for c in range(6):
-        lanes = slice(c * 128, c * 128 + 128)
-        cw, wl = (cwx, lanes) if c < 4 else (cwb, slice(c * 128 - 512, c * 128 - 384))
-
-        def conv(b, sums, lanes=lanes, c=c, cw=cw, wl=wl):
-            r = pl.ds(pl.multiple_of(b * Q, Q), Q)
-            slab = dpre[pl.ds(pl.multiple_of(b * Q + 8, 8), Q + 8), lanes]
-            marks = colm[pl.ds(pl.multiple_of(b * Q, Q), Q + 8)]
-            xin = xbc[pl.ds(pl.multiple_of(b * Q, Q), Q + EDGE), lanes].astype(F32)
-            main = slab[0:Q]
-            out = cw[3:4, wl] * main
-            new = [sums[0] + jnp.sum(main, axis=0, keepdims=True),
-                   sums[1] + jnp.sum(main * xin[EDGE:], axis=0, keepdims=True)]
-            for d in range(1, 4):
-                masked = slab * marks[:, d : d + 1]
-                out = out + cw[3 - d : 4 - d, wl] * masked[d : d + Q]
-                new.append(sums[d + 1] + jnp.sum(masked[0:Q] * xin[EDGE - d : Q + EDGE - d], axis=0, keepdims=True))
-            if c < 4:
-                dx_o[r, lanes] = out.astype(BF)
-            else:
-                dbc_o[r, slice(c * 128 - 512, c * 128 - 384)] = out.astype(BF)
-
-            @pl.when(b == 7)
-            def _():
-                tail_r[:, lanes] = out[Q - EDGE :]
-
-            return tuple(new)
-
-        zero = jnp.zeros((1, 128), F32)
-        sums = lax.fori_loop(0, 8, conv, (zero,) * 5)
-        at = 16 + c if c < 4 else 36 + c
-        small_o[at : at + 1] = sums[0]
-        for d in range(4):
-            at = (3 - d) * 4 + c if c < 4 else 28 + (3 - d) * 2 + c
-            small_o[at : at + 1] = sums[d + 1]
-    ret_in.wait_recv()
-    returned = jnp.where(context == 0, ret_r[...], 0.0)
-    last = tail_r[...] + jnp.concatenate([jnp.zeros((EDGE - 8, 768), F32), returned], axis=0)
-    dx_o[1024 - EDGE : 1024] = last[:, 0:512].astype(BF)
-    dbc_o[1024 - EDGE : 1024] = last[:, 512:768].astype(BF)
-    grads_ctx.wait_recv()
-    oz[...] = cs[:, 0:512].astype(F32) + cr[:, 0:512].astype(F32)
-    oo[...] = cs[:, 512:1024].astype(F32) + cr[:, 512:1024].astype(F32)
-    ring.gather_wait(out_o)
-    links.finish()
 
 
 MESH = pl.DeviceIdType.MESH
@@ -506,10 +266,13 @@
             self.copy(i).wait_send()
 
 
-def forward_kernel(
+def main_kernel(
     wz, wx, wbc, wdt, norm, wo, tok, cot, seg, cwx, cwb, cbx, cbb, dtb, alog, dsk, gg, ex, ext,
-    in_o, zo_o, xn_o, xbc_o, pre_o, dtr_o, colm_o, gain_o, st_o, dy_o, dz_o, branch_o, carry_o, gate_o, gz_o, go_o,
-    mine1, mine2, etok_b, eseg, xs, st, st_low, st_in, y_s, er_s, c_s, z_s, dn_s, row_s, row_r, yn_o, send, recv,
+    in_o, zo_o, xn_o, gain_o, dz_o, gate_o, dx_o, dbc_o, ddt_o, small_o, out_o, oz, oo,
+    mine1, mine2, etok_b, eseg, xs, st, st_low, st_in, y_s, er_s, c_s, z_s, dn_s, row_s, row_r, yn_o,
+    xbc_o, pre_o, dtr_o, colm_o, st_o, dy_o, branch_o, carry_o, gz_o, go_o,
+    acts, grad, heads, g_in, tail_r, ret_s, ret_r, near, relay, from_d, from_u,
+    sz, so, chunk, rg, cs, cr, send, recv,
 ):
     shard, context, tensor, core, chip, chips, sibling, others, partner, ranks, group, at = places()
     mine1[:, 0:512] = wx[...]
@@ -694,10 +457,234 @@
 
     lax.fori_loop(0, 8, finish, 0)
     carry_o[...] = st[...].astype(BF)
+    carry_in = links.copy(carry_o, g_in, partner)
+    ring = Ring(links, tensor, group)
+    ring.reduce_first(branch_o, near, from_d, from_u)
     for m in range(8):
         lanes = slice(m * 128, m * 128 + 128)
         gz_o[m] = mm_tn(xn_o[:, lanes], dz_o[...]).astype(BF).reshape(2, 64, 512)
         go_o[m] = mm_tn(cot[:, lanes], yn_o[...]).astype(BF).reshape(2, 64, 512)
+    sib_in = (links.copy(gz_o.at[:, 1 - core], sz, sibling), links.copy(go_o.at[:, 1 - core], so, sibling))
+    a_neg = -jnp.exp(alog[...])
+    causal, anti = triangles()
+    lower = as_low(causal)
+    upper = as_low(anti)
+    expand = ex[...]
+    expand_t = ext[...]
+    dsk_e = mm2(dsk[...], expand)
+
+    def head_sum(v):
+        return mm2(v, expand_t)
+
+    y_s[0:Q] = st_o[...]
+
+    def forward(b, carry):
+        r = pl.ds(pl.multiple_of(b * Q, Q), Q)
+        marks = colm_o[r]
+        dt = softplus(dtr_o[r] + dtb[...])
+        cum = mm3_left(lower, dt * a_neg)
+        last = cum[Q - 1 : Q]
+        tail = jnp.exp(last - cum) * marks[:, 6:7] * dt
+        keep_e = mm2(jnp.exp(last) * marks[Q - 1 : Q, 5:6], expand)
+        tail_e = mm2(tail, expand)
+        pieces = []
+        for c in range(6):
+            lanes = slice(c * 128, c * 128 + 128)
+            pre = pre_o[r, lanes]
+            act = pre * sigmoid(pre)
+            acts[r, lanes] = act
+            if c < 4:
+                pieces.append((act * tail_e[:, lanes]).astype(BF))
+            if c == 4:
+                b_low = act.astype(BF)
+        fresh = mm_tn(b_low, jnp.concatenate(pieces, axis=1))
+        y_s[pl.ds(pl.multiple_of(b * Q + Q, Q), Q)] = keep_e * y_s[r] + fresh
+        return carry
+
+    lax.fori_loop(0, 7, forward, 0)
+    r7 = slice(7 * Q, 8 * Q)
+    for c in range(6):
+        lanes = slice(c * 128, c * 128 + 128)
+        pre = pre_o[r7, lanes]
+        acts[r7, lanes] = pre * sigmoid(pre)
+    for copy in sib_in:
+        copy.wait_recv()
+
+    def merge(c, carry):
+        for mine, theirs, at in ((gz_o, sz, 0), (go_o, so, 512)):
+            chunk[c, :, at : at + 512] = (mine[c, core].astype(F32) + theirs[c].astype(F32)).astype(BF)
+        return carry
+
+    lax.fori_loop(0, 8, merge, 0)
+    grads_in = [links.copy(chunk.at[chips[k]], rg.at[k - 1], others[k]) for k in range(1, 8)]
+    carry_in.wait_recv()
+    grad[...] = jnp.where(context == 0, g_in[...].astype(F32), 0.0)
+    heads[...] = jnp.zeros_like(heads)
+    xs[0:8] = jnp.zeros((8, 768), F32)
+    xs[1032:1040] = jnp.zeros((8, 768), F32)
+
+    def backward(i, carry):
+        b = 7 - i
+        r = pl.ds(pl.multiple_of(b * Q, Q), Q)
+        rp = pl.ds(pl.multiple_of(b * Q + 8, 8), Q)
+        marks = colm_o[r]
+        raw = dtr_o[r] + dtb[...]
+        dt = softplus(raw)
+        cum = mm3_left(lower, dt * a_neg)
+        cum_t = cum.T
+        last = cum[Q - 1 : Q]
+        enter = jnp.exp(cum) * marks[:, 5:6]
+        tail = jnp.exp(last - cum) * marks[:, 6:7]
+        dt_e = mm2(dt, expand)
+        enter_e = mm2(enter, expand)
+        tail_e = mm2(tail, expand)
+        keep_e = enter_e[Q - 1 : Q]
+        b_low = acts[r, 512:640].astype(BF)
+        c_low = acts[r, 640:768].astype(BF)
+        state = y_s[r]
+        state_low = state.astype(BF)
+        g_now = grad[...]
+        g_low = g_now.astype(BF)
+        inter = mm(c_low, state_low)
+        back = mm(b_low, g_low)
+        mask = causal & (marks[:, 0:1] == seg[pl.ds(b, 1), :].astype(F32))
+        scores = jnp.where(mask, mm_nt(c_low, b_low), 0.0)
+        kept = jnp.sum(state * g_now, axis=0, keepdims=True) * keep_e
+        entered, tailed, e_terms, q_terms, x_terms, k_terms = [], [], [], [], [], []
+        rows, cols = [], []
+        d_scores = jnp.zeros((Q, Q), F32)
+        for p in range(4):
+            lanes = slice(p * 128, p * 128 + 128)
+            x = acts[r, lanes]
+            dys = dy_o[r, lanes]
+            xdt = x * dt_e[:, lanes]
+            xdt_low = xdt.astype(BF)
+            ed = enter_e[:, lanes] * dys
+            tx = tail_e[:, lanes] * xdt
+            entered.append(ed.astype(BF))
+            tailed.append(tx.astype(BF))
+            dy_two = halves(dys.astype(BF))
+            dw_two = mm_nt(dy_two, xdt_low)
+            ws = []
+            for k in range(2):
+                h = 2 * p + k
+                decay = jnp.exp(jnp.minimum(cum[:, h : h + 1] - cum_t[h : h + 1, :], 0.0))
+                weight = decay * scores
+                dw = dw_two[k * Q : k * Q + Q]
+                d_scores = d_scores + decay * dw
+                both = weight * dw
+                rows.append(jnp.sum(both, axis=1, keepdims=True))
+                cols.append(jnp.sum(both, axis=0, keepdims=True))
+                ws.append(weight.astype(BF))
+            dxdt = mm_tn(jnp.concatenate(ws, axis=0), dy_two) + tail_e[:, lanes] * back[:, lanes]
+            e_terms.append(ed * inter[:, lanes] - tx * back[:, lanes])
+            q_terms.append(jnp.sum(tx * back[:, lanes], axis=0, keepdims=True) + kept[:, lanes])
+            x_terms.append(dxdt * x)
+            k_terms.append(jnp.sum(dys * x, axis=0, keepdims=True))
+            pre = pre_o[r, lanes]
+            sig = sigmoid(pre)
+            xs[rp, lanes] = (dxdt * dt_e[:, lanes] + dsk_e[:, lanes] * dys) * (sig * (1.0 + pre * (1.0 - sig)))
+        entered = jnp.concatenate(entered, axis=1)
+        tailed = jnp.concatenate(tailed, axis=1)
+        ds_low = jnp.where(mask, d_scores, 0.0).astype(BF)
+        d_c = mm_nt(entered, state_low) + mm(ds_low, b_low)
+        d_b = mm_nt(tailed, g_low) + mm_tn(ds_low, c_low)
+        grad[...] = keep_e * g_now + mm_tn(c_low, entered)
+        for c, value in ((4, d_b), (5, d_c)):
+            lanes = slice(c * 128, c * 128 + 128)
+            pre = pre_o[r, lanes]
+            sig = sigmoid(pre)
+            xs[rp, lanes] = value * (sig * (1.0 + pre * (1.0 - sig)))
+        d_cum = jnp.concatenate(rows, axis=1) - jnp.concatenate(cols, axis=0).T
+        d_cum = d_cum + head_sum(jnp.concatenate(e_terms, axis=1))
+        d_log = mm3_left(upper, d_cum) + head_sum(jnp.concatenate(q_terms, axis=1))
+        d_dt = d_log * a_neg + head_sum(jnp.concatenate(x_terms, axis=1))
+        d_raw = d_dt * sigmoid(raw)
+        ddt_o[r] = jnp.concatenate([d_raw, jnp.zeros((Q, 120), F32)], axis=1).astype(BF)
+        heads[0:1] += jnp.sum(d_raw, axis=0, keepdims=True)
+        heads[1:2] += jnp.sum(d_log * dt, axis=0, keepdims=True) * a_neg
+        heads[2:3] += head_sum(jnp.concatenate(k_terms, axis=1))
+        return carry
+
+    lax.fori_loop(0, 1, backward, 0)
+    ring.reduce_second(branch_o, near, relay, from_d, from_u)
+    lax.fori_loop(1, 4, backward, 0)
+    ring.reduce_wait()
+
+    def finish_out(i, carry):
+        r = pl.ds(pl.multiple_of(i * 64, 64), 64)
+        rt = pl.ds(pl.multiple_of(tensor * 256 + i * 64, 64), 64)
+        total = branch_o[rt].astype(F32) + from_d[r].astype(F32) + from_u[r].astype(F32)
+        out_o[rt] = (tok[rt].astype(F32) + total).astype(BF)
+        return carry
+
+    lax.fori_loop(0, 4, finish_out, 0)
+    ring.gather_first(out_o)
+    lax.fori_loop(4, 8, backward, 0)
+    small_o[...] = jnp.zeros_like(small_o)
+    small_o[24:32, 0:8] = heads[...]
+
+    for c in range(6):
+        lanes = slice(c * 128, c * 128 + 128)
+        first = xs[0:16, lanes]
+        cw, wl = (cwx, lanes) if c < 4 else (cwb, slice(c * 128 - 512, c * 128 - 384))
+        flags = jnp.concatenate([jnp.zeros((8, 8), F32), colm_o[0:8]], axis=0)
+        total = jnp.zeros((8, 128), F32)
+        for d in range(1, 4):
+            total = total + cw[3 - d : 4 - d, wl] * (first * flags[:, d : d + 1])[d : d + 8]
+        ret_s[:, lanes] = total
+    ret_in = links.copy(ret_s, ret_r, partner)
+    ring.gather_second(out_o)
+    for copy in grads_in:
+        copy.wait_recv()
+    for at in range(0, 1024, 128):
+        lanes = slice(at, at + 128)
+        cs[:, lanes] = add_slots(chunk[chip, :, lanes].astype(F32), rg, lanes).astype(BF)
+    grads_ctx = links.copy(cs, cr, partner)
+    for c in range(6):
+        lanes = slice(c * 128, c * 128 + 128)
+        cw, wl = (cwx, lanes) if c < 4 else (cwb, slice(c * 128 - 512, c * 128 - 384))
+
+        def conv(b, sums, lanes=lanes, c=c, cw=cw, wl=wl):
+            r = pl.ds(pl.multiple_of(b * Q, Q), Q)
+            slab = xs[pl.ds(pl.multiple_of(b * Q + 8, 8), Q + 8), lanes]
+            marks = colm_o[pl.ds(pl.multiple_of(b * Q, Q), Q + 8)]
+            xin = xbc_o[pl.ds(pl.multiple_of(b * Q, Q), Q + EDGE), lanes].astype(F32)
+            main = slab[0:Q]
+            out = cw[3:4, wl] * main
+            new = [sums[0] + jnp.sum(main, axis=0, keepdims=True),
+                   sums[1] + jnp.sum(main * xin[EDGE:], axis=0, keepdims=True)]
+            for d in range(1, 4):
+                masked = slab * marks[:, d : d + 1]
+                out = out + cw[3 - d : 4 - d, wl] * masked[d : d + Q]
+                new.append(sums[d + 1] + jnp.sum(masked[0:Q] * xin[EDGE - d : Q + EDGE - d], axis=0, keepdims=True))
+            if c < 4:
+                dx_o[r, lanes] = out.astype(BF)
+            else:
+                dbc_o[r, slice(c * 128 - 512, c * 128 - 384)] = out.astype(BF)
+
+            @pl.when(b == 7)
+            def _():
+                tail_r[:, lanes] = out[Q - EDGE :]
+
+            return tuple(new)
+
+        zero = jnp.zeros((1, 128), F32)
+        sums = lax.fori_loop(0, 8, conv, (zero,) * 5)
+        at = 16 + c if c < 4 else 36 + c
+        small_o[at : at + 1] = sums[0]
+        for d in range(4):
+            at = (3 - d) * 4 + c if c < 4 else 28 + (3 - d) * 2 + c
+            small_o[at : at + 1] = sums[d + 1]
+    ret_in.wait_recv()
+    returned = jnp.where(context == 0, ret_r[...], 0.0)
+    last = tail_r[...] + jnp.concatenate([jnp.zeros((EDGE - 8, 768), F32), returned], axis=0)
+    dx_o[1024 - EDGE : 1024] = last[:, 0:512].astype(BF)
+    dbc_o[1024 - EDGE : 1024] = last[:, 512:768].astype(BF)
+    grads_ctx.wait_recv()
+    oz[...] = cs[:, 0:512].astype(F32) + cr[:, 0:512].astype(F32)
+    oo[...] = cs[:, 512:1024].astype(F32) + cr[:, 512:1024].astype(F32)
+    ring.gather_wait(out_o)
     links.finish()
     spread1.sent()
     spread2.sent()
@@ -905,35 +892,28 @@
     state = (STATE, inner_width)
     grid = (8, 2, 64, 512)
     heads = (dt_bias[None], a_log[None], d_skip[None])
-    (w_in, w_zo, x_normed, xbc, pre, dt_raw, colm, gain_row, state_in, d_y, d_z, branch_part, d_carry, g_gate_gain, g_w_z, g_w_out) = call(
-        forward_kernel,
-        [((1024, 896), BF), ((1024, 1024), BF), ((length, 1024), BF), ((length + EDGE, 768), BF), ((length, 768), F32), ((length, 8), F32),
-         ((length + 8, 8), F32), ((1, 1024), F32), (state, F32), (wide, F32), (wide, BF), ((length, 1024), BF), (state, BF), ((4, 128), F32), (grid, BF), (grid, BF)],
+    own = (64, 512)
+    half = ((2, 128, 1024), BF)
+    rows = ((256, 1024), BF)
+
+    def vector(shape, last):
+        return [(s, F32) for s in (shape, shape, (8,) + shape, shape, shape, last)]
+
+    (w_in, w_zo, x_normed, gain_row, d_z, g_gate_gain, d_x_low, d_bc, d_dt_low, small, output, o_z, o_out) = call(
+        main_kernel,
+        [((1024, 896), BF), ((1024, 1024), BF), ((length, 1024), BF), ((1, 1024), F32), (wide, BF), ((4, 128), F32),
+         (wide, BF), ((length, 2 * STATE), BF), ((length, 128), BF), ((48, 128), F32), ((length, 1024), BF), (own, F32), (own, F32)],
         [((64, 896), BF), ((64, 1024), BF), ((EDGE, 1024), BF), ((8, 128), jnp.int32), ((length + EDGE, 768), F32), (state, F32), (state, BF), (state, BF),
          (wide, F32), ((length, 8), F32), ((length, STATE), BF), (wide, F32), (wide, F32), ((8, 8, 128), F32), ((3, 8, 8, 128), F32), (wide, BF),
-         ((48,), None), ((48,), None)],
+         ((length + EDGE, 768), BF), ((length, 768), F32), ((length, 8), F32), ((length + 8, 8), F32), (state, F32), (wide, F32),
+         ((length, 1024), BF), (state, BF), (grid, BF), (grid, BF),
+         ((length, 768), F32), (state, F32), ((8, 8), F32),
+         (state, BF), ((EDGE, 768), F32), ((8, 768), F32), ((8, 768), F32), half, half, rows, rows,
+         ((8, 64, 512), BF), ((8, 64, 512), BF), ((8, 64, 1024), BF), ((7, 64, 1024), BF), ((64, 1024), BF), ((64, 1024), BF),
+         ((72,), None), ((72,), None)],
         w_z, w_x, w_bc, w_dt, norm_gain[None], w_out, tokens, cotangent, seg,
         conv_x, conv_bc, conv_xb[None], conv_bcb[None], *heads, gate_gain[None], expand, expand_t,
         collective_id=1,
-    )
-    own = (64, 512)
-
-    def vector(shape, last):
-        return [(s, F32) for s in (shape, shape, (8,) + shape, shape, shape, last)]
-
-    half = ((2, 128, 1024), BF)
-    rows = ((256, 1024), BF)
-    d_x_low, d_bc, d_dt_low, small, output, o_z, o_out = call(
-        back_kernel,
-        [(wide, BF), ((length, 2 * STATE), BF), ((length, 128), BF), ((48, 128), F32), ((length, 1024), BF), (own, F32), (own, F32)],
-        [((8, STATE, inner_width), F32), ((length, 768), F32), ((length + 16, 768), F32), (state, F32), ((8, 8), F32),
-         (state, BF), ((EDGE, 768), F32), ((8, 768), F32), ((8, 768), F32),
-         half, half, rows, rows, rows,
-         ((8, 64, 512), BF), ((8, 64, 512), BF), ((8, 64, 1024), BF), ((7, 64, 1024), BF), ((64, 1024), BF), ((64, 1024), BF),
-         ((32,), None), ((32,), None), ((1,), None)],
-        d_y, colm, seg, xbc, pre, dt_raw, state_in, d_carry, conv_x, conv_bc, *heads, expand, expand_t,
-        branch_part, g_w_z, g_w_out, tokens,
-        specs=(18,), collective_id=3,
     )
     d_tokens, o_x, o_dt, o_bc, o_norm, conv_o, convb_o, cbc_o, cbcb_o, gate_o, dtb_o, alog_o, dsk_o = call(
         tail_kernel,

time: 184 us -> 169 us (0.918)
  Pallas kernels: 169 us -> 154 us
    pallas_call x3 -> x2, Pallas kernels: 169 us -> 154 us  [call(): pl.pallas_call(kernel, out_shape=[jax.ShapeDtypeStruct(s, d) for s, d in...]
where the time goes in v6:
time: 169 us
  Pallas kernels  154 us (91%)
  local copies, waits for them, and re-layouts  14.1 us (8%)
    pallas_call x2, Pallas kernels, call(): pl.pallas_call(kernel, out_shape=[jax.ShapeDtypeStruct(s, d) for s, d in...  154 us
    unnamed x47, local copies, waits for them, and re-layouts  14.1 us

profile of v6, /device:TPU:1, one launch (start us, length us, event | category | flops | bytes accessed | tf_op | source)
XLA Modules:
  0.0 168.9 jit_solution(16942430102084067835)
XLA Ops:
  0.6 1.4 copy.35.wdt
  2.0 100.9 %shard_map.306 = (bf16[1024,896]{1,0:T(8,128)(2,1)}, bf16[1024,1024]{1,0:T(8,128)(2,1)}, bf16[1024,1024]{1,0:T(8,128)(2,1)}, f32[1,1024]{1,0:T(1,128)}, bf16[102...) custom-call(bf16[64,512]{1,0:T(8,128)(2,1)} %wz.1, ...), custom_call_target="tpu_custom_call" | custom-call | tf_op jit(solution)/shard_map/pallas_call | solution.py:853
  102.9 0.0 copy-start
  102.9 53.2 %shard_map.307 = (bf16[1024,1024]{1,0:T(8,128)(2,1)}, f32[64,512]{1,0:T(8,128)}, f32[64,8]{1,0:T(8,128)}, f32[64,256]{1,0:T(8,128)}, f32[1,64]{1,0:T(1,128)}, /*...) custom-call(bf16[1024,512]{1,0:T(8,128)(2,1)} %get-tuple-element.43., ...), custom_call_target="tpu_custom_call" | custom-call | tf_op jit(solution)/shard_map/pallas_call | solution.py:853
  156.1 1.4 copy.36
  157.6 0.0 copy-done
  157.6 1.3 copy.52
  158.9 1.0 copy-done.1
  159.9 0.0 copy-start.6
  160.0 1.3 copy.53
  161.3 0.5 copy.54
  161.9 0.7 copy.55
  162.5 0.7 copy.56
  163.2 0.6 copy.57
  163.8 0.6 copy.58
  164.4 0.6 copy.59
  165.0 0.6 copy.60
  165.6 0.0 copy-done.10
  165.6 0.6 copy.61
  166.2 0.5 copy.62
  166.7 0.5 copy.63
  167.2 0.5 copy.64
  167.7 0.6 copy.65
  168.3 0.7 copy.66
  (25 shorter events, 0.0 us)
Async XLA Ops:
  102.9 54.6 %copy-start = (bf16[1024,1024]{1,0:T(8,128)(2,1)S(1)}, bf16[1024,1024]{1,0:T(8,128)(2,1)}, u32[]{:S(2)}) copy-start(bf16[1024,1024]{1,0:T(8,128)(2,1)} %get-tuple-element.100) | copy-start | bytes 6291460
  157.6 2.3 %copy-start.1 = (bf16[1024,1024]{1,0:T(8,128)(2,1)S(1)}, bf16[1024,1024]{1,0:T(8,128)(2,1)}, u32[]{:S(2)}) copy-start(bf16[1024,1024]{1,0:T(8,128)(2,1)} %get-tuple-element.101) | copy-start | bytes 6291460
  159.9 1.4 copy-start.14
  159.9 1.9 %copy-start.3 = (f32[64,512]{1,0:T(8,128)S(1)}, f32[64,512]{1,0:T(8,128)}, u32[]{:S(2)}) copy-start(f32[64,512]{1,0:T(8,128)} %get-tuple-element.103) | copy-start | bytes 393220
  159.9 2.6 %copy-start.4 = (f32[64,512]{1,0:T(8,128)S(1)}, f32[64,512]{1,0:T(8,128)}, u32[]{:S(2)}) copy-start(f32[64,512]{1,0:T(8,128)} %get-tuple-element.104) | copy-start | bytes 393220
  159.9 3.3 %copy-start.5 = (f32[64,256]{1,0:T(8,128)S(1)}, f32[64,256]{1,0:T(8,128)}, u32[]{:S(2)}) copy-start(f32[64,256]{1,0:T(8,128)} %get-tuple-element.106) | copy-start | bytes 196612
  159.9 3.9 %copy-start.6 = (f32[4,512]{1,0:T(4,128)S(1)}, f32[4,512]{1,0:T(4,128)}, u32[]{:S(2)}) copy-start(f32[4,512]{1,0:T(4,128)} %get-tuple-element.107) | copy-start | bytes 24580
  159.9 4.5 %copy-start.9 = (f32[1,512]{1,0:T(1,128)S(1)}, f32[1,512]{1,0:T(1,128)}, u32[]{:S(2)}) copy-start(f32[1,512]{1,0:T(1,128)} %get-tuple-element.60) | copy-start | bytes 6148
  159.9 5.0 %copy-start.7 = (f32[4,256]{1,0:T(4,128)S(1)}, f32[4,256]{1,0:T(4,128)}, u32[]{:S(2)}) copy-start(f32[4,256]{1,0:T(4,128)} %get-tuple-element.109) | copy-start | bytes 12292
  160.0 5.6 %copy-start.10 = (f32[1,256]{1,0:T(1,128)S(1)}, f32[1,256]{1,0:T(1,128)}, u32[]{:S(2)}) copy-start(f32[1,256]{1,0:T(1,128)} %get-tuple-element.62) | copy-start | bytes 3076
  160.0 6.2 %copy-start.13 = (f32[1,8]{1,0:T(1,128)S(1)}, f32[1,8]{1,0:T(1,128)}, u32[]{:S(2)}) copy-start(f32[1,8]{1,0:T(1,128)} %get-tuple-element.63) | copy-start | bytes 100
  160.0 6.7 %copy-start.12 = (f32[1,8]{1,0:T(1,128)S(1)}, f32[1,8]{1,0:T(1,128)}, u32[]{:S(2)}) copy-start(f32[1,8]{1,0:T(1,128)} %get-tuple-element.64) | copy-start | bytes 100
  160.0 7.2 %copy-start.11 = (f32[1,8]{1,0:T(1,128)S(1)}, f32[1,8]{1,0:T(1,128)}, u32[]{:S(2)}) copy-start(f32[1,8]{1,0:T(1,128)} %get-tuple-element.65) | copy-start | bytes 100
  160.0 7.7 %copy-start.8 = (f32[1,512]{1,0:T(1,128)S(1)}, f32[1,512]{1,0:T(1,128)}, u32[]{:S(2)}) copy-start(f32[1,512]{1,0:T(1,128)} %get-tuple-element.66) | copy-start | bytes 6148
  160.0 8.3 %copy-start.2 = (f32[64,512]{1,0:T(8,128)S(1)}, f32[64,512]{1,0:T(8,128)}, u32[]{:S(2)}) copy-start(f32[64,512]{1,0:T(8,128)} %get-tuple-element.115) | copy-start | bytes 393220

commit v7 on v6

--- a/solution.py
+++ b/solution.py
@@ -21,7 +21,7 @@
 BF = jnp.bfloat16
 Q = 128
 EDGE = 16
-VMEM_LIMIT = 58 * 1024 * 1024
+VMEM_LIMIT = 60 * 1024 * 1024
 
 
 def mm(a, b):
@@ -266,13 +266,22 @@
             self.copy(i).wait_send()
 
 
+def add_slots(total, slots, lanes):
+    for k in range(7):
+        total = total + slots[k, :, lanes].astype(F32)
+    return total
+
+
 def main_kernel(
     wz, wx, wbc, wdt, norm, wo, tok, cot, seg, cwx, cwb, cbx, cbb, dtb, alog, dsk, gg, ex, ext,
-    in_o, zo_o, xn_o, gain_o, dz_o, gate_o, dx_o, dbc_o, ddt_o, small_o, out_o, oz, oo,
-    mine1, mine2, etok_b, eseg, xs, st, st_low, st_in, y_s, er_s, c_s, z_s, dn_s, row_s, row_r, yn_o,
+    out_o, oz, oo, dtok_o, ox, odt, obc, onorm, conv_o, convb_o, bc_o, bcb_o, ggate_o, dtb_o, alog_o, dsk_o,
+    in_o, zo_o, xn_o, gain_o, dz_o, gate_o, dx_o, dbc_o, ddt_o, small_o,
+    mine1, mine2, etok_b, eseg, xs, st, st_low, st_in, y_s, er_s, c_s, row_s, row_r, yn_o,
     xbc_o, pre_o, dtr_o, colm_o, st_o, dy_o, branch_o, carry_o, gz_o, go_o,
     acts, grad, heads, g_in, tail_r, ret_s, ret_r, near, relay, from_d, from_u,
-    sz, so, chunk, rg, cs, cr, send, recv,
+    sz, so, chunk, rg, cs, cr,
+    gx, near2, relay2, from_d2, from_u2, sx, chunk2, rg2, cs2, cr2, t2,
+    sm, sm_s, sm_c, sm_x, sm_r, sm_t, nm, nm_s, nm_c, nm_x, nm_r, nm_t, send, recv,
 ):
     shard, context, tensor, core, chip, chips, sibling, others, partner, ranks, group, at = places()
     mine1[:, 0:512] = wx[...]
@@ -400,8 +409,8 @@
 
     def project(b, carry):
         r = pl.ds(pl.multiple_of(b * Q, Q), Q)
-        z_s[r] = mm(xn_o[r], zo_o[:, 0:512])
-        dn_s[r] = mm(cot[r], zo_o[:, 512:1024])
+        acts[r, 0:512] = mm(xn_o[r], zo_o[:, 0:512])
+        dy_o[r] = mm(cot[r], zo_o[:, 512:1024])
         return carry
 
     lax.fori_loop(0, 8, project, 0)
@@ -412,10 +421,10 @@
         r = pl.ds(pl.multiple_of(b * Q, Q), Q)
         y = y_s[r] + mm2(er_s[r], expand) * mm(c_s[r], st_o[...].astype(BF))
         y_s[r] = y
-        z = z_s[r]
+        z = acts[r, 0:512]
         gated = y * (z * sigmoid(z))
         first_sum = jnp.sum(gated * gated, axis=1, keepdims=True)
-        second_sum = jnp.sum(dn_s[r] * gg[...] * gated, axis=1, keepdims=True)
+        second_sum = jnp.sum(dy_o[r] * gg[...] * gated, axis=1, keepdims=True)
         row_s[b] = jnp.concatenate([first_sum, second_sum, jnp.zeros((Q, 6), F32)], axis=1).T
         return carry
 
@@ -436,8 +445,8 @@
         for p in range(4):
             lanes = slice(p * 128, p * 128 + 128)
             y = y_s[r, lanes]
-            z = z_s[r, lanes]
-            dn = dn_s[r, lanes]
+            z = acts[r, lanes]
+            dn = dy_o[r, lanes]
             sig = sigmoid(z)
             gate = z * sig
             gated = y * gate
@@ -684,56 +693,31 @@
     grads_ctx.wait_recv()
     oz[...] = cs[:, 0:512].astype(F32) + cr[:, 0:512].astype(F32)
     oo[...] = cs[:, 512:1024].astype(F32) + cr[:, 512:1024].astype(F32)
-    ring.gather_wait(out_o)
-    links.finish()
-    spread1.sent()
-    spread2.sent()
-
-
-def add_slots(total, slots, lanes):
-    for k in range(7):
-        total = total + slots[k, :, lanes].astype(F32)
-    return total
-
-
-def tail_kernel(
-    dz, dx, ddt, dbc, small, gate, gain, w_in, w_zo, xn, tok, cot,
-    dtok_o, ox, odt, obc, onorm, conv_o, convb_o, bc_o, bcb_o, gate_o, dtb_o, alog_o, dsk_o,
-    part, gx, near, relay, from_d, from_u, sx, chunk, rg, cs, cr, t2,
-    sm, sm_s, sm_c, sm_x, sm_r, sm_t, nm, nm_s, nm_c, nm_x, nm_r, nm_t, tok_r, cot_r, send, recv, local_sem,
-):
-    shard, context, tensor, core, chip, chips, sibling, others, partner, ranks, group, at = places()
-    own = pl.ds(pl.multiple_of(tensor * 256, 256), 256)
-    fetch = [
-        pltpu.make_async_copy(tok.at[own], tok_r, local_sem.at[0]),
-        pltpu.make_async_copy(cot.at[own], cot_r, local_sem.at[1]),
-    ]
-    for copy in fetch:
-        copy.start()
-    greet([sibling, partner] + others[1:] + group[1:])
-    links = Links(send, recv)
-    sm[...] = small[...]
-    sm[20:24] = gate[...]
+    for made in ring.first + ring.alone:
+        made.wait_send()
+        links.started = [other for other in links.started if other is not made]
+    sm[...] = small_o[...]
+    sm[20:24] = gate_o[...]
     wide = Ring(links, tensor, group)
 
     def make(r):
-        total = mm_nt(dz[r], w_zo[:, 0:512]) + mm_nt(dx[r], w_in[:, 0:512]) + mm_nt(ddt[r], w_in[:, 768:896]) + mm_nt(dbc[r], w_in[:, 512:768])
-        part[r] = total.astype(BF)
-
-    wide.reduce_first(part, near, from_d, from_u, make)
+        total = mm_nt(dz_o[r], zo_o[:, 0:512]) + mm_nt(dx_o[r], in_o[:, 0:512]) + mm_nt(ddt_o[r], in_o[:, 768:896]) + mm_nt(dbc_o[r], in_o[:, 512:768])
+        branch_o[r] = total.astype(BF)
+
+    wide.reduce_first(branch_o, near2, from_d2, from_u2, make)
     small_in = links.copy(sm, sm_s, sibling)
 
     def outer(m):
-        block = xn[:, m * 128 : m * 128 + 128]
-        gx[m, :, :, 0:512] = mm_tn(block, dx[...]).astype(BF).reshape(2, 64, 512)
-        gx[m, :, :, 512:640] = mm_tn(block, ddt[...]).astype(BF).reshape(2, 64, 128)
-        gx[m, :, :, 640:896] = mm_tn(block, dbc[...]).astype(BF).reshape(2, 64, 256)
+        block = xn_o[:, m * 128 : m * 128 + 128]
+        gx[m, :, :, 0:512] = mm_tn(block, dx_o[...]).astype(BF).reshape(2, 64, 512)
+        gx[m, :, :, 512:640] = mm_tn(block, ddt_o[...]).astype(BF).reshape(2, 64, 128)
+        gx[m, :, :, 640:896] = mm_tn(block, dbc_o[...]).astype(BF).reshape(2, 64, 256)
 
     make(wide.half(wide.t_up, 0))
     make(wide.half(wide.t_down, 1))
     for m in range(4):
         outer(m)
-    wide.reduce_second(part, near, relay, from_d, from_u)
+    wide.reduce_second(branch_o, near2, relay2, from_d2, from_u2)
     for m in range(4, 8):
         outer(m)
     sib_in = links.copy(gx.at[:, 1 - core], sx, sibling)
@@ -747,26 +731,24 @@
     sib_in.wait_recv()
 
     def merge(c, carry):
-        chunk[c] = (gx[c, core].astype(F32) + sx[c].astype(F32)).astype(BF)
+        chunk2[c] = (gx[c, core].astype(F32) + sx[c].astype(F32)).astype(BF)
         return carry
 
     lax.fori_loop(0, 8, merge, 0)
-    grads_in = [links.copy(chunk.at[chips[k]], rg.at[k - 1], others[k]) for k in range(1, 8)]
-
-    for copy in fetch:
-        copy.wait()
+    grads_in = [links.copy(chunk2.at[chips[k]], rg2.at[k - 1], others[k]) for k in range(1, 8)]
+
     wide.reduce_wait()
 
     def inner(i, g_norm):
         r = pl.ds(pl.multiple_of(i * 64, 64), 64)
         rt = pl.ds(pl.multiple_of(tensor * 256 + i * 64, 64), 64)
-        total = part[rt].astype(F32) + from_d[r].astype(F32) + from_u[r].astype(F32)
-        plain = tok_r[r].astype(F32)
+        total = branch_o[rt].astype(F32) + from_d2[r].astype(F32) + from_u2[r].astype(F32)
+        plain = tok[rt].astype(F32)
         root = lax.rsqrt(jnp.mean(plain * plain, axis=1, keepdims=True) + EPSILON)
         stat = plain * root
-        d_plain = total * gain[...]
+        d_plain = total * gain_o[...]
         mean = jnp.mean(d_plain * plain, axis=1, keepdims=True)
-        dtok_o[rt] = (cot_r[r].astype(F32) + root * d_plain - stat * (root * root) * mean).astype(BF)
+        dtok_o[rt] = (cot[rt].astype(F32) + root * d_plain - stat * (root * root) * mean).astype(BF)
         return g_norm + jnp.sum(total * stat, axis=0, keepdims=True)
 
     g_norm = lax.fori_loop(0, 4, inner, jnp.zeros((1, 1024), F32))
@@ -792,8 +774,8 @@
         copy.wait_recv()
     for col in range(0, 896, 128):
         lanes = slice(col, col + 128)
-        cs[:, lanes] = add_slots(chunk[chip, :, lanes].astype(F32), rg, lanes).astype(BF)
-    grads_ctx = links.copy(cs, cr, partner)
+        cs2[:, lanes] = add_slots(chunk2[chip, :, lanes].astype(F32), rg2, lanes).astype(BF)
+    grads_ctx = links.copy(cs2, cr2, partner)
     wide.gather_second(dtok_o)
     for k in range(1, 8):
         source = lax.rem(chip + 8 - k, 8)
@@ -810,7 +792,7 @@
             conv_o[k : k + 1, p * 128 : p * 128 + 128] = sums[k * 4 + p : k * 4 + p + 1]
     for p in range(4):
         convb_o[:, p * 128 : p * 128 + 128] = sums[16 + p : 17 + p]
-        gate_o[:, p * 128 : p * 128 + 128] = sums[20 + p : 21 + p]
+        ggate_o[:, p * 128 : p * 128 + 128] = sums[20 + p : 21 + p]
     dtb_o[...] = sums[24:25, 0:8]
     alog_o[...] = sums[25:26, 0:8]
     dsk_o[...] = sums[26:27, 0:8]
@@ -824,12 +806,12 @@
     for k in range(1, 4):
         links.copy(nm_t.at[tensor], nm_t.at[tensor], group[k])
     grads_ctx.wait_recv()
-    ox[...] = cs[:, 0:512].astype(F32) + cr[:, 0:512].astype(F32)
-    t2[tensor] = cs[:, 640:896].astype(F32) + cr[:, 640:896].astype(F32)
+    ox[...] = cs2[:, 0:512].astype(F32) + cr2[:, 0:512].astype(F32)
+    t2[tensor] = cs2[:, 640:896].astype(F32) + cr2[:, 640:896].astype(F32)
     grads2_t = links.count
     for k in range(1, 4):
         links.copy(t2.at[tensor], t2.at[tensor], group[k])
-    odt[...] = (cs[:, 512:640].astype(F32) + cr[:, 512:640].astype(F32))[:, 0:8]
+    odt[...] = (cs2[:, 512:640].astype(F32) + cr2[:, 512:640].astype(F32))[:, 0:8]
     for k in range(1, 4):
         source = lax.rem(tensor + 4 - k, 4)
         arrival(None, sm_t.at[source], recv.at[small_t + k - 1], group[k]).wait_recv()
@@ -846,7 +828,10 @@
     row = nm_s[pl.ds(chip, 1), :]
     onorm[...] = jnp.where(core == 0, row[:, 0:64], row[:, 64:128])
     wide.gather_wait(dtok_o)
+    ring.gather_wait(out_o)
     links.finish()
+    spread1.sent()
+    spread2.sent()
 
 
 def call(kernel, out_shapes, scratch, *args, specs=None, collective_id=None):
@@ -899,32 +884,26 @@
     def vector(shape, last):
         return [(s, F32) for s in (shape, shape, (8,) + shape, shape, shape, last)]
 
-    (w_in, w_zo, x_normed, gain_row, d_z, g_gate_gain, d_x_low, d_bc, d_dt_low, small, output, o_z, o_out) = call(
+    (output, o_z, o_out, d_tokens, o_x, o_dt, o_bc, o_norm, conv_o, convb_o, cbc_o, cbcb_o, gate_o, dtb_o, alog_o, dsk_o) = call(
         main_kernel,
+        [((length, 1024), BF), (own, F32), (own, F32), ((length, 1024), BF), (own, F32), ((64, 8), F32), ((64, 256), F32), ((1, 64), F32),
+         ((4, 512), F32), ((1, 512), F32), ((4, 256), F32), ((1, 256), F32), ((1, 512), F32), ((1, 8), F32), ((1, 8), F32), ((1, 8), F32)],
         [((1024, 896), BF), ((1024, 1024), BF), ((length, 1024), BF), ((1, 1024), F32), (wide, BF), ((4, 128), F32),
-         (wide, BF), ((length, 2 * STATE), BF), ((length, 128), BF), ((48, 128), F32), ((length, 1024), BF), (own, F32), (own, F32)],
-        [((64, 896), BF), ((64, 1024), BF), ((EDGE, 1024), BF), ((8, 128), jnp.int32), ((length + EDGE, 768), F32), (state, F32), (state, BF), (state, BF),
-         (wide, F32), ((length, 8), F32), ((length, STATE), BF), (wide, F32), (wide, F32), ((8, 8, 128), F32), ((3, 8, 8, 128), F32), (wide, BF),
+         (wide, BF), ((length, 2 * STATE), BF), ((length, 128), BF), ((48, 128), F32),
+         ((64, 896), BF), ((64, 1024), BF), ((EDGE, 1024), BF), ((8, 128), jnp.int32), ((length + EDGE, 768), F32), (state, F32), (state, BF), (state, BF),
+         (wide, F32), ((length, 8), F32), ((length, STATE), BF), ((8, 8, 128), F32), ((3, 8, 8, 128), F32), (wide, BF),
          ((length + EDGE, 768), BF), ((length, 768), F32), ((length, 8), F32), ((length + 8, 8), F32), (state, F32), (wide, F32),
          ((length, 1024), BF), (state, BF), (grid, BF), (grid, BF),
          ((length, 768), F32), (state, F32), ((8, 8), F32),
          (state, BF), ((EDGE, 768), F32), ((8, 768), F32), ((8, 768), F32), half, half, rows, rows,
          ((8, 64, 512), BF), ((8, 64, 512), BF), ((8, 64, 1024), BF), ((7, 64, 1024), BF), ((64, 1024), BF), ((64, 1024), BF),
-         ((72,), None), ((72,), None)],
+         ((8, 2, 64, 896), BF), half, half, rows, rows,
+         ((8, 64, 896), BF), ((8, 64, 896), BF), ((7, 64, 896), BF), ((64, 896), BF), ((64, 896), BF), ((4, 64, 256), F32),
+         *vector((48, 128), (4, 16, 128)), *vector((8, 128), (4, 8, 128)),
+         ((120,), None), ((120,), None)],
         w_z, w_x, w_bc, w_dt, norm_gain[None], w_out, tokens, cotangent, seg,
         conv_x, conv_bc, conv_xb[None], conv_bcb[None], *heads, gate_gain[None], expand, expand_t,
         collective_id=1,
-    )
-    d_tokens, o_x, o_dt, o_bc, o_norm, conv_o, convb_o, cbc_o, cbcb_o, gate_o, dtb_o, alog_o, dsk_o = call(
-        tail_kernel,
-        [((length, 1024), BF), (own, F32), ((64, 8), F32), ((64, 256), F32), ((1, 64), F32),
-         ((4, 512), F32), ((1, 512), F32), ((4, 256), F32), ((1, 256), F32), ((1, 512), F32), ((1, 8), F32), ((1, 8), F32), ((1, 8), F32)],
-        [((length, 1024), BF), ((8, 2, 64, 896), BF), half, half, rows, rows,
-         ((8, 64, 896), BF), ((8, 64, 896), BF), ((7, 64, 896), BF), ((64, 896), BF), ((64, 896), BF), ((4, 64, 256), F32),
-         *vector((48, 128), (4, 16, 128)), *vector((8, 128), (4, 8, 128)),
-         rows, rows, ((64,), None), ((64,), None), ((2,), None)],
-        d_z, d_x_low, d_dt_low, d_bc, small, g_gate_gain, gain_row, w_in, w_zo, x_normed, tokens, cotangent,
-        specs=(10, 11), collective_id=2,
     )
     return (
         output, d_tokens, o_norm[0], o_z, o_x, o_dt, o_bc, conv_o, convb_o[0], cbc_o, cbcb_o[0],

time: 169 us -> 161 us (0.953)
  Pallas kernels: 154 us -> 145 us
    pallas_call x2 -> x1, Pallas kernels: 154 us -> 145 us  [call(): pl.pallas_call(kernel, out_shape=[jax.ShapeDtypeStruct(s, d) for s, d in...]
    unnamed x47 -> x45, local copies, waits for them, and re-layouts: 14.1 us -> 15 us
where the time goes in v7:
time: 161 us; the launch traced here: 160 us
  Pallas kernels  145 us (90%)
  local copies, waits for them, and re-layouts  15 us (9%)
    pallas_call x1, Pallas kernels, call(): pl.pallas_call(kernel, out_shape=[jax.ShapeDtypeStruct(s, d) for s, d in...  145 us
    unnamed x45, local copies, waits for them, and re-layouts  15 us

profile of v7, /device:TPU:1, one launch (start us, length us, event | category | flops | bytes accessed | tf_op | source)
XLA Modules:
  0.0 160.3 jit_solution(2316302688672125602)
XLA Ops:
  0.6 1.4 copy.35.wdt
  2.0 144.6 %shard_map.306 = (bf16[1024,1024]{1,0:T(8,128)(2,1)}, f32[64,512]{1,0:T(8,128)}, f32[64,512]{1,0:T(8,128)}, bf16[1024,1024]{1,0:T(8,128)(2,1)}, f32[64,512]{1,0:...) custom-call(bf16[64,512]{1,0:T(8,128)(2,1)} %wz.1, ...), custom_call_target="tpu_custom_call" | custom-call | tf_op jit(solution)/shard_map/pallas_call | solution.py:838
  146.6 1.4 copy.36
  148.1 3.2 %copy.52 = bf16[1024,1024]{1,0:T(8,128)(2,1)} copy(bf16[1024,1024]{1,0:T(8,128)(2,1)} %get-tuple-element.80) | data formatting | bytes 4194304
  151.3 0.0 copy-done
  151.3 0.0 copy-start.4
  151.3 0.0 copy-start.5
  151.4 1.3 copy.53
  152.7 0.0 copy-done.13
  152.7 0.5 copy.54
  153.2 0.7 copy.55
  153.9 0.7 copy.56
  154.6 0.6 copy.57
  155.2 0.6 copy.58
  155.8 0.6 copy.59
  156.4 0.6 copy.60
  157.0 0.0 copy-done.9
  157.0 0.6 copy.61
  157.5 0.0 copy-done.12
  157.5 0.5 copy.62
  158.0 0.5 copy.63
  158.6 0.5 copy.64
  159.1 0.6 copy.65
  159.7 0.7 copy.66
  (22 shorter events, 0.0 us)
Async XLA Ops:
  148.1 3.2 %copy-start = (bf16[1024,1024]{1,0:T(8,128)(2,1)S(1)}, bf16[1024,1024]{1,0:T(8,128)(2,1)}, u32[]{:S(2)}) copy-start(bf16[1024,1024]{1,0:T(8,128)(2,1)} %get-tuple-element.81) | copy-start | bytes 6291460
  151.3 1.4 copy-start.13
  151.3 1.9 %copy-start.3 = (f32[64,512]{1,0:T(8,128)S(1)}, f32[64,512]{1,0:T(8,128)}, u32[]{:S(2)}) copy-start(f32[64,512]{1,0:T(8,128)} %get-tuple-element.83) | copy-start | bytes 393220
  151.3 2.6 %copy-start.2 = (f32[64,512]{1,0:T(8,128)S(1)}, f32[64,512]{1,0:T(8,128)}, u32[]{:S(2)}) copy-start(f32[64,512]{1,0:T(8,128)} %get-tuple-element.84) | copy-start | bytes 393220
  151.3 3.3 %copy-start.4 = (f32[64,256]{1,0:T(8,128)S(1)}, f32[64,256]{1,0:T(8,128)}, u32[]{:S(2)}) copy-start(f32[64,256]{1,0:T(8,128)} %get-tuple-element.86) | copy-start | bytes 196612
  151.3 3.9 %copy-start.5 = (f32[4,512]{1,0:T(4,128)S(1)}, f32[4,512]{1,0:T(4,128)}, u32[]{:S(2)}) copy-start(f32[4,512]{1,0:T(4,128)} %get-tuple-element.87) | copy-start | bytes 24580
  151.3 4.5 %copy-start.8 = (f32[1,512]{1,0:T(1,128)S(1)}, f32[1,512]{1,0:T(1,128)}, u32[]{:S(2)}) copy-start(f32[1,512]{1,0:T(1,128)} %get-tuple-element.40) | copy-start | bytes 6148
  151.3 5.0 %copy-start.6 = (f32[4,256]{1,0:T(4,128)S(1)}, f32[4,256]{1,0:T(4,128)}, u32[]{:S(2)}) copy-start(f32[4,256]{1,0:T(4,128)} %get-tuple-element.89) | copy-start | bytes 12292
  151.3 5.6 %copy-start.9 = (f32[1,256]{1,0:T(1,128)S(1)}, f32[1,256]{1,0:T(1,128)}, u32[]{:S(2)}) copy-start(f32[1,256]{1,0:T(1,128)} %get-tuple-element.42) | copy-start | bytes 3076
  151.3 6.2 %copy-start.12 = (f32[1,8]{1,0:T(1,128)S(1)}, f32[1,8]{1,0:T(1,128)}, u32[]{:S(2)}) copy-start(f32[1,8]{1,0:T(1,128)} %get-tuple-element.43) | copy-start | bytes 100
  151.4 6.7 %copy-start.11 = (f32[1,8]{1,0:T(1,128)S(1)}, f32[1,8]{1,0:T(1,128)}, u32[]{:S(2)}) copy-start(f32[1,8]{1,0:T(1,128)} %get-tuple-element.44) | copy-start | bytes 100
  151.4 7.2 %copy-start.10 = (f32[1,8]{1,0:T(1,128)S(1)}, f32[1,8]{1,0:T(1,128)}, u32[]{:S(2)}) copy-start(f32[1,8]{1,0:T(1,128)} %get-tuple-element.45) | copy-start | bytes 100
  151.4 7.7 %copy-start.7 = (f32[1,512]{1,0:T(1,128)S(1)}, f32[1,512]{1,0:T(1,128)}, u32[]{:S(2)}) copy-start(f32[1,512]{1,0:T(1,128)} %get-tuple-element.46) | copy-start | bytes 6148
  151.4 8.3 %copy-start.1 = (f32[64,512]{1,0:T(8,128)S(1)}, f32[64,512]{1,0:T(8,128)}, u32[]{:S(2)}) copy-start(f32[64,512]{1,0:T(8,128)} %get-tuple-element.95) | copy-start | bytes 393220

commit v8 on v7

--- a/solution.py
+++ b/solution.py
@@ -408,12 +408,12 @@
     spread2.collect()
 
     def project(b, carry):
-        r = pl.ds(pl.multiple_of(b * Q, Q), Q)
+        r = pl.ds(pl.multiple_of(b * 256, 256), 256)
         acts[r, 0:512] = mm(xn_o[r], zo_o[:, 0:512])
         dy_o[r] = mm(cot[r], zo_o[:, 512:1024])
         return carry
 
-    lax.fori_loop(0, 8, project, 0)
+    lax.fori_loop(0, 4, project, 0)
     state_in.wait_recv()
     st_o[...] = jnp.where(context > 0, st_in[...].astype(F32), 0.0)
 

time: 161 us -> 160 us (level)
  no operation moved by 1% of the time
where the time goes in v8:
time: 160 us
  Pallas kernels  144 us (90%)
  local copies, waits for them, and re-layouts  15 us (9%)
    pallas_call x1, Pallas kernels, call(): pl.pallas_call(kernel, out_shape=[jax.ShapeDtypeStruct(s, d) for s, d in...  144 us
    unnamed x45, local copies, waits for them, and re-layouts  15 us

profile of v8, /device:TPU:1, one launch (start us, length us, event | category | flops | bytes accessed | tf_op | source)
XLA Modules:
  0.0 160.0 jit_solution(17204122003962881686)
XLA Ops:
  0.6 1.4 copy.35.wdt
  2.0 144.3 %shard_map.306 = (bf16[1024,1024]{1,0:T(8,128)(2,1)}, f32[64,512]{1,0:T(8,128)}, f32[64,512]{1,0:T(8,128)}, bf16[1024,1024]{1,0:T(8,128)(2,1)}, f32[64,512]{1,0:...) custom-call(bf16[64,512]{1,0:T(8,128)(2,1)} %wz.1, ...), custom_call_target="tpu_custom_call" | custom-call | tf_op jit(solution)/shard_map/pallas_call | solution.py:838
  146.3 1.4 copy.36
  147.7 3.2 %copy.52 = bf16[1024,1024]{1,0:T(8,128)(2,1)} copy(bf16[1024,1024]{1,0:T(8,128)(2,1)} %get-tuple-element.80) | data formatting | bytes 4194304
  150.9 0.0 copy-done
  151.0 0.0 copy-start.4
  151.0 0.0 copy-start.5
  151.1 1.3 copy.53
  152.4 0.0 copy-done.13
  152.4 0.5 copy.54
  152.9 0.7 copy.55
  153.5 0.7 copy.56
  154.2 0.0 copy-done.4
  154.2 0.6 copy.57
  154.8 0.6 copy.58
  155.4 0.6 copy.59
  156.0 0.6 copy.60
  156.6 0.6 copy.61
  157.2 0.0 copy-done.12
  157.2 0.5 copy.62
  157.7 0.5 copy.63
  158.2 0.5 copy.64
  158.7 0.6 copy.65
  159.3 0.7 copy.66
  (22 shorter events, 0.0 us)
Async XLA Ops:
  147.7 3.2 %copy-start = (bf16[1024,1024]{1,0:T(8,128)(2,1)S(1)}, bf16[1024,1024]{1,0:T(8,128)(2,1)}, u32[]{:S(2)}) copy-start(bf16[1024,1024]{1,0:T(8,128)(2,1)} %get-tuple-element.81) | copy-start | bytes 6291460
  150.9 1.4 copy-start.13
  150.9 1.9 %copy-start.3 = (f32[64,512]{1,0:T(8,128)S(1)}, f32[64,512]{1,0:T(8,128)}, u32[]{:S(2)}) copy-start(f32[64,512]{1,0:T(8,128)} %get-tuple-element.83) | copy-start | bytes 393220
  150.9 2.6 %copy-start.2 = (f32[64,512]{1,0:T(8,128)S(1)}, f32[64,512]{1,0:T(8,128)}, u32[]{:S(2)}) copy-start(f32[64,512]{1,0:T(8,128)} %get-tuple-element.84) | copy-start | bytes 393220
  151.0 3.3 %copy-start.4 = (f32[64,256]{1,0:T(8,128)S(1)}, f32[64,256]{1,0:T(8,128)}, u32[]{:S(2)}) copy-start(f32[64,256]{1,0:T(8,128)} %get-tuple-element.86) | copy-start | bytes 196612
  151.0 3.9 %copy-start.5 = (f32[4,512]{1,0:T(4,128)S(1)}, f32[4,512]{1,0:T(4,128)}, u32[]{:S(2)}) copy-start(f32[4,512]{1,0:T(4,128)} %get-tuple-element.87) | copy-start | bytes 24580
  151.0 4.5 %copy-start.8 = (f32[1,512]{1,0:T(1,128)S(1)}, f32[1,512]{1,0:T(1,128)}, u32[]{:S(2)}) copy-start(f32[1,512]{1,0:T(1,128)} %get-tuple-element.40) | copy-start | bytes 6148
  151.0 5.0 %copy-start.6 = (f32[4,256]{1,0:T(4,128)S(1)}, f32[4,256]{1,0:T(4,128)}, u32[]{:S(2)}) copy-start(f32[4,256]{1,0:T(4,128)} %get-tuple-element.89) | copy-start | bytes 12292
  151.0 5.6 %copy-start.9 = (f32[1,256]{1,0:T(1,128)S(1)}, f32[1,256]{1,0:T(1,128)}, u32[]{:S(2)}) copy-start(f32[1,256]{1,0:T(1,128)} %get-tuple-element.42) | copy-start | bytes 3076
  151.0 6.2 %copy-start.12 = (f32[1,8]{1,0:T(1,128)S(1)}, f32[1,8]{1,0:T(1,128)}, u32[]{:S(2)}) copy-start(f32[1,8]{1,0:T(1,128)} %get-tuple-element.43) | copy-start | bytes 100
  151.0 6.7 %copy-start.11 = (f32[1,8]{1,0:T(1,128)S(1)}, f32[1,8]{1,0:T(1,128)}, u32[]{:S(2)}) copy-start(f32[1,8]{1,0:T(1,128)} %get-tuple-element.44) | copy-start | bytes 100
  151.0 7.2 %copy-start.10 = (f32[1,8]{1,0:T(1,128)S(1)}, f32[1,8]{1,0:T(1,128)}, u32[]{:S(2)}) copy-start(f32[1,8]{1,0:T(1,128)} %get-tuple-element.45) | copy-start | bytes 100
  151.0 7.7 %copy-start.7 = (f32[1,512]{1,0:T(1,128)S(1)}, f32[1,512]{1,0:T(1,128)}, u32[]{:S(2)}) copy-start(f32[1,512]{1,0:T(1,128)} %get-tuple-element.46) | copy-start | bytes 6148
  151.0 8.3 %copy-start.1 = (f32[64,512]{1,0:T(8,128)S(1)}, f32[64,512]{1,0:T(8,128)}, u32[]{:S(2)}) copy-start(f32[64,512]{1,0:T(8,128)} %get-tuple-element.95) | copy-start | bytes 393220
